TPU v7x, 32 devices: a whole 2x2x4 slice. The times are simulated.
32 devices in a mesh: section: 2 (over core), dp: 16 (over z, y, x).
Axes of the slice: x: 2, y: 2, z: 4, core: 2. Of those that a mesh axis runs over, the one named last changes fastest.
Arguments:
- tokens: bfloat16 [16384, 768], P('dp'), may hold values from -6 to 6
- seq_ends: int32 [16384], P('dp'), may hold values from 0 to 512, as said below
- qkv_weight: bfloat16 [2, 768, 2304], P('section'), may hold values from -0.21875 to 0.21875
- qv_bias: float32 [2, 1536], P('section'), may hold values from -3 to 3
- out_weight: bfloat16 [2, 768, 768], P('section'), may hold values from -0.625 to 0.625
- out_bias: float32 [2, 768], P('section'), may hold values from -2 to 2
- gain_one: float32 [2, 768], P('section'), may hold values from 0.1 to 1.9
- shift_one: float32 [2, 768], P('section'), may hold values from -2 to 2
- up_weight: bfloat16 [2, 768, 3072], P('section'), may hold values from -0.21875 to 0.21875
- up_bias: float32 [2, 3072], P('section'), may hold values from -3 to 3
- down_weight: bfloat16 [2, 3072, 768], P('section'), may hold values from -0.109375 to 0.109375
- down_bias: float32 [2, 768], P('section'), may hold values from -2 to 2
- gain_two: float32 [2, 768], P('section'), may hold values from 0.1 to 1.9
- shift_two: float32 [2, 768], P('section'), may hold values from -2 to 2
- head_weight: bfloat16 [768], replicated, may hold values from -0.21875 to 0.21875
- out_cotangent: bfloat16 [16384, 768], P('dp'), may hold values from -6 to 6
- term_cotangent: float32 [16384], P('dp'), may hold values from -6 to 6
Outputs:
- hidden_states: bfloat16 [2, 16384, 768], P('section', 'dp')
- term_weights: float32 [8192, 2], P('dp', 'section')
- input_grads: bfloat16 [2, 16384, 768], P('section', 'dp')
- grad_qkv_weight: float32 [2, 768, 2304], P('section', 'dp')
- grad_qv_bias: float32 [2, 1536], P('section', 'dp')
- grad_out_weight: float32 [2, 768, 768], P('section', 'dp')
- grad_out_bias: float32 [2, 768], P('section', 'dp')
- grad_gain_one: float32 [2, 768], P('section', 'dp')
- grad_shift_one: float32 [2, 768], P('section', 'dp')
- grad_up_weight: float32 [2, 768, 3072], P('section', 'dp')
- grad_up_bias: float32 [2, 3072], P('section', 'dp')
- grad_down_weight: float32 [2, 3072, 768], P('section', 'dp')
- grad_down_bias: float32 [2, 768], P('section', 'dp')
- grad_gain_two: float32 [2, 768], P('section', 'dp')
- grad_shift_two: float32 [2, 768], P('section', 'dp')
- grad_head: float32 [384, 2], P('dp', 'section')
Inputs may be any that keep to these rules, and one draw needn't show every extreme that they name: `seq_ends`: within each aligned block of 512 slots (one micro-batch), passages are runs of slots with equal nonzero values, each value being one past the run's last slot within the block; padding slots hold 0 and come after the passages at the block's end. Most passages are short; some blocks have no padding.
All inputs are finite; a program needn't handle non-finite values.
Results may differ from a plain program's by a relative error of at most 0.03.
Values may be sent and summed in bfloat16 or wider, within the bound.
No kernel may reach another device: no remote copies, remote signals or barrier semaphores. Data moves between devices by JAX's collectives and lax.ppermute only.
A program may use at most 320 MiB of HBM per device.

v0:
```python
from functools import reduce

import jax
import jax.numpy as jnp
from jax import lax
from jax.sharding import PartitionSpec as P

HEADS = 12
HEAD_DIM = 64
MB_TOK = 512
MICRO = 2


SCALE = 0.125
EPS = 1e-06


def from_behind(array, axis, by):
    length = lax.axis_size(axis)
    pairs = [(i, i + by) for i in range(length) if 0 <= i + by < length]
    return lax.ppermute(array, axis, pairs)


def layer_norm(values, gain, shift):
    center = values - jnp.mean(values, axis=-1, keepdims=True)
    spread = jnp.mean(center * center, axis=-1, keepdims=True)
    return center * lax.rsqrt(spread + EPS) * gain + shift


def smooth_gate(values):
    return jax.nn.gelu(values, approximate=False)


def split_heads(matrix):
    return matrix.reshape(matrix.shape[0], HEADS, HEAD_DIM)


def masked_scores(queries, key_rows, block_ends):
    scores = jnp.einsum(
        "qhd,khd->hqk",
        split_heads(queries),
        split_heads(key_rows),
        preferred_element_type=jnp.float32,
    )
    same_doc = block_ends[:, None] == block_ends[None, :]
    return jnp.where(same_doc[None], scores, -1e30)


def layer_forward(inputs, block_ends, params):
    (
        qkv_weight,
        qv_bias,
        out_weight,
        out_bias,
        gain_one,
        shift_one,
        up_weight,
        up_bias,
        down_weight,
        down_bias,
        gain_two,
        shift_two,
    ) = params
    row_count, model_width = inputs.shape
    projected = jnp.dot(inputs, qkv_weight, preferred_element_type=jnp.float32)
    queries = ((projected[:, :model_width] + qv_bias[:model_width]) * SCALE).astype(jnp.bfloat16)
    key_rows = projected[:, model_width : 2 * model_width].astype(jnp.bfloat16)
    value_rows = (projected[:, 2 * model_width :] + qv_bias[model_width:]).astype(jnp.bfloat16)
    scores = masked_scores(queries, key_rows, block_ends)
    row_peak = jnp.max(scores, axis=-1, keepdims=True)
    weights = jnp.exp(scores - row_peak)
    totals = jnp.sum(weights, axis=-1, keepdims=True)
    log_total = (row_peak + jnp.log(totals))[..., 0]
    chances = (weights / totals).astype(jnp.bfloat16)
    mixed = jnp.einsum(
        "hqk,khd->qhd", chances, split_heads(value_rows), preferred_element_type=jnp.float32
    )
    mixed = mixed.reshape(row_count, model_width).astype(jnp.bfloat16)
    attended = jnp.dot(mixed, out_weight, preferred_element_type=jnp.float32) + out_bias
    first_sum = inputs.astype(jnp.float32) + attended
    normed = layer_norm(first_sum, gain_one, shift_one)
    normed_low = normed.astype(jnp.bfloat16)
    up_rows = jnp.dot(normed_low, up_weight, preferred_element_type=jnp.float32) + up_bias
    active = smooth_gate(up_rows).astype(jnp.bfloat16)
    second_sum = (
        normed + jnp.dot(active, down_weight, preferred_element_type=jnp.float32) + down_bias
    )
    output = layer_norm(second_sum, gain_two, shift_two)
    stored = (
        queries,
        key_rows,
        value_rows,
        log_total,
        chances,
        mixed,
        first_sum,
        normed_low,
        up_rows,
        active,
        second_sum,
    )
    return (output, stored)


def layer_backward(inputs, block_ends, params, stored, cotangent):
    (
        qkv_weight,
        qv_bias,
        out_weight,
        out_bias,
        gain_one,
        shift_one,
        up_weight,
        up_bias,
        down_weight,
        down_bias,
        gain_two,
        shift_two,
    ) = params
    (
        queries,
        key_rows,
        value_rows,
        log_total,
        chances,
        mixed,
        first_sum,
        normed_low,
        up_rows,
        active,
        second_sum,
    ) = stored
    row_count, model_width = inputs.shape
    dummy, back_two = jax.vjp(layer_norm, second_sum, gain_two, shift_two)
    d_second, d_gain_two, d_shift_two = back_two(cotangent)
    d_down = d_second.astype(jnp.bfloat16)
    g_down_weight = jnp.einsum("tf,td->fd", active, d_down, preferred_element_type=jnp.float32)
    g_down_bias = jnp.sum(d_down.astype(jnp.float32), axis=0)
    d_active = jnp.einsum("td,fd->tf", d_down, down_weight, preferred_element_type=jnp.float32)
    dummy, back_gate = jax.vjp(smooth_gate, up_rows)
    d_up = back_gate(d_active)[0].astype(jnp.bfloat16)
    g_up_weight = jnp.einsum("td,tf->df", normed_low, d_up, preferred_element_type=jnp.float32)
    g_up_bias = jnp.sum(d_up.astype(jnp.float32), axis=0)
    d_normed = d_second + jnp.einsum(
        "tf,df->td", d_up, up_weight, preferred_element_type=jnp.float32
    )
    dummy, back_one = jax.vjp(layer_norm, first_sum, gain_one, shift_one)
    d_first, d_gain_one, d_shift_one = back_one(d_normed)
    d_attended = d_first.astype(jnp.bfloat16)
    g_out_weight = jnp.einsum("td,te->de", mixed, d_attended, preferred_element_type=jnp.float32)
    g_out_bias = jnp.sum(d_attended.astype(jnp.float32), axis=0)
    d_mixed = jnp.einsum(
        "te,de->td", d_attended, out_weight, preferred_element_type=jnp.float32
    ).astype(jnp.bfloat16)
    d_mixed = split_heads(d_mixed)
    scores = masked_scores(queries, key_rows, block_ends)
    floats = jnp.exp(scores - log_total[..., None])
    d_values = jnp.einsum("hqk,qhd->khd", chances, d_mixed, preferred_element_type=jnp.float32)
    d_values = d_values.reshape(row_count, model_width).astype(jnp.bfloat16)
    d_chances = jnp.einsum(
        "qhd,khd->hqk", d_mixed, split_heads(value_rows), preferred_element_type=jnp.float32
    )
    d_scores = (floats * (d_chances - jnp.sum(d_chances * floats, axis=-1, keepdims=True))).astype(
        jnp.bfloat16
    )
    d_queries = jnp.einsum(
        "hqk,khd->qhd", d_scores, split_heads(key_rows), preferred_element_type=jnp.float32
    )
    d_queries = d_queries.reshape(row_count, model_width).astype(jnp.bfloat16) * SCALE
    d_keys = jnp.einsum(
        "hqk,qhd->khd", d_scores, split_heads(queries), preferred_element_type=jnp.float32
    )
    d_keys = d_keys.reshape(row_count, model_width).astype(jnp.bfloat16)
    d_projected = jnp.concatenate([d_queries, d_keys, d_values], axis=1)
    g_qkv_weight = jnp.einsum("td,te->de", inputs, d_projected, preferred_element_type=jnp.float32)
    g_qv_bias = jnp.concatenate(
        [
            jnp.sum(d_queries.astype(jnp.float32), axis=0),
            jnp.sum(d_values.astype(jnp.float32), axis=0),
        ]
    )
    d_inputs = d_first + jnp.einsum(
        "te,de->td", d_projected, qkv_weight, preferred_element_type=jnp.float32
    )
    gradients = (
        g_qkv_weight,
        g_qv_bias,
        g_out_weight,
        g_out_bias,
        d_gain_one,
        d_shift_one,
        g_up_weight,
        g_up_bias,
        g_down_weight,
        g_down_bias,
        d_gain_two,
        d_shift_two,
    )
    return (d_inputs.astype(jnp.bfloat16), gradients)


def add_tuples(former, latter):
    return tuple((first_part + second_part for first_part, second_part in zip(former, latter)))


def per_device(
    tokens,
    seq_ends,
    qkv_weight,
    qv_bias,
    out_weight,
    out_bias,
    gain_one,
    shift_one,
    up_weight,
    up_bias,
    down_weight,
    down_bias,
    gain_two,
    shift_two,
    head_weight,
    out_cotangent,
    term_cotangent,
):
    params = tuple(
        (
            weight[0]
            for weight in (
                qkv_weight,
                qv_bias,
                out_weight,
                out_bias,
                gain_one,
                shift_one,
                up_weight,
                up_bias,
                down_weight,
                down_bias,
                gain_two,
                shift_two,
            )
        )
    )
    is_first = lax.axis_index("section") == 0
    model_width = tokens.shape[1]
    token_blocks = tokens.reshape(MICRO, MB_TOK, model_width)
    end_blocks = seq_ends.reshape(MICRO, MB_TOK)
    cot_blocks = out_cotangent.reshape(MICRO, MB_TOK, model_width)
    term_blocks = term_cotangent.reshape(MICRO, MB_TOK)
    head_float = head_weight.astype(jnp.float32)

    def choose(early, late):
        return jnp.where(is_first, early, late)

    received = jnp.zeros((MB_TOK, model_width), jnp.bfloat16)
    tick_inputs = []
    tick_outputs = []
    for tick in range(MICRO + 1):
        block_here = choose(end_blocks[min(tick, MICRO - 1)], end_blocks[max(tick - 1, 0)])
        layer_input = choose(token_blocks[min(tick, MICRO - 1)], received)
        output, stored = layer_forward(layer_input, block_here, params)
        tick_inputs.append(layer_input)
        tick_outputs.append(output)
        if tick < MICRO:
            received = from_behind(output.astype(jnp.bfloat16), "section", 1)
    block_inputs = [choose(tick_inputs[index], tick_inputs[index + 1]) for index in range(MICRO)]
    block_outputs = [choose(tick_outputs[index], tick_outputs[index + 1]) for index in range(MICRO)]
    all_outputs = jnp.concatenate(block_outputs, axis=0)
    logits = jnp.dot(all_outputs, head_float, precision=lax.Precision.HIGHEST)
    term_all = jnp.where(seq_ends > 0, jax.nn.softplus(logits), 0.0)
    is_last = jnp.where(is_first, 0.0, 1.0)
    received_grad = jnp.zeros((MB_TOK, model_width), jnp.bfloat16)
    tick_grads = []
    collected = []
    for tick in range(MICRO + 1):
        late_index = max(MICRO - 1 - tick, 0)
        early_index = min(MICRO - tick, MICRO - 1)
        active_flag = jnp.where(is_first, float(tick >= 1), float(tick < MICRO))
        layer_input = choose(block_inputs[early_index], block_inputs[late_index])
        block_here = choose(end_blocks[early_index], end_blocks[late_index])
        output, stored = layer_forward(layer_input, block_here, params)
        live = (block_here > 0).astype(jnp.float32)
        slope = (
            jax.nn.sigmoid(jnp.dot(output, head_float, precision=lax.Precision.HIGHEST))
            * term_blocks[late_index]
            * live
        )
        top_grad = (
            live[:, None] * cot_blocks[late_index].astype(jnp.float32)
            + slope[:, None] * head_float[None, :]
        )
        cotangent = choose(received_grad.astype(jnp.float32), top_grad) * active_flag
        head_term = jnp.dot(slope, output, precision=lax.Precision.HIGHEST) * (
            is_last * active_flag
        )
        d_inputs, gradients = layer_backward(layer_input, block_here, params, stored, cotangent)
        gradients = gradients + (head_term,)
        tick_grads.append(d_inputs)
        collected.append(gradients)
        if tick < MICRO:
            received_grad = from_behind(d_inputs, "section", -1)
    summed = reduce(add_tuples, collected)
    shares = lax.psum_scatter(
        tuple((part[None] for part in summed)), "dp", scatter_dimension=1, tiled=True
    )
    head_pairs = shares[12][0].reshape(-1, 2)
    term_pairs = term_all.reshape(-1, 2)
    term_count = term_pairs.shape[0]
    outgoing = jnp.concatenate([term_pairs[:, 0], head_pairs[:, 0]])
    incoming = from_behind(outgoing, "section", -1)
    term_out = choose(incoming[:term_count], term_pairs[:, 1])[:, None]
    head_out = choose(incoming[term_count:], head_pairs[:, 1])[:, None]
    hidden_out = all_outputs.astype(jnp.bfloat16)[None]
    input_out = jnp.concatenate(
        [
            choose(tick_grads[MICRO - index], tick_grads[MICRO - 1 - index])
            for index in range(MICRO)
        ],
        axis=0,
    )[None]
    return (
        hidden_out,
        term_out,
        input_out,
        shares[0],
        shares[1],
        shares[2],
        shares[3],
        shares[4],
        shares[5],
        shares[6],
        shares[7],
        shares[8],
        shares[9],
        shares[10],
        shares[11],
        head_out,
    )


def solution(mesh):
    in_specs = (
        P("dp", None),
        P("dp"),
        P("section", None, None),
        P("section", None),
        P("section", None, None),
        P("section", None),
        P("section", None),
        P("section", None),
        P("section", None, None),
        P("section", None),
        P("section", None, None),
        P("section", None),
        P("section", None),
        P("section", None),
        P(),
        P("dp", None),
        P("dp"),
    )
    out_specs = (
        P("section", "dp", None),
        P("dp", "section"),
        P("section", "dp", None),
        P("section", "dp", None),
        P("section", "dp"),
        P("section", "dp", None),
        P("section", "dp"),
        P("section", "dp"),
        P("section", "dp"),
        P("section", "dp", None),
        P("section", "dp"),
        P("section", "dp", None),
        P("section", "dp"),
        P("section", "dp"),
        P("section", "dp"),
        P("dp", "section"),
    )
    return jax.shard_map(
        per_device, mesh=mesh, in_specs=in_specs, out_specs=out_specs, check_vma=False
    )
```

profile of v0, /device:TPU:0, one launch (start us, length us, event | category | flops | bytes accessed | tf_op | source)
XLA Modules:
  0.0 2178.5 jit_solution(6158789000036714662)
XLA Ops:
  27.0 11.0 fusion.544
  47.8 34.3 %fusion.546 = (f32[512]{0:T(512)}, f32[512,768]{1,0:T(8,128)}) fusion(f32[768]{0:T(1024)} %reduce.17, bf16[1,3072,768]{2,1,0:T(8,128)(2,1)} %param.27, bf16[1,768,3072]{2,1,0:T(8,128)(2,1)} %param.25, f32[3072]{0:T(1024)} %bitcast.485, f32[512,768]{1,0:T(8,128)} %copy-done.75, f32[768]{0:T(1024)} %reduce.16, f32[768]{0:T(1024)S(1)} %reduce.15, ...), kind=kOutput, calls=%fused_computation.748 | convolution fusion | flops 4940365312 | bytes 12610560 | tf_op jit(solution)/shard_map/dot_general | solution.py:86
  102.6 11.0 fusion.551
  122.7 24.0 %fusion.553 = (f32[512]{0:T(512)}, f32[512,768]{1,0:T(8,128)}) fusion(f32[768]{0:T(1024)} %reduce.17, bf16[1,3072,768]{2,1,0:T(8,128)(2,1)} %param.27, bf16[1,768,3072]{2,1,0:T(8,128)(2,1)} %param.25, f32[3072]{0:T(1024)} %bitcast.486, f32[512,768]{1,0:T(8,128)} %copy-done.76, f32[512]{0:T(512)} %add_rsqrt_fusion.3, f32[512]{0:T(512)} %copy-done.175, ...), kind=kOutput, calls=%fused_computation.751 | convolution fusion | flops 4940365312 | bytes 12610560 | tf_op jit(solution)/shard_map/dot_general | solution.py:86
  260.6 47.4 %multiply_convert_fusion.5 = (bf16[512,3072]{1,0:T(8,128)(2,1)S(1)}, f32[512,3072]{1,0:T(8,128)}, bf16[512,3072]{1,0:T(8,128)(2,1)S(1)}, f32[512,3072]{1,0:T(8,1...) fusion(f32[3072]{0:T(1024)S(1)} %bitcast.488, f32[512,3072]{1,0:T(8,128)} %fusion.98, ...), kind=kOutput, calls=%fused_computation.89 | convolution fusion | flops 2729312256 | bytes 53499904 | tf_op jit(solution)/shard_map/dot_general | solution.py:83
  325.5 10.1 convert_reduce_fusion.2
  354.8 10.6 multiply_reduce_fusion.2
  365.8 7.5 multiply_convert_fusion.2
  398.3 9.8 convert_reduce_fusion.1
  425.3 10.7 multiply_reduce_fusion.1
  436.6 7.3 multiply_convert_fusion.1
  469.0 10.1 convert_reduce_fusion
  490.4 6.1 convert_reduce_fusion.9
  496.6 10.4 multiply_reduce_fusion
  507.1 7.1 multiply_convert_fusion
  547.4 7.0 add_bitcast_fusion.2
  566.3 8.4 add_bitcast_fusion.1
  583.0 8.6 add_bitcast_fusion
  601.0 11.1 fusion.558
  612.1 6.1 fusion.300
  621.3 23.6 %fusion.560 = (f32[512]{0:T(512)}, f32[512,768]{1,0:T(8,128)}) fusion(f32[768]{0:T(1024)} %reduce.17, bf16[1,3072,768]{2,1,0:T(8,128)(2,1)} %param.27, bf16[1,768,3072]{2,1,0:T(8,128)(2,1)} %param.25, f32[3072]{0:T(1024)} %bitcast.487, f32[512,768]{1,0:T(8,128)} %copy-done.74, f32[512]{0:T(512)} %add_rsqrt_fusion.1, f32[512]{0:T(512)} %copy-done.174, ...), kind=kOutput, calls=%fused_computation.754 | convolution fusion | flops 4940365312 | bytes 12610560 | tf_op jit(solution)/shard_map/dot_general | solution.py:86
  673.0 98.7 %reduce-scatter.46.cloned.1.call-done = f32[48,1]{1,0:T(8,128)} async-done(((f32[768,1]{1,0:T(8,128)}), f32[48,1]{1,0:T(8,128)}) %reduce-scatter.46.cloned.1.call-update) | async-done | bytes 208
  772.9 124.6 %reduce-scatter.48.cloned.1.call-done = f32[48,1]{1,0:T(8,128)} async-done(((f32[768,1]{1,0:T(8,128)}), f32[48,1]{1,0:T(8,128)}) %reduce-scatter.48.cloned.1.call-update) | async-done | bytes 208
  898.9 123.9 %reduce-scatter.52.cloned.1.call-done = f32[48,1]{1,0:T(8,128)} async-done(((f32[768,1]{1,0:T(8,128)}), f32[48,1]{1,0:T(8,128)}) %reduce-scatter.52.cloned.1.call-update) | async-done | bytes 208
  1024.1 124.6 %reduce-scatter.54.cloned.1.call-done = f32[48,1]{1,0:T(8,128)} async-done(((f32[768,1]{1,0:T(8,128)}), f32[48,1]{1,0:T(8,128)}) %reduce-scatter.54.cloned.1.call-update) | async-done | bytes 208
  1150.0 124.1 %reduce-scatter.56.cloned.1.call-done = f32[48,1]{1,0:T(8,128)} async-done(((f32[768,1]{1,0:T(8,128)}), f32[48,1]{1,0:T(8,128)}) %reduce-scatter.56.cloned.1.call-update) | async-done | bytes 208
  1275.4 125.7 %reduce-scatter.42.cloned.1.call-done = f32[96,1]{1,0:T(8,128)} async-done(((f32[1536,1]{1,0:T(8,128)}), f32[96,1]{1,0:T(8,128)}) %reduce-scatter.42.cloned.1.call-update) | async-done | bytes 400
  1402.4 127.8 %reduce-scatter.50.cloned.1.call-done = f32[192,1]{1,0:T(8,128)} async-done(((f32[3072,1]{1,0:T(8,128)}), f32[192,1]{1,0:T(8,128)}) %reduce-scatter.50.cloned.1.call-update) | async-done | bytes 784
  1531.8 131.0 %reduce-scatter.34.cloned.1.call-done = f32[1,48,768]{2,1,0:T(8,128)} async-done(((f32[1,768,768]{2,1,0:T(8,128)}), f32[1,48,768]{2,1,0:T(8,128)}) %reduce-scatter.34.cloned.1.call-update) | async-done | bytes 147472 | tf_op jit(solution)/shard_map/reduce_scatter | solution.py:303
  1662.8 155.5 %reduce-scatter.32.cloned.1.call-done = f32[1,48,2304]{2,1,0:T(8,128)} async-done(((f32[1,768,2304]{2,1,0:T(8,128)}), f32[1,48,2304]{2,1,0:T(8,128)}) %reduce-scatter.32.cloned.1.call-update) | async-done | bytes 442384 | tf_op jit(solution)/shard_map/reduce_scatter | solution.py:303
  1818.3 176.1 %reduce-scatter.36.cloned.1.call-done = f32[1,48,3072]{2,1,0:T(8,128)} async-done(((f32[1,768,3072]{2,1,0:T(8,128)}), f32[1,48,3072]{2,1,0:T(8,128)}) %reduce-scatter.36.cloned.1.call-update) | async-done | bytes 589840 | tf_op jit(solution)/shard_map/reduce_scatter | solution.py:303
  1994.4 177.1 %reduce-scatter.38.cloned.1.call-done = f32[1,192,768]{2,1,0:T(8,128)} async-done(((f32[1,3072,768]{2,1,0:T(8,128)}), f32[1,192,768]{2,1,0:T(8,128)}) %reduce-scatter.38.cloned.1.call-update) | async-done | bytes 589840 | tf_op jit(solution)/shard_map/reduce_scatter | solution.py:303
  (734 shorter events, 389.9 us)
Async XLA Ops:
  7.2 648.4 %reduce-scatter.40.cloned.1.call-start = ((), (), s32[]{:S(2)}) async-start(), calls=%async_computation.17 | async-start | bytes 417792
  47.1 102.0 %copy-start.100 = (f32[768]{0:T(1024)}, f32[768]{0:T(1024)S(1)}, u32[]{:S(2)}) copy-start(f32[768]{0:T(1024)S(1)} %reduce.19) | copy-start | bytes 9220
  47.8 101.3 %copy-start.77 = (f32[768]{0:T(1024)}, f32[768]{0:T(1024)S(1)}, u32[]{:S(2)}) copy-start(f32[768]{0:T(1024)S(1)} %reduce.18) | copy-start | bytes 9220
  86.4 4.7 collective-permute-start
  151.7 5.2 collective-permute-start.1
  244.1 67.3 %copy-start.137 = (f32[512]{0:T(512)}, f32[512]{0:T(512)S(1)}, u32[]{:S(2)}) copy-start(f32[512]{0:T(512)S(1)} %broadcast_multiply_fusion.1) | copy-start | bytes 6148
  257.0 51.1 %slice-start.11 = ((s8[4718592]{0:T(1024)(128)(4,1)}), s8[4194304]{0:T(1024)(128)(4,1)S(1)}, s32[]{:S(2)}) async-start(s8[4718592]{0:T(1024)(128)(4,1)} %bitcast.473), calls=%async_computation.37 | async-start | bytes 8388608
  258.0 83.3 %copy-start.47 = (f32[512,768]{1,0:T(8,128)}, f32[512,768]{1,0:T(8,128)S(1)}, u32[]{:S(2)}) copy-start(f32[512,768]{1,0:T(8,128)S(1)} %get-tuple-element.140) | copy-start | bytes 4718596
  258.0 83.3 %copy-start.151 = (f32[512]{0:T(512)}, f32[512]{0:T(512)S(1)}, u32[]{:S(2)}) copy-start(f32[512]{0:T(512)S(1)} %broadcast_multiply_fusion.5) | copy-start | bytes 6148
  258.3 49.8 %copy-start.159 = (f32[512]{0:T(512)}, f32[512]{0:T(512)S(1)}, u32[]{:S(2)}) copy-start(f32[512]{0:T(512)S(1)} %multiply_reduce_fusion.20) | copy-start | bytes 6148
  260.6 80.7 %copy-start.172 = (f32[512]{0:T(512)}, f32[512]{0:T(512)S(1)}, u32[]{:S(2)}) copy-start(f32[512]{0:T(512)S(1)} %fusion.412) | copy-start | bytes 6148
  260.6 47.5 %copy-start.179 = (f32[768]{0:T(1024)S(1)}, f32[768]{0:T(1024)}, u32[]{:S(2)}) copy-start(f32[768]{0:T(1024)} %reduce.17) | copy-start | bytes 9220
  260.6 47.5 %slice-start.12 = ((s8[4718592]{0:T(1024)(128)(4,1)}), s8[524288]{0:T(1024)(128)(4,1)S(1)}, s32[]{:S(2)}) async-start(s8[4718592]{0:T(1024)(128)(4,1)} %bitcast.473), calls=%async_computation.38 | async-start | bytes 1048576
  354.8 23.5 %copy-start.87 = (bf16[12,64,512]{2,1,0:T(8,128)(2,1)}, bf16[12,64,512]{2,1,0:T(8,128)(2,1)S(1)}, u32[]{:S(2)}) copy-start(bf16[12,64,512]{2,1,0:T(8,128)(2,1)S(1)} %get-tuple-element.168) | copy-start | bytes 2359300
  381.5 8.8 collective-permute-start.3
  386.1 285.5 %reduce-scatter.44.cloned.1.call-start = ((), (), s32[]{:S(2)}) async-start(), calls=%async_computation.19 | async-start | bytes 417792
  451.2 10.7 collective-permute-start.4
  518.3 253.3 %reduce-scatter.46.cloned.1.call-start = ((), (), s32[]{:S(2)}) async-start(), calls=%async_computation.20 | async-start | bytes 417792
  520.0 377.5 %reduce-scatter.48.cloned.1.call-start = ((), (), s32[]{:S(2)}) async-start(), calls=%async_computation.21 | async-start | bytes 417792
  521.7 501.0 %reduce-scatter.52.cloned.1.call-start = ((), (), s32[]{:S(2)}) async-start(), calls=%async_computation.23 | async-start | bytes 417792
  523.5 625.2 %reduce-scatter.54.cloned.1.call-start = ((), (), s32[]{:S(2)}) async-start(), calls=%async_computation.24 | async-start | bytes 417792
  525.1 748.9 %reduce-scatter.56.cloned.1.call-start = ((), (), s32[]{:S(2)}) async-start(), calls=%async_computation.25 | async-start | bytes 417792
  528.3 872.8 %reduce-scatter.42.cloned.1.call-start = ((), (), s32[]{:S(2)}) async-start(), calls=%async_computation.18 | async-start | bytes 835584
  530.5 999.8 %reduce-scatter.50.cloned.1.call-start = ((), (), s32[]{:S(2)}) async-start(), calls=%async_computation.22 | async-start | bytes 1671168
  533.0 1129.9 %reduce-scatter.34.cloned.1.call-start = ((), (), s32[]{:S(2)}) async-start(), calls=%async_computation.14 | async-start | bytes 2506752 | tf_op jit(solution)/shard_map/reduce_scatter | solution.py:303
  538.1 1280.2 %reduce-scatter.32.cloned.1.call-start = ((), (), s32[]{:S(2)}) async-start(), calls=%async_computation.13 | async-start | bytes 7520256 | tf_op jit(solution)/shard_map/reduce_scatter | solution.py:303
  554.4 1440.0 %reduce-scatter.36.cloned.1.call-start = ((), (), s32[]{:S(2)}) async-start(), calls=%async_computation.15 | async-start | bytes 10027008 | tf_op jit(solution)/shard_map/reduce_scatter | solution.py:303
  574.7 1596.8 %reduce-scatter.38.cloned.1.call-start = ((), (), s32[]{:S(2)}) async-start(), calls=%async_computation.16 | async-start | bytes 10027008 | tf_op jit(solution)/shard_map/reduce_scatter | solution.py:303
  621.2 26.0 %copy-start.79 = (f32[768]{0:T(1024)S(1)}, f32[768]{0:T(1024)}, u32[]{:S(2)}) copy-start(f32[768]{0:T(1024)} %copy-done.77) | copy-start | bytes 9220
  621.3 26.0 %copy-start.102 = (f32[768]{0:T(1024)S(1)}, f32[768]{0:T(1024)}, u32[]{:S(2)}) copy-start(f32[768]{0:T(1024)} %copy-done.100) | copy-start | bytes 9220
  621.3 26.0 %copy-start.135 = (f32[512]{0:T(512)S(1)}, f32[512]{0:T(512)}, u32[]{:S(2)}) copy-start(f32[512]{0:T(512)} %copy-done.134) | copy-start | bytes 6148
  658.6 6.3 collective-permute-start.2
  (218 other events, 1139.7 us)
Sparse Core Ops, SparseCore 0:
  386.2 125.2 reduce-scatter.39
  518.5 127.7 reduce-scatter.43
  650.9 120.6 reduce-scatter.45
  776.8 120.6 reduce-scatter.47
  902.1 120.6 reduce-scatter.51
  1028.0 120.6 reduce-scatter.53
  1153.3 120.6 reduce-scatter.55
  1279.5 121.5 reduce-scatter.41
  1406.6 123.6 reduce-scatter.49
  1536.4 126.4 reduce-scatter.33
  1668.7 149.5 reduce-scatter.31
  1824.4 169.9 reduce-scatter.35
  2001.6 169.8 reduce-scatter.37
where the time goes:
time: 2190 us; the launch traced here: 2180 us
  waiting for transfers between devices  1490 us (68%)
  matrix products  424 us (19%)
  other arithmetic  120 us (5%)
  local copies, waits for them, and re-layouts  115 us (5%)
    unnamed x22, waiting for transfers between devices  850 us
    reduce_scatter x4, waiting for transfers between devices, per_device(): lax.psum_scatter(tuple((part[None] for part in summed)), 'dp', scatter_di...  640 us
    dot_general x6, matrix products, layer_forward(): jnp.dot(active, down_weight, preferred_element_type=jnp.float32)  90.4 us
    dot_general x3, matrix products, layer_forward(): jnp.dot(normed_low, up_weight, preferred_element_type=jnp.float32) + up_bias  57.5 us
    unnamed x483, local copies, waits for them, and re-layouts  47.8 us
  transfers between devices with their start and end apart: 18, of which 12 were waited for; matrix products, arithmetic and copies ran while one was open for 13% of the time, Pallas kernels for 0%

commit v1 on v0

v1 whole, which is shorter than its diff:
```python
import functools

import jax
import jax.numpy as jnp
from jax import lax
from jax.experimental import pallas as pl
from jax.experimental.pallas import tpu as pltpu
from jax.sharding import PartitionSpec as P

HEADS = 12
HEAD_DIM = 64
MB_TOK = 512
SCALE = 0.125
EPS = 1e-06
D = 768
FF = 3072
HALF = D // 2
PAIR = 2 * HEAD_DIM
STEPS = D // PAIR
ROWS = 256
CHUNK = 768
FSTEPS = FF // CHUNK
BF = jnp.bfloat16
F32 = jnp.float32
MIB = 1 << 20

QB, VB, OB, G1, S1, DB, G2, S2, UB, HD = 0, 1, 2, 3, 4, 5, 6, 7, 8, 12
VROWS = 16


def dot(left, right, left_dim, right_dim):
    return lax.dot_general(
        left, right, (((left_dim,), (right_dim,)), ((), ())), preferred_element_type=F32
    )


def row_mean(values):
    return jnp.mean(values, axis=-1, keepdims=True)


def col_sum(values):
    return jnp.sum(values, axis=0, keepdims=True)


def pick_copy(is_own, own, other, target, sem):
    @pl.when(is_own)
    def _():
        pltpu.make_async_copy(own, target, sem).start()

    @pl.when(jnp.logical_not(is_own))
    def _():
        pltpu.make_async_copy(other, target, sem).start()


def head_masks():
    lane = lax.broadcasted_iota(jnp.int32, (1, PAIR), 1)
    first = jnp.where(lane < HEAD_DIM, 1.0, 0.0)
    return (first, 1.0 - first)


def attn_fwd_kernel(
    layer, scal, x_ref, endr_ref, endc_ref, vec_ref, wq_own, wq_rcv, wo_own, wo_rcv,
    qkv_ref, a_ref, o_ref, xh_ref, rstd_ref, n1_ref, wq, wo, bias, sems,
):
    step = pl.program_id(0)
    is_own = scal[0] == layer

    @pl.when(step == 0)
    def _():
        for part in range(3):
            cols = slice(part * D, (part + 1) * D)
            pick_copy(is_own, wq_own.at[:, cols], wq_rcv.at[:, cols], wq.at[:, cols], sems.at[part])
        pick_copy(is_own, wo_own, wo_rcv, wo, sems.at[3])
        bias[...] = jnp.where(endc_ref[...] == endr_ref[0], 0.0, -1e30)
        for part in range(3):
            cols = slice(part * D, (part + 1) * D)
            pltpu.make_async_copy(wq_own.at[:, cols], wq.at[:, cols], sems.at[part]).wait()
            for tile in range(3):
                here = slice(part * D + tile * 256, part * D + (tile + 1) * 256)
                local = slice(tile * 256, (tile + 1) * 256)
                value = dot(x_ref[...], wq[:, here], 1, 0)
                if part == 0:
                    value = (value + vec_ref[QB : QB + 1, local]) * SCALE
                if part == 2:
                    value = value + vec_ref[VB : VB + 1, local]
                qkv_ref[:, here] = value.astype(BF)

    off = pl.multiple_of(step * PAIR, PAIR)
    q = qkv_ref[:, pl.ds(off, PAIR)]
    k = qkv_ref[:, pl.ds(pl.multiple_of(off + D, PAIR), PAIR)]
    v = qkv_ref[:, pl.ds(pl.multiple_of(off + 2 * D, PAIR), PAIR)]
    masks = head_masks()
    outs = [None] * (MB_TOK // ROWS)
    for head in range(2):
        mask = masks[head].astype(BF)
        kh = k * mask
        vh = v * mask
        for block in range(MB_TOK // ROWS):
            rows = slice(block * ROWS, (block + 1) * ROWS)
            s = dot(q[rows], kh, 1, 1) + bias[rows, :]
            peak = jnp.max(s, axis=-1, keepdims=True)
            p = jnp.exp(s - peak)
            total = jnp.sum(p, axis=-1, keepdims=True)
            a = (p * (1.0 / total)).astype(BF)
            a_ref[head, rows, :] = a
            o = dot(a, vh, 1, 0)
            outs[block] = o if outs[block] is None else outs[block] + o
    for block in range(MB_TOK // ROWS):
        o_ref[block * ROWS : (block + 1) * ROWS, pl.ds(off, PAIR)] = outs[block].astype(BF)

    @pl.when(step == STEPS - 1)
    def _():
        pltpu.make_async_copy(wo_own, wo, sems.at[3]).wait()
        for block in range(MB_TOK // ROWS):
            rows = slice(block * ROWS, (block + 1) * ROWS)
            r1 = x_ref[rows, :].astype(F32) + dot(o_ref[rows, :], wo[...], 1, 0) + vec_ref[OB : OB + 1, :]
            center = r1 - row_mean(r1)
            rstd = lax.rsqrt(row_mean(center * center) + EPS)
            xh = center * rstd
            xh_ref[rows, :] = xh
            rstd_ref[rows, :] = rstd
            n1_ref[rows, :] = (xh * vec_ref[G1 : G1 + 1, :] + vec_ref[S1 : S1 + 1, :]).astype(BF)


def whole(shape):
    return pl.BlockSpec(shape, lambda i, s: (0,) * len(shape))


ANY = pl.BlockSpec(memory_space=pl.ANY)
DMA = pltpu.SemaphoreType.DMA


def params(limit, **more):
    return pltpu.CompilerParams(vmem_limit_bytes=limit * MIB, dimension_semantics=("arbitrary",), **more)


def cost(flops, nbytes, trans=0):
    return pl.CostEstimate(flops=int(flops), bytes_accessed=int(nbytes), transcendentals=int(trans))


def attn_fwd(layer, scal, x, endr, endc, vec, wq_own, wq_rcv, wo_own, wo_rcv):
    t = MB_TOK
    x_spec = pl.BlockSpec((t, D), (lambda i, s: (s[0], 0)) if x.shape[0] > t else (lambda i, s: (0, 0)))
    return pl.pallas_call(
        functools.partial(attn_fwd_kernel, layer),
        grid_spec=pltpu.PrefetchScalarGridSpec(
            num_scalar_prefetch=1,
            grid=(STEPS,),
            in_specs=[
                x_spec,
                pl.BlockSpec((1, 1, t), lambda i, s: (s[0], 0, 0)),
                pl.BlockSpec((t, 1), lambda i, s: (s[0], 0)),
                whole((VROWS, D)),
                ANY, ANY, ANY, ANY,
            ],
            out_specs=[
                whole((t, 3 * D)),
                pl.BlockSpec((2, t, t), lambda i, s: (i, 0, 0)),
                whole((t, D)),
                whole((t, D)),
                whole((t, 1)),
                whole((t, D)),
            ],
            scratch_shapes=[
                pltpu.VMEM((D, 3 * D), BF),
                pltpu.VMEM((D, D), BF),
                pltpu.VMEM((t, t), F32),
                DMA((4,)),
            ],
        ),
        out_shape=[
            jax.ShapeDtypeStruct((t, 3 * D), BF),
            jax.ShapeDtypeStruct((HEADS, t, t), BF),
            jax.ShapeDtypeStruct((t, D), BF),
            jax.ShapeDtypeStruct((t, D), F32),
            jax.ShapeDtypeStruct((t, 1), F32),
            jax.ShapeDtypeStruct((t, D), BF),
        ],
        compiler_params=params(40),
        cost_estimate=cost(8e9, 20e6, HEADS * t * t),
        name="attention_forward",
    )(scal, x, endr, endc, vec, wq_own, wq_rcv, wo_own, wo_rcv)


def erf_tail(magnitude, bell):
    t = 1.0 / (1.0 + (0.3275911 * 0.7071067811865476) * magnitude)
    poly = 0.5 * 1.061405429
    for factor in (-1.453152027, 1.421413741, -0.284496736, 0.254829592):
        poly = poly * t + 0.5 * factor
    return poly * t * bell


def gelu_and_slope(u):
    bell = jnp.exp(u * u * -0.5)
    tail = erf_tail(jnp.abs(u), bell)
    cdf = jnp.where(u < 0.0, tail, 1.0 - tail)
    value = u * cdf
    return value, cdf + u * bell * 0.3989422804014327


def ffn_fwd_kernel(
    layer, scal, n1_ref, xh1_ref, vec_ref, wu_own, wu_rcv, wd_own, wd_rcv,
    g_ref, gp_ref, h_ref, xh2_ref, rstd_ref, wu, wd, acc, sems,
):
    step = pl.program_id(0)
    is_own = scal[0] == layer

    @pl.when(step == 0)
    def _():
        for part in range(FSTEPS):
            cols = slice(part * CHUNK, (part + 1) * CHUNK)
            pick_copy(is_own, wu_own.at[:, cols], wu_rcv.at[:, cols], wu.at[part], sems.at[part])
            pick_copy(is_own, wd_own.at[cols], wd_rcv.at[cols], wd.at[part], sems.at[FSTEPS + part])

    pltpu.make_async_copy(wu_own.at[:, :CHUNK], wu.at[step], sems.at[step]).wait()
    pltpu.make_async_copy(wd_own.at[:CHUNK], wd.at[step], sems.at[FSTEPS + step]).wait()
    up_bias = vec_ref[pl.ds(UB + step, 1), :]
    for block in range(MB_TOK // ROWS):
        rows = slice(block * ROWS, (block + 1) * ROWS)
        total = None
        for tile in range(CHUNK // 256):
            cols = slice(tile * 256, (tile + 1) * 256)
            u = dot(n1_ref[rows, :], wu[step, :, cols], 1, 0) + up_bias[:, cols]
            value, slope = gelu_and_slope(u)
            value = value.astype(BF)
            g_ref[rows, cols] = value
            gp_ref[rows, cols] = slope.astype(BF)
        total = dot(g_ref[rows, :], wd[step], 1, 0)

        @pl.when(step == 0)
        def _():
            acc[rows, :] = total

        @pl.when(step > 0)
        def _():
            acc[rows, :] += total

    @pl.when(step == FSTEPS - 1)
    def _():
        for block in range(MB_TOK // ROWS):
            rows = slice(block * ROWS, (block + 1) * ROWS)
            n1 = xh1_ref[rows, :] * vec_ref[G1 : G1 + 1, :] + vec_ref[S1 : S1 + 1, :]
            r2 = n1 + acc[rows, :] + vec_ref[DB : DB + 1, :]
            center = r2 - row_mean(r2)
            rstd = lax.rsqrt(row_mean(center * center) + EPS)
            xh = center * rstd
            xh2_ref[rows, :] = xh
            rstd_ref[rows, :] = rstd
            h_ref[rows, :] = (xh * vec_ref[G2 : G2 + 1, :] + vec_ref[S2 : S2 + 1, :]).astype(BF)


def ffn_fwd(layer, scal, n1, xh1, vec, wu_own, wu_rcv, wd_own, wd_rcv):
    t = MB_TOK
    return pl.pallas_call(
        functools.partial(ffn_fwd_kernel, layer),
        grid_spec=pltpu.PrefetchScalarGridSpec(
            num_scalar_prefetch=1,
            grid=(FSTEPS,),
            in_specs=[whole((t, D)), whole((t, D)), whole((VROWS, D)), ANY, ANY, ANY, ANY],
            out_specs=[
                pl.BlockSpec((t, CHUNK), lambda i, s: (0, i)),
                pl.BlockSpec((t, CHUNK), lambda i, s: (0, i)),
                whole((t, D)),
                whole((t, D)),
                whole((t, 1)),
            ],
            scratch_shapes=[
                pltpu.VMEM((FSTEPS, D, CHUNK), BF),
                pltpu.VMEM((FSTEPS, CHUNK, D), BF),
                pltpu.VMEM((t, D), F32),
                DMA((2 * FSTEPS,)),
            ],
        ),
        out_shape=[
            jax.ShapeDtypeStruct((t, FF), BF),
            jax.ShapeDtypeStruct((t, FF), BF),
            jax.ShapeDtypeStruct((t, D), BF),
            jax.ShapeDtypeStruct((t, D), F32),
            jax.ShapeDtypeStruct((t, 1), F32),
        ],
        compiler_params=params(40),
        cost_estimate=cost(6e9, 20e6, t * FF),
        name="feed_forward",
    )(scal, n1, xh1, vec, wu_own, wu_rcv, wd_own, wd_rcv)


def norm_back(cot, xh, rstd, gain):
    scaled = cot * gain
    return rstd * (scaled - row_mean(scaled) - xh * row_mean(scaled * xh))


def keep_or_send(section, half, keep_ref, send_ref, index, value):
    @pl.when(section == half)
    def _():
        keep_ref[index] = value

    @pl.when(section != half)
    def _():
        send_ref[index] = value


def ffn_bwd_kernel(
    layer, top, scal, cot_ref, *refs
):
    if top:
        endc_ref, termc_ref, head_ref, *refs = refs
    (
        xh2_ref, rstd2_ref, gp_ref, vec_ref, xh1_ref, rstd1_ref, wu_own, wu_rcv, wd_own, wd_rcv,
        dyk_ref, dys_ref, duk_ref, dus_ref, dr1_ref, db_ref, dbs_ref, vg_ref, *refs
    ) = refs
    if top:
        z_ref, *refs = refs
    wu, wd, dr2, dy, acc, sems = refs
    step = pl.program_id(0)
    section = scal[0]
    is_own = section == layer

    @pl.when(step == 0)
    def _():
        for part in range(FSTEPS):
            cols = slice(part * CHUNK, (part + 1) * CHUNK)
            pick_copy(is_own, wd_own.at[cols], wd_rcv.at[cols], wd.at[part], sems.at[FSTEPS + part])
            pick_copy(is_own, wu_own.at[:, cols], wu_rcv.at[:, cols], wu.at[part], sems.at[part])
        vg_ref[...] = jnp.zeros((VROWS, D), F32)
        for block in range(MB_TOK // ROWS):
            rows = slice(block * ROWS, (block + 1) * ROWS)
            xh = xh2_ref[rows, :]
            cot = cot_ref[rows, :].astype(F32)
            if top:
                live = jnp.where(endc_ref[rows, :] > 0, 1.0, 0.0)
                output = xh * vec_ref[G2 : G2 + 1, :] + vec_ref[S2 : S2 + 1, :]
                head = head_ref[...]
                z = jnp.sum(output * head, axis=-1, keepdims=True)
                z_ref[rows, :] = z
                slope = live * termc_ref[rows, :] / (1.0 + jnp.exp(-z))
                cot = live * cot + slope * head
                vg_ref[HD : HD + 1, :] += col_sum(slope * output)
            vg_ref[G2 : G2 + 1, :] += col_sum(cot * xh)
            vg_ref[S2 : S2 + 1, :] += col_sum(cot)
            d_second = norm_back(cot, xh, rstd2_ref[rows, :], vec_ref[G2 : G2 + 1, :])
            low = d_second.astype(BF)
            dr2[rows, :] = d_second
            dy[rows, :] = low
            vg_ref[DB : DB + 1, :] += col_sum(low.astype(F32))
            for half in range(2):
                keep_or_send(
                    section, half, dyk_ref, dys_ref, (rows, slice(None)), low[:, half * HALF : (half + 1) * HALF]
                )

    pltpu.make_async_copy(wd_own.at[:CHUNK], wd.at[step], sems.at[FSTEPS + step]).wait()
    pltpu.make_async_copy(wu_own.at[:, :CHUNK], wu.at[step], sems.at[step]).wait()
    per_half = FSTEPS // 2
    local = pl.multiple_of((step % per_half) * CHUNK, CHUNK)
    bias_total = None
    for block in range(MB_TOK // ROWS):
        rows = slice(block * ROWS, (block + 1) * ROWS)
        d_active = dot(dy[rows, :], wd[step], 1, 1)
        d_up = (d_active * gp_ref[rows, :].astype(F32)).astype(BF)
        part = col_sum(d_up.astype(F32))
        bias_total = part if bias_total is None else bias_total + part

        @pl.when(section == step // per_half)
        def _():
            duk_ref[rows, pl.ds(local, CHUNK)] = d_up

        @pl.when(section != step // per_half)
        def _():
            dus_ref[rows, pl.ds(local, CHUNK)] = d_up

        total = dot(d_up, wu[step], 1, 1)

        @pl.when(step == 0)
        def _():
            acc[rows, :] = total + dr2[rows, :]

        @pl.when(step > 0)
        def _():
            acc[rows, :] += total

    vg_ref[pl.ds(UB + step, 1), :] = bias_total

    @pl.when(step == FSTEPS - 1)
    def _():
        for block in range(MB_TOK // ROWS):
            rows = slice(block * ROWS, (block + 1) * ROWS)
            cot = acc[rows, :]
            xh = xh1_ref[rows, :]
            vg_ref[G1 : G1 + 1, :] += col_sum(cot * xh)
            vg_ref[S1 : S1 + 1, :] += col_sum(cot)
            d_first = norm_back(cot, xh, rstd1_ref[rows, :], vec_ref[G1 : G1 + 1, :])
            low = d_first.astype(BF)
            dr1_ref[rows, :] = d_first
            db_ref[rows, :] = low
            vg_ref[OB : OB + 1, :] += col_sum(low.astype(F32))
            for half in range(2):

                @pl.when(section != half)
                def _():
                    dbs_ref[rows, :] = low[:, half * HALF : (half + 1) * HALF]


def ffn_bwd(layer, scal, cot, top_args, xh2, rstd2, gp, vec, xh1, rstd1, wu_own, wu_rcv, wd_own, wd_rcv):
    t = MB_TOK
    top = top_args is not None
    cot_spec = pl.BlockSpec((t, D), (lambda i, s: (s[0], 0)) if cot.shape[0] > t else (lambda i, s: (0, 0)))
    col = pl.BlockSpec((t, 1), lambda i, s: (s[0], 0))
    in_specs = [cot_spec] + ([col, col, whole((1, D))] if top else []) + [
        whole((t, D)),
        whole((t, 1)),
        pl.BlockSpec((t, CHUNK), lambda i, s: (0, i)),
        whole((VROWS, D)),
        whole((t, D)),
        whole((t, 1)),
        ANY, ANY, ANY, ANY,
    ]
    outs = [
        ((t, HALF), BF), ((t, HALF), BF), ((t, FF // 2), BF), ((t, FF // 2), BF),
        ((t, D), F32), ((t, D), BF), ((t, HALF), BF), ((VROWS, D), F32),
    ] + ([((t, 1), F32)] if top else [])
    args = [cot] + (list(top_args) if top else []) + [
        xh2, rstd2, gp, vec, xh1, rstd1, wu_own, wu_rcv, wd_own, wd_rcv
    ]
    return pl.pallas_call(
        functools.partial(ffn_bwd_kernel, layer, top),
        grid_spec=pltpu.PrefetchScalarGridSpec(
            num_scalar_prefetch=1,
            grid=(FSTEPS,),
            in_specs=in_specs,
            out_specs=[whole(shape) for shape, _ in outs],
            scratch_shapes=[
                pltpu.VMEM((FSTEPS, D, CHUNK), BF),
                pltpu.VMEM((FSTEPS, CHUNK, D), BF),
                pltpu.VMEM((t, D), F32),
                pltpu.VMEM((t, D), BF),
                pltpu.VMEM((t, D), F32),
                DMA((2 * FSTEPS,)),
            ],
        ),
        out_shape=[jax.ShapeDtypeStruct(shape, kind) for shape, kind in outs],
        compiler_params=params(46),
        cost_estimate=cost(6e9, 24e6),
        name="feed_forward_backward",
    )(scal, *args)


def attn_bwd_kernel(
    layer, scal, db_ref, dr1_ref, o_ref, qkv_ref, a_ref, vgin_ref, wq_own, wq_rcv, wo_own, wo_rcv,
    dk_ref, ds_ref, dx_ref, vg_ref, wq, wo, dmix, full, sems,
):
    step = pl.program_id(0)
    section = scal[0]
    is_own = section == layer

    @pl.when(step == 0)
    def _():
        pick_copy(is_own, wo_own, wo_rcv, wo, sems.at[0])
        pick_copy(is_own, wq_own, wq_rcv, wq, sems.at[1])
        vg_ref[...] = vgin_ref[...]
        pltpu.make_async_copy(wo_own, wo, sems.at[0]).wait()
        for tile in range(3):
            cols = slice(tile * 256, (tile + 1) * 256)
            dmix[:, cols] = dot(db_ref[...], wo[cols, :], 1, 1).astype(BF)

    off = pl.multiple_of(step * PAIR, PAIR)
    q = qkv_ref[:, pl.ds(off, PAIR)]
    k = qkv_ref[:, pl.ds(pl.multiple_of(off + D, PAIR), PAIR)]
    v = qkv_ref[:, pl.ds(pl.multiple_of(off + 2 * D, PAIR), PAIR)]
    do = dmix[:, pl.ds(off, PAIR)]
    o = o_ref[:, pl.ds(off, PAIR)]
    product = do.astype(F32) * o.astype(F32)
    masks = head_masks()
    d_q = [None] * (MB_TOK // ROWS)
    d_k = None
    d_v = None
    for head in range(2):
        mask = masks[head].astype(BF)
        kh = k * mask
        vh = v * mask
        qh = q * mask
        doh = do * mask
        inner = jnp.sum(product * masks[head], axis=-1, keepdims=True)
        for block in range(MB_TOK // ROWS):
            rows = slice(block * ROWS, (block + 1) * ROWS)
            a = a_ref[head, rows, :]
            dp = dot(do[rows], vh, 1, 1)
            d_s = (a.astype(F32) * (dp - inner[rows])).astype(BF)
            more_v = dot(a, doh[rows], 0, 0)
            more_q = dot(d_s, kh, 1, 0)
            more_k = dot(d_s, qh[rows], 0, 0)
            d_v = more_v if d_v is None else d_v + more_v
            d_k = more_k if d_k is None else d_k + more_k
            d_q[block] = more_q if d_q[block] is None else d_q[block] + more_q
    d_q = jnp.concatenate(d_q, axis=0).astype(BF) * jnp.asarray(SCALE, BF)
    d_k = d_k.astype(BF)
    d_v = d_v.astype(BF)
    vg_ref[QB : QB + 1, pl.ds(off, PAIR)] = col_sum(d_q.astype(F32))
    vg_ref[VB : VB + 1, pl.ds(off, PAIR)] = col_sum(d_v.astype(F32))
    per_half = STEPS // 2
    for part, value in enumerate((d_q, d_k, d_v)):
        full[:, pl.ds(pl.multiple_of(part * D + off, PAIR), PAIR)] = value
        here = pl.multiple_of(part * HALF + (step % per_half) * PAIR, PAIR)

        @pl.when(section == step // per_half)
        def _():
            dk_ref[:, pl.ds(here, PAIR)] = value

        @pl.when(section != step // per_half)
        def _():
            ds_ref[:, pl.ds(here, PAIR)] = value

    @pl.when(step == STEPS - 1)
    def _():
        pltpu.make_async_copy(wq_own, wq, sems.at[1]).wait()
        for tile in range(3):
            cols = slice(tile * 256, (tile + 1) * 256)
            dx = dr1_ref[:, cols] + dot(full[...], wq[cols, :], 1, 1)
            dx_ref[:, cols] = dx.astype(BF)


def attn_bwd(layer, scal, db, dr1, o, qkv, a, vgin, wq_own, wq_rcv, wo_own, wo_rcv):
    t = MB_TOK
    outs = [((t, 3 * HALF), BF), ((t, 3 * HALF), BF), ((t, D), BF), ((VROWS, D), F32)]
    return pl.pallas_call(
        functools.partial(attn_bwd_kernel, layer),
        grid_spec=pltpu.PrefetchScalarGridSpec(
            num_scalar_prefetch=1,
            grid=(STEPS,),
            in_specs=[
                whole((t, D)), whole((t, D)), whole((t, D)), whole((t, 3 * D)),
                pl.BlockSpec((2, t, t), lambda i, s: (i, 0, 0)),
                whole((VROWS, D)),
                ANY, ANY, ANY, ANY,
            ],
            out_specs=[whole(shape) for shape, _ in outs],
            scratch_shapes=[
                pltpu.VMEM((D, 3 * D), BF),
                pltpu.VMEM((D, D), BF),
                pltpu.VMEM((t, D), BF),
                pltpu.VMEM((t, 3 * D), BF),
                DMA((2,)),
            ],
        ),
        out_shape=[jax.ShapeDtypeStruct(shape, kind) for shape, kind in outs],
        compiler_params=params(46),
        cost_estimate=cost(12e9, 20e6),
        name="attention_backward",
    )(scal, db, dr1, o, qkv, a, vgin, wq_own, wq_rcv, wo_own, wo_rcv)


def split_rows(value, first_block, count, height, bit, my_bit, keep_ref, send_ref, col_index):
    for kept in range(2):

        @pl.when(my_bit == kept)
        def _():
            for block in range(count):
                number = first_block + block
                has = (number // bit) % 2
                place = (block // (2 * bit)) * bit + block % bit
                target = keep_ref if has == kept else send_ref
                target[place, col_index] = value[block * height : (block + 1) * height].astype(BF)


def transposed(left):
    return left.T


def wgrad_down_kernel(n, bit, bit_at, scal, g_own, g_rcv, dy_own, dy_rcv, keep_ref, send_ref):
    value = dot(g_own[...], dy_own[...], 0, 0) + dot(g_rcv[...], dy_rcv[...], 0, 0)
    tall = FF // n
    height = D // n
    count = HALF // tall
    my_bit = scal[bit_at]
    for kept in range(2):

        @pl.when(my_bit == kept)
        def _():
            for block in range(count):
                has = (block // bit) % 2
                place = (block // (2 * bit)) * bit + block % bit
                target = keep_ref if has == kept else send_ref
                for part in range(4):
                    top = block * tall + part * height
                    target[place, part] = value[top : top + height].astype(BF)


def wgrad_down(n, bit, bit_at, scal, g_own, g_rcv, dy_own, dy_rcv):
    t = MB_TOK
    height = D // n
    chunks = FF // HALF
    per = (n // 2) // chunks
    spec = pl.BlockSpec((t, HALF), lambda i, s: (0, i))
    shape = jax.ShapeDtypeStruct((n // 2, 4, height, HALF), BF)
    out_spec = pl.BlockSpec((per, 4, height, HALF), lambda i, s: (i, 0, 0, 0))
    return pl.pallas_call(
        functools.partial(wgrad_down_kernel, n, bit, bit_at),
        grid_spec=pltpu.PrefetchScalarGridSpec(
            num_scalar_prefetch=1,
            grid=(chunks,),
            in_specs=[spec, spec, whole((t, HALF)), whole((t, HALF))],
            out_specs=[out_spec, out_spec],
        ),
        out_shape=[shape, shape],
        compiler_params=params(40),
        cost_estimate=cost(3e9, 10e6),
        name="down_gradient",
    )(scal, g_own, g_rcv, dy_own, dy_rcv)


def wgrad_up_kernel(n, bit, bit_at, scal, a_own, a_rcv, b_own, b_rcv, keep_ref, send_ref):
    height = D // n
    a_left = a_own[...].T
    a_right = a_rcv[...].T
    for col in range(4):
        cols = slice(col * HALF, (col + 1) * HALF)
        value = dot(a_left, b_own[:, cols], 1, 0) + dot(a_right, b_rcv[:, cols], 1, 0)
        split_rows(value, 0, n // 2, height, bit, scal[bit_at], keep_ref, send_ref, col)


def wgrad_up(n, bit, bit_at, scal, a_own, a_rcv, b_own, b_rcv):
    t = MB_TOK
    height = D // n
    spec = pl.BlockSpec((t, HALF), lambda i, s: (0, i))
    shape = jax.ShapeDtypeStruct((n // 2, 4, height, HALF), BF)
    out_spec = pl.BlockSpec((n // 4, 4, height, HALF), lambda i, s: (i, 0, 0, 0))
    return pl.pallas_call(
        functools.partial(wgrad_up_kernel, n, bit, bit_at),
        grid_spec=pltpu.PrefetchScalarGridSpec(
            num_scalar_prefetch=1,
            grid=(2,),
            in_specs=[spec, spec, whole((t, FF // 2)), whole((t, FF // 2))],
            out_specs=[out_spec, out_spec],
        ),
        out_shape=[shape, shape],
        compiler_params=params(40),
        cost_estimate=cost(3e9, 10e6),
        name="up_gradient",
    )(scal, a_own, a_rcv, b_own, b_rcv)


def wgrad_attn_kernel(
    n, bits, bits_at, scal, x_own, x_rcv, o_own, o_rcv, p_own, p_rcv, b_own, b_rcv,
    keep_p, send_p, keep_q, send_q,
):
    height = D // n
    x_left = x_own[...].T
    x_right = x_rcv[...].T
    for col in range(3):
        cols = slice(col * HALF, (col + 1) * HALF)
        value = dot(x_left, p_own[:, cols], 1, 0) + dot(x_right, p_rcv[:, cols], 1, 0)
        which = 0 if col < 2 else 1
        keep, send = ((keep_p, send_p), (keep_q, send_q))[which]
        split_rows(value, 0, n // 2, height, bits[which], scal[bits_at[which]], keep, send, col % 2)
    value = dot(o_own[...].T, b_own[...], 1, 0) + dot(o_rcv[...].T, b_rcv[...], 1, 0)
    split_rows(value, 0, n // 2, height, bits[1], scal[bits_at[1]], keep_q, send_q, 1)


def wgrad_attn(n, bits, bits_at, scal, x_own, x_rcv, o_own, o_rcv, p_own, p_rcv, db, b_rcv):
    t = MB_TOK
    height = D // n
    spec = pl.BlockSpec((t, HALF), lambda i, s: (0, i))
    if x_own.shape[0] > t:
        x_spec = pl.BlockSpec((t, HALF), lambda i, s: (s[0], i))
        y_spec = pl.BlockSpec((t, HALF), lambda i, s: (1 - s[0], i))
    else:
        x_spec = y_spec = spec
    shape = jax.ShapeDtypeStruct((n // 2, 2, height, HALF), BF)
    out_spec = pl.BlockSpec((n // 4, 2, height, HALF), lambda i, s: (i, 0, 0, 0))
    return pl.pallas_call(
        functools.partial(wgrad_attn_kernel, n, bits, bits_at),
        grid_spec=pltpu.PrefetchScalarGridSpec(
            num_scalar_prefetch=1,
            grid=(2,),
            in_specs=[
                x_spec, y_spec, spec, spec,
                whole((t, 3 * HALF)), whole((t, 3 * HALF)),
                pl.BlockSpec((t, HALF), lambda i, s: (0, s[0])),
                whole((t, HALF)),
            ],
            out_specs=[out_spec] * 4,
        ),
        out_shape=[shape] * 4,
        compiler_params=params(40),
        cost_estimate=cost(3e9, 10e6),
        name="attention_gradients",
    )(scal, x_own, x_rcv, o_own, o_rcv, p_own, p_rcv, db, b_rcv)


SWAP = [(0, 1), (1, 0)]


def swap(array):
    return lax.ppermute(array, "section", SWAP)


def across(array, bit, n):
    return lax.ppermute(array, "dp", [(i, i ^ bit) for i in range(n)])


class Halving:
    def __init__(self, n, parts, dims):
        self.n = n
        self.dims = list(dims)
        tail = parts[0].shape[1:]
        self.parts = [part.reshape((2,) * len(self.dims) + tail) for part in parts]

    def outgoing(self, bit, index):
        place = self.dims.index(bit)
        mine = (index // bit) % 2
        total = None
        for part in self.parts:
            piece = lax.dynamic_index_in_dim(part, 1 - mine, place, keepdims=False).astype(F32)
            total = piece if total is None else total + piece
        self.parts = [lax.dynamic_index_in_dim(part, mine, place, keepdims=False) for part in self.parts]
        self.dims.pop(place)
        return total.astype(BF)

    def add(self, received):
        self.parts.append(received)

    def total(self):
        total = None
        for part in self.parts:
            piece = part.astype(F32)
            total = piece if total is None else total + piece
        return total


def bits_down(n, without):
    return [1 << place for place in reversed(range(n.bit_length() - 1)) if (1 << place) != without]


def reduce_pair(n, index, first, second, orders):
    chains = []
    for (keep, send), order in zip((first, second), orders):
        received = across(send, order[0], n)
        chains.append(Halving(n, [keep, received], bits_down(n, order[0])))
    for place in range(1, len(orders[0])):
        bits = [order[place] for order in orders]
        sends = [chain.outgoing(bit, index) for chain, bit in zip(chains, bits)]
        if bits[0] == bits[1]:
            received = across(jnp.concatenate([s.reshape((-1,) + s.shape[-2:]) for s in sends], axis=0), bits[0], n)
            cut = received.shape[0] // 2
            pieces = [received[:cut].reshape(sends[0].shape), received[cut:].reshape(sends[1].shape)]
        else:
            pieces = [across(s, bit, n) for s, bit in zip(sends, bits)]
        for chain, piece in zip(chains, pieces):
            chain.add(piece)
    return [chain.total() for chain in chains]


def per_device(
    tokens, seq_ends, qkv_weight, qv_bias, out_weight, out_bias, gain_one, shift_one, up_weight, up_bias,
    down_weight, down_bias, gain_two, shift_two, head_weight, out_cotangent, term_cotangent,
):
    n = lax.axis_size("dp")
    section = lax.axis_index("section")
    index = lax.axis_index("dp")
    is_first = section == 0
    if n == 16:
        orders = ([1, 2, 4, 8], [2, 1, 4, 8])
    else:
        ups = [1 << place for place in range(n.bit_length() - 1)]
        orders = (ups, ups[2:4] + ups[:2] + ups[4:])
    first_bits = (orders[0][0], orders[1][0])
    scal = jnp.stack([section, (index // first_bits[0]) % 2, (index // first_bits[1]) % 2]).astype(jnp.int32)

    wq, wo, wu, wd = qkv_weight[0], out_weight[0], up_weight[0], down_weight[0]
    wq_r = swap(wq)
    vec_own = jnp.concatenate(
        [
            qv_bias[0].reshape(2, D), out_bias, gain_one, shift_one, down_bias, gain_two, shift_two,
            up_bias[0].reshape(4, D), jnp.zeros((4, D), F32),
        ],
        axis=0,
    )
    vec_r = swap(vec_own)
    wo_r = swap(wo)
    wu_r = swap(wu)
    wd_r = swap(wd)
    vecs = (jnp.where(is_first, vec_own, vec_r), jnp.where(is_first, vec_r, vec_own))

    endr = seq_ends.reshape(2, 1, MB_TOK)
    endc = seq_ends.reshape(2 * MB_TOK, 1)
    termc = term_cotangent.reshape(2 * MB_TOK, 1)
    head = head_weight.astype(F32).reshape(1, D)

    kept = []
    x = tokens
    for layer in range(2):
        qkv, a, o, xh1, rstd1, n1 = attn_fwd(layer, scal, x, endr, endc, vecs[layer], wq, wq_r, wo, wo_r)
        o_r, n1_r = swap(o), swap(n1)
        g, gp, h, xh2, rstd2 = ffn_fwd(layer, scal, n1, xh1, vecs[layer], wu, wu_r, wd, wd_r)
        g_r = swap(g)
        h_r = swap(h)
        kept.append((x, qkv, a, o, o_r, xh1, rstd1, n1, n1_r, g, g_r, gp, xh2, rstd2, h, h_r))
        x = h

    cot = out_cotangent
    top_args = (endc, termc, head)
    sums = [None, None]
    vgs = [None, None]
    for layer in (1, 0):
        x, qkv, a, o, o_r, xh1, rstd1, n1, n1_r, g, g_r, gp, xh2, rstd2, h, h_r = kept[layer]
        got = ffn_bwd(
            layer, scal, cot, top_args if layer else None, xh2, rstd2, gp, vecs[layer], xh1, rstd1, wu, wu_r, wd, wd_r
        )
        dyk, dys, duk, dus, dr1, db, dbs, vg = got[:8]
        if layer:
            z = got[8]
        dy_r, du_r, db_r = swap(dys), swap(dus), swap(dbs)
        down = wgrad_down(n, first_bits[0], 1, scal, g, g_r, dyk, dy_r)
        up = wgrad_up(n, first_bits[1], 2, scal, n1, n1_r, duk, du_r)
        ffn_sums = reduce_pair(n, index, down, up, orders)
        dpk, dps, dx, vg = attn_bwd(layer, scal, db, dr1, o, qkv, a, vg, wq, wq_r, wo, wo_r)
        dp_r = swap(dps)
        x_r = x if layer == 0 else kept[0][15]
        got = wgrad_attn(n, first_bits, (1, 2), scal, x, x_r, o, o_r, dpk, dp_r, db, db_r)
        attn_sums = reduce_pair(n, index, got[:2], got[2:], orders)
        sums[layer] = ffn_sums + attn_sums
        vgs[layer] = vg
        if layer:
            d_top = dx
        cot = dx
    d_low = cot

    vg = jnp.stack(vgs)
    vg = vg + swap(vg)
    for bit in orders[0]:
        vg = vg + across(vg, bit, n)
    mine = jnp.where(is_first, vg[0], vg[1])
    small = D // n

    def share(rows):
        flat = mine[rows].reshape(-1)
        width = flat.shape[0] // n
        return lax.dynamic_slice(flat, (index * width,), (width,))[None]

    head_share = lax.dynamic_slice(vg[1, HD], (index * small,), (small,)).reshape(-1, 2)
    head_out = jnp.where(is_first, head_share[:, 0], head_share[:, 1])[:, None]

    own = [jnp.where(is_first, low, high) for low, high in zip(*sums)]
    other = [swap(jnp.where(is_first, high, low)) for low, high in zip(*sums)]
    left = [jnp.where(is_first, a, b) for a, b in zip(own, other)]
    right = [jnp.where(is_first, b, a) for a, b in zip(own, other)]
    down, up, two, vo = [jnp.stack([a, b]) for a, b in zip(left, right)]
    grad_down = down.transpose(1, 2, 0, 3).reshape(1, FF // n, D)
    grad_up = up.transpose(2, 0, 1, 3).reshape(1, small, FF)
    qkv_parts = jnp.concatenate([two, vo[:, :1]], axis=1)
    grad_qkv = qkv_parts.transpose(2, 1, 0, 3).reshape(1, small, 3 * D)
    grad_out = vo[:, 1].transpose(1, 0, 2).reshape(1, small, D)

    def both(early, late):
        (own_low, other_low), (own_high, other_high) = early, late
        first = jnp.where(is_first, own_low, other_high)
        second = jnp.where(is_first, other_low, own_high)
        return jnp.concatenate([first, second], axis=0)[None]

    hidden = both((kept[0][14], kept[0][15]), (kept[1][14], kept[1][15]))
    input_out = both((d_low, swap(d_low)), (d_top, swap(d_top)))

    z = z[:, 0]
    z_r = swap(z)
    z_all = jnp.concatenate([jnp.where(is_first, z, z_r), jnp.where(is_first, z_r, z)])
    term = jnp.where(seq_ends > 0, jax.nn.softplus(z_all), 0.0).reshape(-1, 2)
    term_out = jnp.where(is_first, term[:, 0], term[:, 1])[:, None]

    return (
        hidden,
        term_out,
        input_out,
        grad_qkv,
        share(slice(QB, VB + 1)),
        grad_out,
        share(slice(OB, OB + 1)),
        share(slice(G1, G1 + 1)),
        share(slice(S1, S1 + 1)),
        grad_up,
        share(slice(UB, UB + 4)),
        grad_down,
        share(slice(DB, DB + 1)),
        share(slice(G2, G2 + 1)),
        share(slice(S2, S2 + 1)),
        head_out,
    )


def solution(mesh):
    in_specs = (
        P("dp", None),
        P("dp"),
        P("section", None, None),
        P("section", None),
        P("section", None, None),
        P("section", None),
        P("section", None),
        P("section", None),
        P("section", None, None),
        P("section", None),
        P("section", None, None),
        P("section", None),
        P("section", None),
        P("section", None),
        P(),
        P("dp", None),
        P("dp"),
    )
    out_specs = (
        P("section", "dp", None),
        P("dp", "section"),
        P("section", "dp", None),
        P("section", "dp", None),
        P("section", "dp"),
        P("section", "dp", None),
        P("section", "dp"),
        P("section", "dp"),
        P("section", "dp"),
        P("section", "dp", None),
        P("section", "dp"),
        P("section", "dp", None),
        P("section", "dp"),
        P("section", "dp"),
        P("section", "dp"),
        P("dp", "section"),
    )
    return jax.shard_map(per_device, mesh=mesh, in_specs=in_specs, out_specs=out_specs, check_vma=False)
```

time: 2190 us -> 506 us (0.23)
  waiting for transfers between devices: 1490 us -> 192 us
  matrix products: 424 us -> 0 us
  Pallas kernels: 0 us -> 174 us
  other arithmetic: 120 us -> 35.5 us
  local copies, waits for them, and re-layouts: 115 us -> 49.9 us
  starting transfers between devices: 10.5 us -> 44.2 us
    unnamed x22 -> x0, waiting for transfers between devices: 850 us -> none
    reduce_scatter x4 -> x0, waiting for transfers between devices: 640 us -> none  [per_device(): lax.psum_scatter(tuple((part[None] for part in summed)), 'dp', scatter_di...]
    dot_general x73 -> x0, matrix products: 391 us -> none  [the longest x6 90.4 us: layer_forward(): jnp.dot(active, down_weight, preferred_element_type=jnp.float32)]
    ppermute x5 -> x57, waiting for transfers between devices: 2.18 us -> 192 us  [the longest x28 175 us: across(): return lax.ppermute(array, 'dp', [(i, i ^ bit) for i in range(n)])]
    pallas_call x0 -> x14, Pallas kernels: none -> 174 us  [the longest x2 35.5 us: ffn_bwd(): pl.pallas_call(functools.partial(ffn_bwd_kernel, layer, top), grid_spec=p...]
    reduce_sum x30 -> x0, other arithmetic: 39.1 us -> none  [the longest x3 9.99 us: layer_forward(): totals = jnp.sum(weights, axis=-1, keepdims=True)]
    convert_element_type x13 -> x20, other arithmetic: 47.9 us -> 9.58 us  [outgoing(): return total.astype(BF)]
    ppermute x5 -> x57, starting transfers between devices: 9.33 us -> 44.2 us  [the longest x28 37 us: across(): return lax.ppermute(array, 'dp', [(i, i ^ bit) for i in range(n)])]
  transfers between devices with their start and end apart: 18 -> 57, of which waited for: 12 -> 24; matrix products, arithmetic and copies ran while one was open for 13% -> 10% of each run, Pallas kernels for 0% -> 12%
where the time goes in v1:
time: 506 us; the launch traced here: 498 us
  waiting for transfers between devices  192 us (38%)
  Pallas kernels  174 us (34%)
  local copies, waits for them, and re-layouts  49.9 us (10%)
  starting transfers between devices  44.2 us (9%)
  other arithmetic  35.5 us (7%)
    ppermute x28, waiting for transfers between devices, across(): return lax.ppermute(array, 'dp', [(i, i ^ bit) for i in range(n)])  175 us
    unnamed x177, local copies, waits for them, and re-layouts  37.3 us
    ppermute x28, starting transfers between devices, across(): return lax.ppermute(array, 'dp', [(i, i ^ bit) for i in range(n)])  37 us
    pallas_call x2, Pallas kernels, ffn_bwd(): pl.pallas_call(functools.partial(ffn_bwd_kernel, layer, top), grid_spec=p...  35.5 us
    pallas_call x2, Pallas kernels, ffn_fwd(): pl.pallas_call(functools.partial(ffn_fwd_kernel, layer), grid_spec=pltpu....  32.5 us
    pallas_call x2, Pallas kernels, attn_bwd(): pl.pallas_call(functools.partial(attn_bwd_kernel, layer), grid_spec=pltpu...  32.3 us
    pallas_call x2, Pallas kernels, attn_fwd(): pl.pallas_call(functools.partial(attn_fwd_kernel, layer), grid_spec=pltpu...  30.9 us
    ppermute x29, waiting for transfers between devices, swap(): return lax.ppermute(array, 'section', SWAP)  17.4 us
  transfers between devices with their start and end apart: 57, of which 24 were waited for; matrix products, arithmetic and copies ran while one was open for 10% of the time, Pallas kernels for 12%

profile of v1, /device:TPU:0, one launch (start us, length us, event | category | flops | bytes accessed | tf_op | source)
XLA Modules:
  0.0 498.4 jit_solution(11180179576280082508)
XLA Ops:
  8.9 13.8 %collective-permute-done.2.wo_rcv = bf16[768,768]{1,0:T(8,128)(2,1)} collective-permute-done((bf16[768,768]{1,0:T(8,128)(2,1)}, bf16[768,768]{1,0:T(8,128)(2,1)}, u32[]{:S(2)}, u32[]{:S(2)}) %collective-permute-start.2) | collective-permute-done | bytes 1179680 | tf_op jit(solution)/shard_map/ppermute | solution.py:692
  26.1 14.9 %attention_forward.2 = (bf16[512,2304]{1,0:T(8,128)(2,1)S(1)}, bf16[12,512,512]{2,1,0:T(8,128)(2,1)}, bf16[512,768]{1,0:T(8,128)(2,1)S(1)}, f32[512,768]{1,0:T(8...) custom-call(s32[3]{0:T(128)S(1)} %pad_add_fusion.scal, bf16[1024,768]{1,0:T(8,128)(2,1)S(1)} %copy-done.13, ...), custom_call_target="tpu_custom_call" | custom-call | flops 8000000000 | bytes 20000000 | tf_op jit(solution)/shard_map/attention_forward/pallas_call | solution.py:144
  42.5 16.7 %feed_forward.2 = (bf16[512,3072]{1,0:T(8,128)(2,1)S(1)}, bf16[512,3072]{1,0:T(8,128)(2,1)S(1)}, bf16[512,768]{1,0:T(8,128)(2,1)S(1)}, f32[512,768]{1,0:T(8,128)S(1)}, f32[512,1]{1,0:T(8,128)S(1)}) custom-call(s32[3]{0:T(128)S(1)} %pad_add_fusion.scal, bf16[512,768]{1,0:T(8,128)(2,1)S(1)} %get-tuple-element.79.n1_ref.a_own, ...), custom_call_target="tpu_custom_call" | custom-call | flops 6000000000 | bytes 20000000 | tf_op jit(solution)/shard_map/feed_forward/pallas_call | solution.py:254
  62.1 16.0 %attention_forward.3 = (bf16[512,2304]{1,0:T(8,128)(2,1)S(1)}, bf16[12,512,512]{2,1,0:T(8,128)(2,1)}, bf16[512,768]{1,0:T(8,128)(2,1)S(1)}, f32[512,768]{1,0:T(8...) custom-call(s32[3]{0:T(128)S(1)} %pad_add_fusion.scal, ...), custom_call_target="tpu_custom_call" | custom-call | flops 8000000000 | bytes 20000000 | tf_op jit(solution)/shard_map/attention_forward/pallas_call | solution.py:144
  79.5 15.8 %feed_forward.3 = (bf16[512,3072]{1,0:T(8,128)(2,1)S(1)}, bf16[512,3072]{1,0:T(8,128)(2,1)S(1)}, bf16[512,768]{1,0:T(8,128)(2,1)S(1)}, f32[512,768]{1,0:T(8,128)S(1)}, f32[512,1]{1,0:T(8,128)S(1)}) custom-call(s32[3]{0:T(128)S(1)} %pad_add_fusion.scal, bf16[512,768]{1,0:T(8,128)(2,1)S(1)} %get-tuple-element.82.n1_ref.a_own, ...), custom_call_target="tpu_custom_call" | custom-call | flops 6000000000 | bytes 20000000 | tf_op jit(solution)/shard_map/feed_forward/pallas_call | solution.py:254
  99.7 18.8 %feed_forward_backward.2 = (bf16[512,384]{1,0:T(8,128)(2,1)S(1)}, bf16[512,384]{1,0:T(8,128)(2,1)S(1)}, bf16[512,1536]{1,0:T(8,128)(2,1)S(1)}, bf16[512,1536]{1,...) custom-call(s32[3]{0:T(128)S(1)} %pad_add_fusion.scal, ...), custom_call_target="tpu_custom_call" | custom-call | flops 6000000000 | bytes 24000000 | tf_op jit(solution)/shard_map/feed_forward_backward/pallas_call | solution.py:423
  121.6 16.7 %attention_backward.2 = (bf16[512,1152]{1,0:T(8,128)(2,1)S(1)}, bf16[512,1152]{1,0:T(8,128)(2,1)S(1)}, bf16[512,768]{1,0:T(8,128)(2,1)S(1)}, f32[16,768]{1,0:T(8,128)S(1)}) custom-call(s32[3]{0:T(128)S(1)} %pad_add_fusion.scal, bf16[512,768]{1,0:T(8,128)(2,1)S(1)} %get-tuple-element.90.db_ref.b_own, f32[512,768]{1,0:T(8,128)} %get-tuple-element.91.dr1_ref, ...), custom_call_target="tpu_custom_call" | custom-call | flops 12000000000 | bytes 20000000 | tf_op jit(solution)/shard_map/attention_backward/pallas_call | solution.py:523
  140.4 16.7 %feed_forward_backward.3 = (bf16[512,384]{1,0:T(8,128)(2,1)S(1)}, bf16[512,384]{1,0:T(8,128)(2,1)S(1)}, bf16[512,1536]{1,0:T(8,128)(2,1)S(1)}, bf16[512,1536]{1,...) custom-call(s32[3]{0:T(128)S(1)} %pad_add_fusion.scal, ...), custom_call_target="tpu_custom_call" | custom-call | flops 6000000000 | bytes 24000000 | tf_op jit(solution)/shard_map/feed_forward_backward/pallas_call | solution.py:423
  161.4 15.6 %attention_backward.3 = (bf16[512,1152]{1,0:T(8,128)(2,1)S(1)}, bf16[512,1152]{1,0:T(8,128)(2,1)S(1)}, bf16[512,768]{1,0:T(8,128)(2,1)S(1)}, f32[16,768]{1,0:T(8,128)S(1)}) custom-call(s32[3]{0:T(128)S(1)} %pad_add_fusion.scal, bf16[512,768]{1,0:T(8,128)(2,1)S(1)} %get-tuple-element.101.db_ref.b_own, f32[512,768]{1,0:T(8,128)} %copy-done.24, ...), custom_call_target="tpu_custom_call" | custom-call | flops 12000000000 | bytes 20000000 | tf_op jit(solution)/shard_map/attention_backward/pallas_call | solution.py:523
  181.7 2.9 collective-permute-start.31
  191.2 3.3 collective-permute-done.32
  196.4 2.9 collective-permute-done.33
  220.1 8.2 %attention_gradients.3 = (bf16[8,2,48,384]{3,2,1,0:T(8,128)(2,1)S(1)}, bf16[8,2,48,384]{3,2,1,0:T(8,128)(2,1)}, bf16[8,2,48,384]{3,2,1,0:T(8,128)(2,1)S(1)}, bf16[8,2,48,384]{3,2,1,0:T(8,128)(2,1)}) custom-call(s32[3]{0:T(128)S(1)} %pad_add_fusion.scal, bf16[512,768]{1,0:T(8,128)(2,1)S(1)} %get-tuple-element.81.x_ref.x_own, ...), custom_call_target="tpu_custom_call" | custom-call | flops 3000000000 | bytes 10000000 | tf_op jit(solution)/shard_map/attention_gradients/pallas_call | solution.py:668
  229.8 7.7 %attention_gradients.2 = (bf16[8,2,48,384]{3,2,1,0:T(8,128)(2,1)S(1)}, bf16[8,2,48,384]{3,2,1,0:T(8,128)(2,1)}, bf16[8,2,48,384]{3,2,1,0:T(8,128)(2,1)S(1)}, bf16[8,2,48,384]{3,2,1,0:T(8,128)(2,1)S(1)}) custom-call(s32[3]{0:T(128)S(1)} %pad_add_fusion.scal, bf16[1024,768]{1,0:T(8,128)(2,1)S(1)} %copy-done.14, bf16[1024,768]{1,0:T(8,128)(2,1)S(1)} %copy-done.14, ...), custom_call_target="tpu_custom_call" | custom-call | flops 3000000000 | bytes 10000000 | tf_op jit(solution)/shard_map/attention_gradients/pallas_call | solution.py:668
  244.6 5.6 %up_gradient.3 = (bf16[8,4,48,384]{3,2,1,0:T(8,128)(2,1)S(1)}, bf16[8,4,48,384]{3,2,1,0:T(8,128)(2,1)S(1)}) custom-call(s32[3]{0:T(128)S(1)} %pad_add_fusion.scal, bf16[512,768]{1,0:T(8,128)(2,1)S(1)} %copy-done.35, bf16[512,768]{1,0:T(8,128)(2,1)S(1)} %copy-done.45, bf16[512,1536]{1,0:T(8,128)(2,1)S(1)} %copy-done.16, bf16[512,1536]{1,0:T(8,128)(2,1)S(1)} %copy-done.23), custom_call_target="tpu_custom_call" | custom-call | flops 3000000000 | bytes 10000000 | tf_op jit(solution)/shard_map/up_gradient/pallas_call | solution.py:625
  253.0 7.0 %up_gradient.2 = (bf16[8,4,48,384]{3,2,1,0:T(8,128)(2,1)S(1)}, bf16[8,4,48,384]{3,2,1,0:T(8,128)(2,1)S(1)}) custom-call(s32[3]{0:T(128)S(1)} %pad_add_fusion.scal, bf16[512,768]{1,0:T(8,128)(2,1)S(1)} %copy-done.32, bf16[512,768]{1,0:T(8,128)(2,1)} %collective-permute-done.35.a_rcv, bf16[512,1536]{1,0:T(8,128)(2,1)S(1)} %copy-done.18, ...), custom_call_target="tpu_custom_call" | custom-call | flops 3000000000 | bytes 10000000 | tf_op jit(solution)/shard_map/up_gradient/pallas_call | solution.py:625
  269.5 11.0 %collective-permute-done.15 = bf16[8,2,48,384]{3,2,1,0:T(8,128)(2,1)S(1)} collective-permute-done((bf16[8,2,48,384]{3,2,1,0:T(8,128)(2,1)S(1)}, bf16[8,2,48,384]{3,2,1,0:T(8,128)(2,1)S(1)}, u32[]{:S(2)}, u32[]{:S(2)}) %collective-permute-start.15) | collective-permute-done | bytes 589856 | tf_op jit(solution)/shard_map/ppermute | solution.py:696
  282.1 29.4 %collective-permute-done.23 = bf16[2,2,2,48,384]{4,3,2,1,0:T(8,128)(2,1)S(1)} collective-permute-done((bf16[2,2,2,48,384]{4,3,2,1,0:T(8,128)(2,1)S(1)}, bf16[2,2,2,48,384]{4,3,2,1,0:T(8,128)(2,1)S(1)}, u32[]{:S(2)}, u32[]{:S(2)}) %collective-permute-start.23) | collective-permute-done | bytes 294944 | tf_op jit(solution)/shard_map/ppermute | solution.py:696
  314.7 5.2 %collective-permute-done.14 = bf16[2,2,2,48,384]{4,3,2,1,0:T(8,128)(2,1)S(1)} collective-permute-done((bf16[2,2,2,48,384]{4,3,2,1,0:T(8,128)(2,1)S(1)}, bf16[2,2,2,48,384]{4,3,2,1,0:T(8,128)(2,1)S(1)}, u32[]{:S(2)}, u32[]{:S(2)}) %collective-permute-start.14) | collective-permute-done | bytes 294944 | tf_op jit(solution)/shard_map/ppermute | solution.py:696
  323.3 5.4 %collective-permute-done.26 = bf16[8,48,384]{2,1,0:T(8,128)(2,1)S(1)} collective-permute-done((bf16[8,48,384]{2,1,0:T(8,128)(2,1)S(1)}, bf16[8,48,384]{2,1,0:T(8,128)(2,1)S(1)}, u32[]{:S(2)}, u32[]{:S(2)}) %collective-permute-start.26) | collective-permute-done | bytes 294944 | tf_op jit(solution)/shard_map/ppermute | solution.py:696
  331.5 3.9 collective-permute-done.17
  335.4 4.1 collective-permute-start.27
  340.6 6.3 %collective-permute-done.27 = bf16[4,48,384]{2,1,0:T(8,128)(2,1)S(1)} collective-permute-done((bf16[4,48,384]{2,1,0:T(8,128)(2,1)S(1)}, bf16[4,48,384]{2,1,0:T(8,128)(2,1)S(1)}, u32[]{:S(2)}, u32[]{:S(2)}) %collective-permute-start.27) | collective-permute-done | bytes 147488 | tf_op jit(solution)/shard_map/ppermute | solution.py:696
  348.5 6.1 %collective-permute-done.18 = bf16[4,48,384]{2,1,0:T(8,128)(2,1)S(1)} collective-permute-done((bf16[4,48,384]{2,1,0:T(8,128)(2,1)S(1)}, bf16[4,48,384]{2,1,0:T(8,128)(2,1)S(1)}, u32[]{:S(2)}, u32[]{:S(2)}) %collective-permute-start.18) | collective-permute-done | bytes 147488 | tf_op jit(solution)/shard_map/ppermute | solution.py:696
  361.2 6.3 %down_gradient.3 = (bf16[8,4,48,384]{3,2,1,0:T(8,128)(2,1)S(1)}, bf16[8,4,48,384]{3,2,1,0:T(8,128)(2,1)S(1)}) custom-call(s32[3]{0:T(128)S(1)} %pad_add_fusion.scal, bf16[512,3072]{1,0:T(8,128)(2,1)S(1)} %copy-done.12, bf16[512,3072]{1,0:T(8,128)(2,1)S(1)} %collective-permute-done.49.g_rcv, bf16[512,384]{1,0:T(8,128)(2,1)S(1)} %copy-done.49, ...), custom_call_target="tpu_custom_call" | custom-call | flops 3000000000 | bytes 10000000 | tf_op jit(solution)/shard_map/down_gradient/pallas_call | solution.py:594
  369.1 8.3 %down_gradient.2 = (bf16[8,4,48,384]{3,2,1,0:T(8,128)(2,1)S(1)}, bf16[8,4,48,384]{3,2,1,0:T(8,128)(2,1)S(1)}) custom-call(s32[3]{0:T(128)S(1)} %pad_add_fusion.scal, bf16[512,3072]{1,0:T(8,128)(2,1)S(1)} %copy-done.10, bf16[512,3072]{1,0:T(8,128)(2,1)} %collective-permute-done.39.g_rcv, bf16[512,384]{1,0:T(8,128)(2,1)S(1)} %copy-done.51, ...), custom_call_target="tpu_custom_call" | custom-call | flops 3000000000 | bytes 10000000 | tf_op jit(solution)/shard_map/down_gradient/pallas_call | solution.py:594
  381.3 7.0 %collective-permute-done.38 = bf16[2,2,4,48,384]{4,3,2,1,0:T(8,128)(2,1)} collective-permute-done((bf16[2,2,4,48,384]{4,3,2,1,0:T(8,128)(2,1)}, bf16[2,2,4,48,384]{4,3,2,1,0:T(8,128)(2,1)}, u32[]{:S(2)}, u32[]{:S(2)}) %collective-permute-start.38) | collective-permute-done | bytes 589856 | tf_op jit(solution)/shard_map/ppermute | solution.py:696
  389.4 24.1 %collective-permute-done.51 = bf16[8,4,48,384]{3,2,1,0:T(8,128)(2,1)S(1)} collective-permute-done((bf16[8,4,48,384]{3,2,1,0:T(8,128)(2,1)S(1)}, bf16[8,4,48,384]{3,2,1,0:T(8,128)(2,1)S(1)}, u32[]{:S(2)}, u32[]{:S(2)}) %collective-permute-start.51) | collective-permute-done | bytes 1179680 | tf_op jit(solution)/shard_map/ppermute | solution.py:696
  414.3 23.8 %collective-permute-done.41 = bf16[8,4,48,384]{3,2,1,0:T(8,128)(2,1)S(1)} collective-permute-done((bf16[8,4,48,384]{3,2,1,0:T(8,128)(2,1)S(1)}, bf16[8,4,48,384]{3,2,1,0:T(8,128)(2,1)S(1)}, u32[]{:S(2)}, u32[]{:S(2)}) %collective-permute-start.41) | collective-permute-done | bytes 1179680 | tf_op jit(solution)/shard_map/ppermute | solution.py:696
  439.3 13.8 %collective-permute-done.42 = bf16[2,2,4,48,384]{4,3,2,1,0:T(8,128)(2,1)S(1)} collective-permute-done((bf16[2,2,4,48,384]{4,3,2,1,0:T(8,128)(2,1)S(1)}, bf16[2,2,4,48,384]{4,3,2,1,0:T(8,128)(2,1)S(1)}, u32[]{:S(2)}, u32[]{:S(2)}) %collective-permute-start.42) | collective-permute-done | bytes 589856 | tf_op jit(solution)/shard_map/ppermute | solution.py:696
  456.8 16.6 %collective-permute-done.43 = bf16[16,48,384]{2,1,0:T(8,128)(2,1)S(1)} collective-permute-done((bf16[16,48,384]{2,1,0:T(8,128)(2,1)S(1)}, bf16[16,48,384]{2,1,0:T(8,128)(2,1)S(1)}, u32[]{:S(2)}, u32[]{:S(2)}) %collective-permute-start.43) | collective-permute-done | bytes 589856 | tf_op jit(solution)/shard_map/ppermute | solution.py:696
  476.7 11.1 %collective-permute-done.44 = bf16[8,48,384]{2,1,0:T(8,128)(2,1)S(1)} collective-permute-done((bf16[8,48,384]{2,1,0:T(8,128)(2,1)S(1)}, bf16[8,48,384]{2,1,0:T(8,128)(2,1)S(1)}, u32[]{:S(2)}, u32[]{:S(2)}) %collective-permute-start.44) | collective-permute-done | bytes 294944 | tf_op jit(solution)/shard_map/ppermute | solution.py:696
  (384 shorter events, 131.1 us)
Async XLA Ops:
  0.7 41.8 %collective-permute-start.3 = (bf16[768,3072]{1,0:T(8,128)(2,1)}, bf16[768,3072]{1,0:T(8,128)(2,1)}, u32[]{:S(2)}, u32[]{:S(2)}) collective-permute-start(bf16[768,3072]{1,0:T(8,128)(2,1)} %bitcast.348), channel_id=1, source_target_pairs={{0,16},{16,0},{1,17},{17,1},{2,18},{18,2},{3,19},{19,3},{4,20},{20... | collective-permute-start | bytes 14155784 | tf_op jit(solution)/shard_map/ppermute | solution.py:692
  1.2 41.3 %collective-permute-start.4 = (bf16[3072,768]{1,0:T(8,128)(2,1)}, bf16[3072,768]{1,0:T(8,128)(2,1)}, u32[]{:S(2)}, u32[]{:S(2)}) collective-permute-start(bf16[3072,768]{1,0:T(8,128)(2,1)} %bitcast.353), channel_id=1, source_target_pairs={{0,16},{16,0},{1,17},{17,1},{2,18},{18,2},{3,19},{19,3},{4,20},{20... | collective-permute-start | bytes 14155784 | tf_op jit(solution)/shard_map/ppermute | solution.py:692
  1.3 21.4 %collective-permute-start.1 = (bf16[768,2304]{1,0:T(8,128)(2,1)}, bf16[768,2304]{1,0:T(8,128)(2,1)}, u32[]{:S(2)}, u32[]{:S(2)}) collective-permute-start(bf16[768,2304]{1,0:T(8,128)(2,1)} %bitcast.338), channel_id=1, source_target_pairs={{0,16},{16,0},{1,17},{17,1},{2,18},{18,2},{3,19},{19,3},{4,20},{20... | collective-permute-start | bytes 10616840 | tf_op jit(solution)/shard_map/ppermute | solution.py:692
  1.7 20.9 %collective-permute-start.2 = (bf16[768,768]{1,0:T(8,128)(2,1)}, bf16[768,768]{1,0:T(8,128)(2,1)}, u32[]{:S(2)}, u32[]{:S(2)}) collective-permute-start(bf16[768,768]{1,0:T(8,128)(2,1)} %bitcast.343), channel_id=1, source_target_pairs={{0,16},{16,0},{1,17},{17,1},{2,18},{18,2},{3,19},{19,3},{4,20},{20... | collective-permute-start | bytes 3538952 | tf_op jit(solution)/shard_map/ppermute | solution.py:692
  184.6 22.6 %collective-permute-start.10 = (bf16[512,768]{1,0:T(8,128)(2,1)}, bf16[512,768]{1,0:T(8,128)(2,1)}, u32[]{:S(2)}, u32[]{:S(2)}) collective-permute-start(bf16[512,768]{1,0:T(8,128)(2,1)} %copy-done.36), channel_id=1, source_target_pairs={{0,16},{16,0},{1,17},{17,1},{2,18},{18,2},{3,19},{19,3},{4,20},{20... | collective-permute-start | bytes 2359304 | tf_op jit(solution)/shard_map/ppermute | solution.py:692
  184.6 27.3 %collective-permute-start.19 = (bf16[512,768]{1,0:T(8,128)(2,1)}, bf16[512,768]{1,0:T(8,128)(2,1)}, u32[]{:S(2)}, u32[]{:S(2)}) collective-permute-start(bf16[512,768]{1,0:T(8,128)(2,1)} %copy-done.38), channel_id=1, source_target_pairs={{0,16},{16,0},{1,17},{17,1},{2,18},{18,2},{3,19},{19,3},{4,20},{20... | collective-permute-start | bytes 2359304 | tf_op jit(solution)/shard_map/ppermute | solution.py:692
  185.1 26.9 %collective-permute-start.8 = (bf16[512,768]{1,0:T(8,128)(2,1)S(1)}, bf16[512,768]{1,0:T(8,128)(2,1)}, u32[]{:S(2)}, u32[]{:S(2)}) collective-permute-start(bf16[512,768]{1,0:T(8,128)(2,1)S(1)} %get-tuple-element.96.cot_ref), channel_id=1, source_target_pairs={{0,16},{16,0},{1,17},{17,1},{2,18},{18,2},{3,19},{19,3},{4,20},{20... | collective-permute-start | bytes 2359304 | tf_op jit(solution)/shard_map/ppermute | solution.py:692
  185.1 24.0 %collective-permute-start.21 = (bf16[512,384]{1,0:T(8,128)(2,1)}, bf16[512,384]{1,0:T(8,128)(2,1)}, u32[]{:S(2)}, u32[]{:S(2)}) collective-permute-start(bf16[512,384]{1,0:T(8,128)(2,1)} %copy-done.56), channel_id=1, source_target_pairs={{0,16},{16,0},{1,17},{17,1},{2,18},{18,2},{3,19},{19,3},{4,20},{20... | collective-permute-start | bytes 1179656 | tf_op jit(solution)/shard_map/ppermute | solution.py:692
  211.9 27.3 %collective-permute-start.46 = (bf16[512,1536]{1,0:T(8,128)(2,1)}, bf16[512,1536]{1,0:T(8,128)(2,1)S(1)}, u32[]{:S(2)}, u32[]{:S(2)}) collective-permute-start(bf16[512,1536]{1,0:T(8,128)(2,1)} %copy-done.19), channel_id=1, source_target_pairs={{0,16},{16,0},{1,17},{17,1},{2,18},{18,2},{3,19},{19,3},{4,20},{20... | collective-permute-start | bytes 4718600 | tf_op jit(solution)/shard_map/ppermute | solution.py:692
  213.4 38.1 %collective-permute-start.36 = (bf16[512,1536]{1,0:T(8,128)(2,1)S(1)}, bf16[512,1536]{1,0:T(8,128)(2,1)}, u32[]{:S(2)}, u32[]{:S(2)}) collective-permute-start(bf16[512,1536]{1,0:T(8,128)(2,1)S(1)} %copy-done.21), channel_id=1, source_target_pairs={{0,16},{16,0},{1,17},{17,1},{2,18},{18,2},{3,19},{19,3},{4,20},{20... | collective-permute-start | bytes 4718600 | tf_op jit(solution)/shard_map/ppermute | solution.py:692
  218.0 20.3 %collective-permute-start.45 = (bf16[512,768]{1,0:T(8,128)(2,1)S(1)}, bf16[512,768]{1,0:T(8,128)(2,1)S(1)}, u32[]{:S(2)}, u32[]{:S(2)}) collective-permute-start(bf16[512,768]{1,0:T(8,128)(2,1)S(1)} %copy-done.34), channel_id=1, source_target_pairs={{0,16},{16,0},{1,17},{17,1},{2,18},{18,2},{3,19},{19,3},{4,20},{20... | collective-permute-start | bytes 2359304 | tf_op jit(solution)/shard_map/ppermute | solution.py:692
  219.7 31.6 %collective-permute-start.35 = (bf16[512,768]{1,0:T(8,128)(2,1)S(1)}, bf16[512,768]{1,0:T(8,128)(2,1)}, u32[]{:S(2)}, u32[]{:S(2)}) collective-permute-start(bf16[512,768]{1,0:T(8,128)(2,1)S(1)} %copy-done.32), channel_id=1, source_target_pairs={{0,16},{16,0},{1,17},{17,1},{2,18},{18,2},{3,19},{19,3},{4,20},{20... | collective-permute-start | bytes 2359304 | tf_op jit(solution)/shard_map/ppermute | solution.py:692
  228.3 31.8 %collective-permute-start.22 = (bf16[8,2,48,384]{3,2,1,0:T(8,128)(2,1)}, bf16[8,2,48,384]{3,2,1,0:T(8,128)(2,1)}, u32[]{:S(2)}, u32[]{:S(2)}) collective-permute-start(bf16[8,2,48,384]{3,2,1,0:T(8,128)(2,1)} %get-tuple-element.119), channel_id=1, source_target_pairs={{0,1},{1,0},{2,3},{3,2},{4,5},{5,4},{6,7},{7,6},{8,9},{9,8},{10,11... | collective-permute-start | bytes 1769480 | tf_op jit(solution)/shard_map/ppermute | solution.py:696
  239.2 121.5 %collective-permute-start.49 = (bf16[512,3072]{1,0:T(8,128)(2,1)S(1)}, bf16[512,3072]{1,0:T(8,128)(2,1)S(1)}, u32[]{:S(2)}, u32[]{:S(2)}) collective-permute-start(bf16[512,3072]{1,0:T(8,128)(2,1)S(1)} %copy-done.12), channel_id=1, source_target_pairs={{0,16},{16,0},{1,17},{17,1},{2,18},{18,2},{3,19},{19,3},{4,20},{20... | collective-permute-start | bytes 9437192 | tf_op jit(solution)/shard_map/ppermute | solution.py:692
  240.4 22.3 %collective-permute-start.13 = (bf16[8,2,48,384]{3,2,1,0:T(8,128)(2,1)}, bf16[8,2,48,384]{3,2,1,0:T(8,128)(2,1)}, u32[]{:S(2)}, u32[]{:S(2)}) collective-permute-start(bf16[8,2,48,384]{3,2,1,0:T(8,128)(2,1)} %get-tuple-element.112), channel_id=1, source_target_pairs={{0,1},{1,0},{2,3},{3,2},{4,5},{5,4},{6,7},{7,6},{8,9},{9,8},{10,11... | collective-permute-start | bytes 1769480 | tf_op jit(solution)/shard_map/ppermute | solution.py:696
  251.3 117.8 %collective-permute-start.39 = (bf16[512,3072]{1,0:T(8,128)(2,1)S(1)}, bf16[512,3072]{1,0:T(8,128)(2,1)}, u32[]{:S(2)}, u32[]{:S(2)}) collective-permute-start(bf16[512,3072]{1,0:T(8,128)(2,1)S(1)} %copy-done.10), channel_id=1, source_target_pairs={{0,16},{16,0},{1,17},{17,1},{2,18},{18,2},{3,19},{19,3},{4,20},{20... | collective-permute-start | bytes 9437192 | tf_op jit(solution)/shard_map/ppermute | solution.py:692
  251.5 16.4 %collective-permute-start.24 = (bf16[8,2,48,384]{3,2,1,0:T(8,128)(2,1)}, bf16[8,2,48,384]{3,2,1,0:T(8,128)(2,1)S(1)}, u32[]{:S(2)}, u32[]{:S(2)}) collective-permute-start(bf16[8,2,48,384]{3,2,1,0:T(8,128)(2,1)} %get-tuple-element.121), channel_id=1, source_target_pairs={{0,2},{1,3},{2,0},{3,1},{4,6},{5,7},{6,4},{7,5},{8,10},{9,11},{10,... | collective-permute-start | bytes 1769480 | tf_op jit(solution)/shard_map/ppermute | solution.py:696
  260.1 20.4 %collective-permute-start.15 = (bf16[8,2,48,384]{3,2,1,0:T(8,128)(2,1)S(1)}, bf16[8,2,48,384]{3,2,1,0:T(8,128)(2,1)S(1)}, u32[]{:S(2)}, u32[]{:S(2)}) collective-permute-start(bf16[8,2,48,384]{3,2,1,0:T(8,128)(2,1)S(1)} %copy-done.47), channel_id=1, source_target_pairs={{0,2},{1,3},{2,0},{3,1},{4,6},{5,7},{6,4},{7,5},{8,10},{9,11},{10,... | collective-permute-start | bytes 1769480 | tf_op jit(solution)/shard_map/ppermute | solution.py:696
  262.7 93.7 %collective-permute-start.47 = (bf16[8,4,48,384]{3,2,1,0:T(8,128)(2,1)S(1)}, bf16[8,4,48,384]{3,2,1,0:T(8,128)(2,1)S(1)}, u32[]{:S(2)}, u32[]{:S(2)}) collective-permute-start(bf16[8,4,48,384]{3,2,1,0:T(8,128)(2,1)S(1)} %copy-done.30), channel_id=1, source_target_pairs={{0,2},{1,3},{2,0},{3,1},{4,6},{5,7},{6,4},{7,5},{8,10},{9,11},{10,... | collective-permute-start | bytes 3538952 | tf_op jit(solution)/shard_map/ppermute | solution.py:696
  267.9 43.6 %collective-permute-start.23 = (bf16[2,2,2,48,384]{4,3,2,1,0:T(8,128)(2,1)S(1)}, bf16[2,2,2,48,384]{4,3,2,1,0:T(8,128)(2,1)S(1)}, u32[]{:S(2)}, u32[]{:S(2)}) collective-permute-start(bf16[2,2,2,48,384]{4,3,2,1,0:T(8,128)(2,1)S(1)} %fusion.10), channel_id=1, source_target_pairs={{0,2},{1,3},{2,0},{3,1},{4,6},{5,7},{6,4},{7,5},{8,10},{9,11},{10,... | collective-permute-start | bytes 884744 | tf_op jit(solution)/shard_map/ppermute | solution.py:696
  280.5 32.6 %collective-permute-start.25 = (bf16[2,2,2,48,384]{4,3,2,1,0:T(8,128)(2,1)S(1)}, bf16[2,2,2,48,384]{4,3,2,1,0:T(8,128)(2,1)S(1)}, u32[]{:S(2)}, u32[]{:S(2)}) collective-permute-start(bf16[2,2,2,48,384]{4,3,2,1,0:T(8,128)(2,1)S(1)} %fusion.11), channel_id=1, source_target_pairs={{0,1},{1,0},{2,3},{3,2},{4,5},{5,4},{6,7},{7,6},{8,9},{9,8},{10,11... | collective-permute-start | bytes 884744 | tf_op jit(solution)/shard_map/ppermute | solution.py:696
  319.8 38.1 %collective-permute-start.37 = (bf16[8,4,48,384]{3,2,1,0:T(8,128)(2,1)S(1)}, bf16[8,4,48,384]{3,2,1,0:T(8,128)(2,1)S(1)}, u32[]{:S(2)}, u32[]{:S(2)}) collective-permute-start(bf16[8,4,48,384]{3,2,1,0:T(8,128)(2,1)S(1)} %get-tuple-element.127), channel_id=1, source_target_pairs={{0,2},{1,3},{2,0},{3,1},{4,6},{5,7},{6,4},{7,5},{8,10},{9,11},{10,... | collective-permute-start | bytes 3538952 | tf_op jit(solution)/shard_map/ppermute | solution.py:696
  358.0 117.7 %collective-permute-start.28 = (f32[2,48,384]{2,1,0:T(8,128)}, f32[2,48,384]{2,1,0:T(8,128)}, u32[]{:S(2)}, u32[]{:S(2)}) collective-permute-start(f32[2,48,384]{2,1,0:T(8,128)} %get-tuple-element.180), channel_id=1, source_target_pairs={{0,16},{16,0},{1,17},{17,1},{2,18},{18,2},{3,19},{19,3},{4,20},{20... | collective-permute-start | bytes 442376 | tf_op jit(solution)/shard_map/ppermute | solution.py:692
  359.2 21.9 %collective-permute-start.48 = (bf16[2,2,4,48,384]{4,3,2,1,0:T(8,128)(2,1)}, bf16[2,2,4,48,384]{4,3,2,1,0:T(8,128)(2,1)S(1)}, u32[]{:S(2)}, u32[]{:S(2)}) collective-permute-start(bf16[2,2,4,48,384]{4,3,2,1,0:T(8,128)(2,1)} %fusion.2), channel_id=1, source_target_pairs={{0,1},{1,0},{2,3},{3,2},{4,5},{5,4},{6,7},{7,6},{8,9},{9,8},{10,11... | collective-permute-start | bytes 1769480 | tf_op jit(solution)/shard_map/ppermute | solution.py:696
  360.7 27.6 %collective-permute-start.38 = (bf16[2,2,4,48,384]{4,3,2,1,0:T(8,128)(2,1)}, bf16[2,2,4,48,384]{4,3,2,1,0:T(8,128)(2,1)}, u32[]{:S(2)}, u32[]{:S(2)}) collective-permute-start(bf16[2,2,4,48,384]{4,3,2,1,0:T(8,128)(2,1)} %fusion), channel_id=1, source_target_pairs={{0,1},{1,0},{2,3},{3,2},{4,5},{5,4},{6,7},{7,6},{8,9},{9,8},{10,11... | collective-permute-start | bytes 1769480 | tf_op jit(solution)/shard_map/ppermute | solution.py:696
  367.5 45.9 %collective-permute-start.51 = (bf16[8,4,48,384]{3,2,1,0:T(8,128)(2,1)S(1)}, bf16[8,4,48,384]{3,2,1,0:T(8,128)(2,1)S(1)}, u32[]{:S(2)}, u32[]{:S(2)}) collective-permute-start(bf16[8,4,48,384]{3,2,1,0:T(8,128)(2,1)S(1)} %get-tuple-element.141), channel_id=1, source_target_pairs={{0,1},{1,0},{2,3},{3,2},{4,5},{5,4},{6,7},{7,6},{8,9},{9,8},{10,11... | collective-permute-start | bytes 3538952 | tf_op jit(solution)/shard_map/ppermute | solution.py:696
  377.4 60.8 %collective-permute-start.41 = (bf16[8,4,48,384]{3,2,1,0:T(8,128)(2,1)S(1)}, bf16[8,4,48,384]{3,2,1,0:T(8,128)(2,1)S(1)}, u32[]{:S(2)}, u32[]{:S(2)}) collective-permute-start(bf16[8,4,48,384]{3,2,1,0:T(8,128)(2,1)S(1)} %get-tuple-element.132), channel_id=1, source_target_pairs={{0,1},{1,0},{2,3},{3,2},{4,5},{5,4},{6,7},{7,6},{8,9},{9,8},{10,11... | collective-permute-start | bytes 3538952 | tf_op jit(solution)/shard_map/ppermute | solution.py:696
  381.2 72.2 %collective-permute-start.29 = (f32[2,48,384]{2,1,0:T(8,128)S(1)}, f32[2,48,384]{2,1,0:T(8,128)S(1)}, u32[]{:S(2)}, u32[]{:S(2)}) collective-permute-start(f32[2,48,384]{2,1,0:T(8,128)S(1)} %get-tuple-element.183), channel_id=1, source_target_pairs={{0,16},{16,0},{1,17},{17,1},{2,18},{18,2},{3,19},{19,3},{4,20},{20... | collective-permute-start | bytes 442376 | tf_op jit(solution)/shard_map/ppermute | solution.py:692
  413.6 25.4 %collective-permute-start.52 = (bf16[2,2,4,48,384]{4,3,2,1,0:T(8,128)(2,1)S(1)}, bf16[2,2,4,48,384]{4,3,2,1,0:T(8,128)(2,1)S(1)}, u32[]{:S(2)}, u32[]{:S(2)}) collective-permute-start(bf16[2,2,4,48,384]{4,3,2,1,0:T(8,128)(2,1)S(1)} %fusion.3), channel_id=1, source_target_pairs={{0,2},{1,3},{2,0},{3,1},{4,6},{5,7},{6,4},{7,5},{8,10},{9,11},{10,... | collective-permute-start | bytes 1769480 | tf_op jit(solution)/shard_map/ppermute | solution.py:696
  438.3 14.8 %collective-permute-start.42 = (bf16[2,2,4,48,384]{4,3,2,1,0:T(8,128)(2,1)S(1)}, bf16[2,2,4,48,384]{4,3,2,1,0:T(8,128)(2,1)S(1)}, u32[]{:S(2)}, u32[]{:S(2)}) collective-permute-start(bf16[2,2,4,48,384]{4,3,2,1,0:T(8,128)(2,1)S(1)} %fusion.1), channel_id=1, source_target_pairs={{0,2},{1,3},{2,0},{3,1},{4,6},{5,7},{6,4},{7,5},{8,10},{9,11},{10,... | collective-permute-start | bytes 1769480 | tf_op jit(solution)/shard_map/ppermute | solution.py:696
  453.3 20.2 %collective-permute-start.43 = (bf16[16,48,384]{2,1,0:T(8,128)(2,1)S(1)}, bf16[16,48,384]{2,1,0:T(8,128)(2,1)S(1)}, u32[]{:S(2)}, u32[]{:S(2)}) collective-permute-start(bf16[16,48,384]{2,1,0:T(8,128)(2,1)S(1)} %pad_maximum_fusion), channel_id=1, source_target_pairs={{0,4},{1,5},{2,6},{3,7},{4,0},{5,1},{6,2},{7,3},{8,12},{9,13},{10,... | collective-permute-start | bytes 1769480 | tf_op jit(solution)/shard_map/ppermute | solution.py:696
  455.1 21.6 %collective-permute-start.54 = (bf16[8,48,384]{2,1,0:T(8,128)(2,1)S(1)}, bf16[8,48,384]{2,1,0:T(8,128)(2,1)S(1)}, u32[]{:S(2)}, u32[]{:S(2)}) collective-permute-start(bf16[8,48,384]{2,1,0:T(8,128)(2,1)S(1)} %pad_maximum_fusion.5), channel_id=1, source_target_pairs={{0,8},{1,9},{2,10},{3,11},{4,12},{5,13},{6,14},{7,15},{8,0},{9,1},... | collective-permute-start | bytes 884744 | tf_op jit(solution)/shard_map/ppermute | solution.py:696
  (112 other events, 1116.8 us)

commit v2 on v0

v2 whole, which is shorter than its diff:
```python
import functools

import jax
import jax.numpy as jnp
from jax import lax
from jax.experimental import pallas as pl
from jax.experimental.pallas import tpu as pltpu
from jax.sharding import PartitionSpec as P

HEADS = 12
HEAD_DIM = 64
MB_TOK = 512
SCALE = 0.125
EPS = 1e-06
D = 768
FF = 3072
HALF = D // 2
PAIR = 2 * HEAD_DIM
PAIRS = D // PAIR
ROWS = 256
CHUNK = 768
CHUNKS = FF // CHUNK
BF = jnp.bfloat16
F32 = jnp.float32
MIB = 1 << 20
T = MB_TOK
BLOCKS = [slice(top, top + ROWS) for top in range(0, T, ROWS)]

QB, VB, OB, G1, S1, DB, G2, S2, UB, HD = 0, 1, 2, 3, 4, 5, 6, 7, 8, 12
PARAMS = 12
GRADS = 13
SEND = 1024
MORE = FF // 2 + HALF - SEND
QKV_SEND = 640
QKV_MORE = 3 * HALF - QKV_SEND

ANY = pl.BlockSpec(memory_space=pl.ANY)
VMEM = pl.BlockSpec(memory_space=pltpu.VMEM)
SMEM = pl.BlockSpec(memory_space=pltpu.SMEM)
DMA = pltpu.SemaphoreType.DMA


def at(place):
    return (slice(0, 1), slice(place * D, (place + 1) * D))


def as_column(row):
    return jnp.broadcast_to(row, (128, row.shape[1])).T[:, :1]


def as_row(column):
    return jnp.broadcast_to(column, (column.shape[0], 128)).T[:1, :]


def dot(left, right, left_dim, right_dim):
    return lax.dot_general(
        left, right, (((left_dim,), (right_dim,)), ((), ())), preferred_element_type=F32
    )


def row_mean(values):
    return jnp.mean(values, axis=-1, keepdims=True)


def col_sum(values):
    return jnp.sum(values, axis=0, keepdims=True)


def head_masks():
    lane = lax.broadcasted_iota(jnp.int32, (1, PAIR), 1)
    first = jnp.where(lane < HEAD_DIM, 1.0, 0.0)
    return (first, 1.0 - first)


def lanes(start, width):
    return pl.ds(pl.multiple_of(start, 128), width)


class Copies:
    def __init__(self, sems):
        self.sems = sems
        self.used = 0
        self.open = []

    def sem(self):
        self.used += 1
        return self.sems.at[self.used - 1]

    def load(self, source, target):
        copy = pltpu.make_async_copy(source, target, self.sem())
        copy.start()
        return copy

    def store(self, source, target):
        self.open.append(self.load(source, target))

    def pick(self, is_own, own, received, target):
        sem = self.sem()
        mine = pltpu.make_async_copy(own, target, sem)

        @pl.when(is_own)
        def _():
            mine.start()

        @pl.when(jnp.logical_not(is_own))
        def _():
            pltpu.make_async_copy(received, target, sem).start()

        return mine

    def finish(self):
        for copy in self.open:
            copy.wait()


def kernel_call(body, name, specs, args, outs, scratch, copies, us, grant=60):
    def wrapped(*refs):
        body(Copies(refs[-1]), *refs[:-1])

    return pl.pallas_call(
        wrapped,
        in_specs=specs,
        out_specs=[spec for _, _, spec in outs],
        out_shape=[jax.ShapeDtypeStruct(shape, kind) for shape, kind, _ in outs],
        scratch_shapes=list(scratch) + [DMA((copies,))],
        compiler_params=pltpu.CompilerParams(vmem_limit_bytes=grant * MIB),
        cost_estimate=pl.CostEstimate(flops=us * 10**9 + 1000, bytes_accessed=us * 2 * 10**6 + 1000, transcendentals=0),
        name=name,
    )(*args)


def pack_vectors(vectors):
    width = sum(vector.shape[1] for vector in vectors)

    def body(copies, *refs):
        out = refs[-1]
        start = 0
        for ref in refs[:-1]:
            out[0:1, start : start + ref.shape[1]] = ref[...]
            start += ref.shape[1]

    return kernel_call(body, "pack_vectors", [VMEM] * len(vectors), vectors, [((1, width), F32, VMEM)], [], 1, 1)[0]


def project(x_ref, weight, weight_copies, vec, qkv):
    for part in range(3):
        weight_copies[part].wait()
        for tile in range(3):
            here = slice(part * D + tile * 256, part * D + (tile + 1) * 256)
            value = dot(x_ref[...], weight[:, here], 1, 0)
            if part != 1:
                place = (QB if part == 0 else VB) * D + tile * 256
                value = value + vec[0:1, place : place + 256]
            if part == 0:
                value = value * SCALE
            qkv[:, here] = value.astype(BF)


def attend(qkv, bias, a_slots, a_hbm, a_sems, o_ref):
    masks = head_masks()

    def pair(step, carry):
        slot = lax.rem(step, 2)
        out_copy = pltpu.make_async_copy(a_slots.at[slot], a_hbm.at[pl.ds(2 * step, 2)], a_sems.at[slot])

        @pl.when(step >= 2)
        def _():
            out_copy.wait()

        off = step * PAIR
        q = qkv[:, lanes(off, PAIR)]
        k = qkv[:, lanes(off + D, PAIR)]
        v = qkv[:, lanes(off + 2 * D, PAIR)]
        outs = [None] * len(BLOCKS)
        for head in range(2):
            mask = masks[head].astype(BF)
            kh = k * mask
            vh = v * mask
            for block, rows in enumerate(BLOCKS):
                s = dot(q[rows], kh, 1, 1) + bias[rows, :]
                p = jnp.exp(s - jnp.max(s, axis=-1, keepdims=True))
                a = (p * (1.0 / jnp.sum(p, axis=-1, keepdims=True))).astype(BF)
                a_slots[slot, head, rows, :] = a
                o = dot(a, vh, 1, 0)
                outs[block] = o if outs[block] is None else outs[block] + o
        for rows, out in zip(BLOCKS, outs):
            o_ref[rows, lanes(off, PAIR)] = out.astype(BF)
        out_copy.start()
        return carry

    lax.fori_loop(0, PAIRS, pair, 0)


def attend_end(a_slots, a_hbm, a_sems):
    for slot in range(2):
        pltpu.make_async_copy(a_slots.at[slot], a_hbm.at[pl.ds(0, 2)], a_sems.at[slot]).wait()


def norm_one(x_ref, o_ref, weight, vec, xh_ref, n1_ref):
    rstds = []
    for rows in BLOCKS:
        r1 = x_ref[rows, :].astype(F32) + dot(o_ref[rows, :], weight[...], 1, 0) + vec[at(OB)]
        center = r1 - row_mean(r1)
        rstd = lax.rsqrt(row_mean(center * center) + EPS)
        xh = center * rstd
        xh_ref[rows, :] = xh
        n1_ref[rows, :] = (xh * vec[at(G1)] + vec[at(S1)]).astype(BF)
        rstds.append(rstd)
    return as_row(jnp.concatenate(rstds, axis=0))


def erf_tail(magnitude, bell):
    t = 1.0 / (1.0 + (0.3275911 * 0.7071067811865476) * magnitude)
    poly = 0.5 * 1.061405429
    for factor in (-1.453152027, 1.421413741, -0.284496736, 0.254829592):
        poly = poly * t + 0.5 * factor
    return poly * t * bell


def gelu_and_slope(u):
    bell = jnp.exp(u * u * -0.5)
    tail = erf_tail(jnp.abs(u), bell)
    cdf = jnp.where(u < 0.0, tail, 1.0 - tail)
    value = u * cdf
    return value, cdf + u * bell * 0.3989422804014327


def mlp(n1_ref, wu, wu_copies, wd, wd_copies, vec, g_hbm, gp_hbm, g_slots, gp_slots, g_sems, acc):
    def chunk(step, carry):
        slot = lax.rem(step, 2)
        cols = lanes(step * CHUNK, CHUNK)
        out = pltpu.make_async_copy(g_slots.at[slot], g_hbm.at[:, cols], g_sems.at[slot])
        slope_out = pltpu.make_async_copy(gp_slots.at[slot], gp_hbm.at[:, cols], g_sems.at[2 + slot])

        @pl.when(step >= 2)
        def _():
            out.wait()
            slope_out.wait()

        wu_copies(step).wait()
        if wd is not None:
            wd_copies(step).wait()
        bias = vec[0:1, lanes(UB * D + step * CHUNK, CHUNK)]
        ups = [dot(n1_ref[rows, :], wu[step], 1, 0) + bias for rows in BLOCKS]
        for rows, up in zip(BLOCKS, ups):
            value, slope = gelu_and_slope(up)
            value = value.astype(BF)
            g_slots[slot, rows, :] = value
            gp_slots[slot, rows, :] = slope.astype(BF)
            if wd is not None:
                acc[rows, :] += dot(value, wd[step], 1, 0)
        out.start()
        slope_out.start()
        return carry

    lax.fori_loop(0, CHUNKS, chunk, 0)


def mlp_end(g_hbm, gp_hbm, g_slots, gp_slots, g_sems):
    for slot in range(2):
        pltpu.make_async_copy(g_slots.at[slot], g_hbm.at[:, :CHUNK], g_sems.at[slot]).wait()
        pltpu.make_async_copy(gp_slots.at[slot], gp_hbm.at[:, :CHUNK], g_sems.at[2 + slot]).wait()


def norm_two(rows, r2, vec):
    center = r2 - row_mean(r2)
    rstd = lax.rsqrt(row_mean(center * center) + EPS)
    xh = center * rstd
    return xh, rstd, xh * vec[at(G2)] + vec[at(S2)]


def norm_back(cot, xh, rstd, gain):
    scaled = cot * gain
    return rstd * (scaled - row_mean(scaled) - xh * row_mean(scaled * xh))


def norm_two_back(rows, cot, xh, rstd, vec, dr2_ref, dy_ref, vg_ref):
    vg_ref[at(G2)] += col_sum(cot * xh)
    vg_ref[at(S2)] += col_sum(cot)
    d_second = norm_back(cot, xh, rstd, vec[at(G2)])
    low = d_second.astype(BF)
    dr2_ref[rows, :] = d_second
    dy_ref[rows, :] = low
    vg_ref[at(DB)] += col_sum(low.astype(F32))


def mlp_back(dy_ref, gp, wu, wu_copies, wd, wd_copies, acc, du, vg_ref):
    def chunk(step, carry):
        cols = lanes(step * CHUNK, CHUNK)
        wd_copies(step).wait()
        wu_copies(step).wait()
        total = None
        for rows in BLOCKS:
            d_active = dot(dy_ref[rows, :], wd[step], 1, 1)
            d_up = (d_active * gp[rows, cols].astype(F32)).astype(BF)
            part = col_sum(d_up.astype(F32))
            total = part if total is None else total + part
            du[rows, cols] = d_up
            acc[rows, :] += dot(d_up, wu[step], 1, 1)
        vg_ref[0:1, lanes(UB * D + step * CHUNK, CHUNK)] = total
        return carry

    lax.fori_loop(0, CHUNKS, chunk, 0)


def norm_one_back(acc, xh_ref, rstd, vec, dr1_ref, db_ref, vg_ref):
    for rows in BLOCKS:
        cot = acc[rows, :]
        xh = xh_ref[rows, :]
        vg_ref[at(G1)] += col_sum(cot * xh)
        vg_ref[at(S1)] += col_sum(cot)
        d_first = norm_back(cot, xh, rstd[rows], vec[at(G1)])
        low = d_first.astype(BF)
        dr1_ref[rows, :] = d_first
        db_ref[rows, :] = low
        vg_ref[at(OB)] += col_sum(low.astype(F32))


def attend_back(qkv, a_hbm, a_slots, a_sems, o_ref, dmix, full, vg_ref):
    masks = head_masks()

    def fetch(step, slot):
        return pltpu.make_async_copy(a_hbm.at[pl.ds(2 * step, 2)], a_slots.at[slot], a_sems.at[slot])

    def pair(step, carry):
        slot = lax.rem(step, 2)
        off = step * PAIR
        q = qkv[:, lanes(off, PAIR)]
        k = qkv[:, lanes(off + D, PAIR)]
        v = qkv[:, lanes(off + 2 * D, PAIR)]
        do = dmix[:, lanes(off, PAIR)]
        product = do.astype(F32) * o_ref[:, lanes(off, PAIR)].astype(F32)
        fetch(step, slot).wait()
        d_q = [None] * len(BLOCKS)
        d_k = None
        d_v = None
        for head in range(2):
            mask = masks[head].astype(BF)
            kh = k * mask
            vh = v * mask
            qh = q * mask
            doh = do * mask
            inner = jnp.sum(product * masks[head], axis=-1, keepdims=True)
            for block, rows in enumerate(BLOCKS):
                a = a_slots[slot, head, rows, :]
                d_p = dot(do[rows], vh, 1, 1)
                d_s = (a.astype(F32) * (d_p - inner[rows])).astype(BF)
                more_v = dot(a, doh[rows], 0, 0)
                more_q = dot(d_s, kh, 1, 0)
                more_k = dot(d_s, qh[rows], 0, 0)
                d_v = more_v if d_v is None else d_v + more_v
                d_k = more_k if d_k is None else d_k + more_k
                d_q[block] = more_q if d_q[block] is None else d_q[block] + more_q
        d_q = jnp.concatenate(d_q, axis=0).astype(BF) * jnp.asarray(SCALE, BF)
        d_k = d_k.astype(BF)
        d_v = d_v.astype(BF)
        vg_ref[0:1, lanes(QB * D + off, PAIR)] = col_sum(d_q.astype(F32))
        vg_ref[0:1, lanes(VB * D + off, PAIR)] = col_sum(d_v.astype(F32))
        for part, value in enumerate((d_q, d_k, d_v)):
            full[:, lanes(part * D + off, PAIR)] = value

        @pl.when(step + 2 < PAIRS)
        def _():
            fetch(step + 2, slot).start()

        return carry

    lax.fori_loop(0, PAIRS, pair, 0)


def split_store(copies, section, source, keep, send, parts=1):
    width = source.shape[1] // parts
    half = width // 2
    for part in range(parts):
        target = slice(part * half, (part + 1) * half)
        copies.store(source.at[:, lanes(part * width + section * half, half)], keep.at[:, target])
        copies.store(source.at[:, lanes(part * width + (1 - section) * half, half)], send.at[:, target])


def first_attention(scal, tokens, ends, vec_own, vec_rcv, wq_own, wq_rcv, wo_own, wo_rcv):
    def body(
        copies, scal, x_hbm, ends_ref, vec_own, vec_rcv, wq_own, wq_rcv, wo_own, wo_rcv,
        qkv_hbm, a_hbm, xh_hbm, pack_hbm, rstd_ref,
        x, wq, wo, vec, bias, qkv, a_slots, o, xh, n1, a_sems,
    ):
        section = scal[0]
        is_own = section == 0
        x_copy = copies.load(x_hbm.at[pl.ds(pl.multiple_of(section * T, T), T)], x)
        wq_copies = [
            copies.pick(is_own, wq_own.at[:, cols], wq_rcv.at[:, cols], wq.at[:, cols])
            for cols in (slice(part * D, (part + 1) * D) for part in range(3))
        ]
        wo_copy = copies.pick(is_own, wo_own, wo_rcv, wo)
        vec[...] = jnp.where(is_own, vec_own[...], vec_rcv[...])
        make_bias(section, ends_ref, bias)
        x_copy.wait()
        project(x, wq, wq_copies, vec, qkv)
        copies.store(qkv, qkv_hbm)
        attend(qkv, bias, a_slots, a_hbm, a_sems, o)
        copies.store(o, pack_hbm.at[:, :D])
        wo_copy.wait()
        rstd_ref[...] = norm_one(x, o, wo, vec, xh, n1)
        copies.store(xh, xh_hbm)
        copies.store(n1, pack_hbm.at[:, D:])
        attend_end(a_slots, a_hbm, a_sems)
        copies.finish()

    return kernel_call(
        body, "first_attention", [SMEM, ANY, VMEM, VMEM, VMEM, ANY, ANY, ANY, ANY],
        (scal, tokens, ends, vec_own, vec_rcv, wq_own, wq_rcv, wo_own, wo_rcv),
        [
            ((T, 3 * D), BF, ANY), ((HEADS, T, T), BF, ANY), ((T, D), F32, ANY), ((T, 2 * D), BF, ANY),
            ((1, T), F32, VMEM),
        ],
        [
            pltpu.VMEM((T, D), BF), pltpu.VMEM((D, 3 * D), BF), pltpu.VMEM((D, D), BF),
            pltpu.VMEM((1, PARAMS * D), F32), pltpu.VMEM((T, T), F32), pltpu.VMEM((T, 3 * D), BF),
            pltpu.VMEM((2, 2, T, T), BF), pltpu.VMEM((T, D), BF), pltpu.VMEM((T, D), F32), pltpu.VMEM((T, D), BF),
            DMA((2,)),
        ],
        16, 15,
    )


def make_bias(section, ends_ref, bias):
    ends = ends_ref[0:1, lanes(section * T, T)].astype(F32)
    square = jnp.broadcast_to(ends, (T, T))
    bias[...] = jnp.where(square == square.T, 0.0, -1e30)


def pick_chunks(copies, is_own, own, received, target, by_rows):
    base = copies.used

    def cut(array, start):
        return array.at[pl.ds(start, CHUNK)] if by_rows else array.at[:, pl.ds(start, CHUNK)]

    for step in range(CHUNKS):
        copies.pick(is_own, cut(own, step * CHUNK), cut(received, step * CHUNK), target.at[step])

    def chunk_copy(step):
        return pltpu.make_async_copy(cut(own, 0), target.at[step], copies.sems.at[base + step])

    return chunk_copy


def pick_both(copies, is_own, wu_own, wu_rcv, wu, wd_own, wd_rcv, wd):
    base = copies.used
    for step in range(CHUNKS):
        cols = pl.ds(step * CHUNK, CHUNK)
        copies.pick(is_own, wu_own.at[:, cols], wu_rcv.at[:, cols], wu.at[step])
        copies.pick(is_own, wd_own.at[cols], wd_rcv.at[cols], wd.at[step])

    def wu_copy(step):
        return pltpu.make_async_copy(wu_own.at[:, pl.ds(0, CHUNK)], wu.at[step], copies.sems.at[base + 2 * step])

    def wd_copy(step):
        return pltpu.make_async_copy(wd_own.at[pl.ds(0, CHUNK)], wd.at[step], copies.sems.at[base + 2 * step + 1])

    return wu_copy, wd_copy


def middle(scal, pack, xh1, ends, vec_own, vec_rcv, wq_own, wq_rcv, wo_own, wo_rcv, wu_own, wu_rcv, wd_own, wd_rcv):
    def body(
        copies, scal, pack_hbm, xh1_hbm, ends_ref, vec_own, vec_rcv, wq_own, wq_rcv, wo_own, wo_rcv,
        wu_own, wu_rcv, wd_own, wd_rcv,
        out_hbm, gp_hbm, xh2_hbm, qkv_hbm, a_hbm, xh1b_hbm, gb_hbm, gpb_hbm, rstd2_ref, rstd1_ref,
        n1, xh, acc, wu, wd, wub, wq, wo, vec, vecb, bias, g_slots, gp_slots, qkv, a_slots, h, o, n1b, xhb,
        a_sems, g_sems,
    ):
        section = scal[0]
        low = section == 0
        high = section == 1
        g_hbm = out_hbm.at[:, :FF]
        n1_copy = copies.load(pack_hbm.at[:, D:], n1)
        xh_copy = copies.load(xh1_hbm, xh)
        wu_copies, wd_copies = pick_both(copies, low, wu_own, wu_rcv, wu, wd_own, wd_rcv, wd)
        wq_copies = [
            copies.pick(high, wq_own.at[:, cols], wq_rcv.at[:, cols], wq.at[:, cols])
            for cols in (slice(part * D, (part + 1) * D) for part in range(3))
        ]
        wo_copy = copies.pick(high, wo_own, wo_rcv, wo)
        wub_copies = pick_chunks(copies, high, wu_own, wu_rcv, wub, False)
        vec[...] = jnp.where(low, vec_own[...], vec_rcv[...])
        vecb[...] = jnp.where(high, vec_own[...], vec_rcv[...])
        make_bias(section, ends_ref, bias)
        xh_copy.wait()
        acc[...] = xh[...] * vec[at(G1)] + (vec[at(S1)] + vec[at(DB)])
        n1_copy.wait()
        mlp(n1, wu, wu_copies, wd, wd_copies, vec, g_hbm, gp_hbm, g_slots, gp_slots, g_sems, acc)
        rstds = []
        for rows in BLOCKS:
            normed, rstd, output = norm_two(rows, acc[rows, :], vec)
            xh[rows, :] = normed
            h[rows, :] = output.astype(BF)
            rstds.append(rstd)
        rstd2_ref[...] = as_row(jnp.concatenate(rstds, axis=0))
        copies.store(xh, xh2_hbm)
        copies.store(h, out_hbm.at[:, FF : FF + D])
        project(h, wq, wq_copies, vecb, qkv)
        copies.store(qkv, qkv_hbm)
        attend(qkv, bias, a_slots, a_hbm, a_sems, o)
        copies.store(o, out_hbm.at[:, FF + D : FF + 2 * D])
        wo_copy.wait()
        rstd1_ref[...] = norm_one(h, o, wo, vecb, xhb, n1b)
        copies.store(xhb, xh1b_hbm)
        copies.store(n1b, out_hbm.at[:, FF + 2 * D :])
        mlp_end(g_hbm, gp_hbm, g_slots, gp_slots, g_sems)
        mlp(n1b, wub, wub_copies, None, None, vecb, gb_hbm, gpb_hbm, g_slots, gp_slots, g_sems, None)
        attend_end(a_slots, a_hbm, a_sems)
        mlp_end(gb_hbm, gpb_hbm, g_slots, gp_slots, g_sems)
        copies.finish()

    f_act, wide = ((T, D), F32, ANY), ((T, FF), BF, ANY)
    line = ((1, T), F32, VMEM)
    return kernel_call(
        body, "middle", [SMEM, ANY, ANY, VMEM, VMEM, VMEM] + [ANY] * 8,
        (scal, pack, xh1, ends, vec_own, vec_rcv, wq_own, wq_rcv, wo_own, wo_rcv, wu_own, wu_rcv, wd_own, wd_rcv),
        [
            ((T, FF + 3 * D), BF, ANY), wide, f_act, ((T, 3 * D), BF, ANY), ((HEADS, T, T), BF, ANY), f_act, wide, wide,
            line, line,
        ],
        [
            pltpu.VMEM((T, D), BF), pltpu.VMEM((T, D), F32), pltpu.VMEM((T, D), F32),
            pltpu.VMEM((CHUNKS, D, CHUNK), BF), pltpu.VMEM((CHUNKS, CHUNK, D), BF), pltpu.VMEM((CHUNKS, D, CHUNK), BF),
            pltpu.VMEM((D, 3 * D), BF), pltpu.VMEM((D, D), BF),
            pltpu.VMEM((1, PARAMS * D), F32), pltpu.VMEM((1, PARAMS * D), F32), pltpu.VMEM((T, T), F32),
            pltpu.VMEM((2, T, CHUNK), BF), pltpu.VMEM((2, T, CHUNK), BF),
            pltpu.VMEM((T, 3 * D), BF), pltpu.VMEM((2, 2, T, T), BF),
            pltpu.VMEM((T, D), BF), pltpu.VMEM((T, D), BF), pltpu.VMEM((T, D), BF), pltpu.VMEM((T, D), F32),
            DMA((2,)), DMA((4,)),
        ],
        32, 30,
    )


def top(scal, g, xh1, vec_own, vec_rcv, wd_own, wd_rcv, cot, ends, termc, head):
    def body(
        copies, scal, g_hbm, xh1_hbm, vec_own, vec_rcv, wd_own, wd_rcv, cot_hbm, ends_ref, termc_ref, head_ref,
        h_hbm, dr2_hbm, dyk_hbm, dys_hbm, dy_hbm, z_ref, vg_ref,
        g, xh, wd, cot, vec, acc, h, dr2, dy,
    ):
        section = scal[0]
        is_own = section == 1
        xh_copy = copies.load(xh1_hbm, xh)
        wd_copies = []
        g_copies = []
        for step in range(CHUNKS):
            cols = slice(step * CHUNK, (step + 1) * CHUNK)
            g_copies.append(copies.load(g_hbm.at[:, cols], g.at[:, cols]))
            wd_copies.append(copies.pick(is_own, wd_own.at[cols], wd_rcv.at[cols], wd.at[cols]))
        cot_copy = copies.load(cot_hbm.at[pl.ds(pl.multiple_of(section * T, T), T)], cot)
        vec[...] = jnp.where(is_own, vec_own[...], vec_rcv[...])
        vg_ref[...] = jnp.zeros((1, GRADS * D), F32)
        mine = lanes(section * T, T)
        live_col = as_column(jnp.where(ends_ref[0:1, mine] > 0, 1.0, 0.0))
        term_col = as_column(termc_ref[0:1, mine])
        head = head_ref[...].astype(F32)
        xh_copy.wait()
        acc[...] = xh[...] * vec[at(G1)] + (vec[at(S1)] + vec[at(DB)])
        for step in range(CHUNKS):
            cols = slice(step * CHUNK, (step + 1) * CHUNK)
            g_copies[step].wait()
            wd_copies[step].wait()
            if step % 2:
                wide = slice((step - 1) * CHUNK, (step + 1) * CHUNK)
                for rows in BLOCKS:
                    acc[rows, :] += dot(g[rows, wide], wd[wide, :], 1, 0)
        cot_copy.wait()
        zs = []
        for rows in BLOCKS:
            normed, rstd, output = norm_two(rows, acc[rows, :], vec)
            h[rows, :] = output.astype(BF)
            z = jnp.sum(output * head, axis=-1, keepdims=True)
            zs.append(z)
            live = live_col[rows]
            slope = live * term_col[rows] / (1.0 + jnp.exp(-z))
            cotangent = live * cot[rows, :].astype(F32) + slope * head
            vg_ref[at(HD)] += col_sum(slope * output)
            norm_two_back(rows, cotangent, normed, rstd, vec, dr2, dy, vg_ref)
        z_ref[...] = as_row(jnp.concatenate(zs, axis=0))
        split_store(copies, section, dy, dyk_hbm, dys_hbm)
        copies.store(dy, dy_hbm)
        copies.store(dr2, dr2_hbm)
        copies.store(h, h_hbm)
        copies.finish()

    return kernel_call(
        body, "top", [SMEM, ANY, ANY, VMEM, VMEM, ANY, ANY, ANY, VMEM, VMEM, VMEM],
        (scal, g, xh1, vec_own, vec_rcv, wd_own, wd_rcv, cot, ends, termc, head),
        [
            ((T, D), BF, ANY), ((T, D), F32, ANY), ((T, HALF), BF, ANY), ((T, HALF), BF, ANY), ((T, D), BF, ANY),
            ((1, T), F32, VMEM), ((1, GRADS * D), F32, VMEM),
        ],
        [
            pltpu.VMEM((T, FF), BF), pltpu.VMEM((T, D), F32), pltpu.VMEM((FF, D), BF), pltpu.VMEM((T, D), BF),
            pltpu.VMEM((1, PARAMS * D), F32), pltpu.VMEM((T, D), F32), pltpu.VMEM((T, D), BF),
            pltpu.VMEM((T, D), F32), pltpu.VMEM((T, D), BF),
        ],
        16, 10,
    )


def back_outputs():
    return [
        ((T, FF // 2), BF, ANY), ((T, SEND), BF, ANY), ((T, MORE), BF, ANY), ((T, D), F32, ANY), ((T, D), BF, ANY),
        ((1, GRADS * D), F32, VMEM),
    ]


def back_scratch():
    return [
        pltpu.VMEM((T, D), BF), pltpu.VMEM((T, FF), BF), pltpu.VMEM((T, D), F32),
        pltpu.VMEM((CHUNKS, D, CHUNK), BF), pltpu.VMEM((CHUNKS, CHUNK, D), BF),
        pltpu.VMEM((1, PARAMS * D), F32), pltpu.VMEM((T, D), F32), pltpu.VMEM((T, FF), BF),
        pltpu.VMEM((T, D), F32), pltpu.VMEM((T, D), BF),
    ]


def mlp_backward(layer, scal, dr2, dy, vgin, gp, xh1, rstd1, vec_own, vec_rcv, wu_own, wu_rcv, wd_own, wd_rcv):
    def body(
        copies, scal, dr2_hbm, dy_hbm, vgin_ref, gp_hbm, xh1_hbm, rstd1_ref, vec_own, vec_rcv,
        wu_own, wu_rcv, wd_own, wd_rcv, *refs,
    ):
        duk_hbm, send_hbm, more_hbm, dr1_hbm, db_hbm, vg_ref, dy, gp, acc, wu, wd, vec, xh, du, dr1, db = refs
        section = scal[0]
        is_own = section == layer
        dy_copy = copies.load(dy_hbm, dy)
        acc_copy = copies.load(dr2_hbm, acc)
        gp_copy = copies.load(gp_hbm, gp)
        wu_copies, wd_copies = pick_both(copies, is_own, wu_own, wu_rcv, wu, wd_own, wd_rcv, wd)
        xh_copy = copies.load(xh1_hbm, xh)
        vec[...] = jnp.where(is_own, vec_own[...], vec_rcv[...])
        vg_ref[...] = vgin_ref[...]
        rstd = as_column(rstd1_ref[...])
        dy_copy.wait()
        acc_copy.wait()
        gp_copy.wait()
        mlp_back(dy, gp, wu, wu_copies, wd, wd_copies, acc, du, vg_ref)
        half = FF // 2
        copies.store(du.at[:, lanes(section * half, half)], duk_hbm)
        copies.store(du.at[:, lanes((1 - section) * half, SEND)], send_hbm)
        copies.store(du.at[:, lanes((1 - section) * half + SEND, half - SEND)], more_hbm.at[:, : half - SEND])
        xh_copy.wait()
        norm_one_back(acc, xh, rstd, vec, dr1, db, vg_ref)
        copies.store(db, db_hbm)
        copies.store(db.at[:, lanes((1 - section) * HALF, HALF)], more_hbm.at[:, half - SEND :])
        copies.store(dr1, dr1_hbm)
        copies.finish()

    return kernel_call(
        body, "mlp_backward", [SMEM, ANY, ANY, VMEM, ANY, ANY, VMEM, VMEM, VMEM] + [ANY] * 4,
        (scal, dr2, dy, vgin, gp, xh1, rstd1, vec_own, vec_rcv, wu_own, wu_rcv, wd_own, wd_rcv),
        back_outputs(), back_scratch(), 24, 13 * layer,
    )


def attention_back(
    low, scal, db, dr1, pack, o_at, qkv, a, vgin, wq_own, wq_rcv, wo_own, wo_rcv, below=()
):
    high = not low

    def body(
        copies, scal, db_hbm, dr1_hbm, pack_hbm, qkv_hbm, a_hbm, vgin_ref, wq_own, wq_rcv, wo_own, wo_rcv, *refs
    ):
        if high:
            (
                xh2_hbm, rstd2_ref, vec_own, vec_rcv,
                dpk_hbm, send_hbm, more_hbm, dx_hbm, vg_ref, dyk_hbm, dy_hbm, dr2_hbm, vgb_ref,
                dbv, dr1v, ov, qkvv, wq, wo, dmix, full, dx, a_slots, a_sems, dy, acc, xh, vec,
            ) = refs
        else:
            dpk_hbm, send_hbm, more_hbm, dx_hbm, vg_ref, *refs = refs
            dbv, dr1v, ov, qkvv, wq, wo, dmix, full, dx, a_slots, a_sems = refs
        section = scal[0]
        is_own = section == (0 if low else 1)
        db_copy = copies.load(db_hbm, dbv)
        wo_copy = copies.pick(is_own, wo_own, wo_rcv, wo)
        qkv_copy = copies.load(qkv_hbm, qkvv)
        o_copy = copies.load(pack_hbm.at[:, o_at : o_at + D], ov)
        for slot in range(2):
            pltpu.make_async_copy(a_hbm.at[pl.ds(2 * slot, 2)], a_slots.at[slot], a_sems.at[slot]).start()
        wq_copy = copies.pick(is_own, wq_own, wq_rcv, wq)
        dr1_copy = copies.load(dr1_hbm, dr1v)
        if high:
            xh2_copy = copies.load(xh2_hbm, xh)
            vec[...] = jnp.where(section == 0, vec_own[...], vec_rcv[...])
            vgb_ref[...] = jnp.zeros((1, GRADS * D), F32)
            rstd2 = as_column(rstd2_ref[...])
        vg_ref[...] = vgin_ref[...]
        db_copy.wait()
        wo_copy.wait()
        for tile in range(3):
            cols = slice(tile * 256, (tile + 1) * 256)
            dmix[:, cols] = dot(dbv[...], wo[cols, :], 1, 1).astype(BF)
        qkv_copy.wait()
        o_copy.wait()
        attend_back(qkvv, a_hbm, a_slots, a_sems, ov, dmix, full, vg_ref)
        for part in range(3):
            target = slice(part * HALF, (part + 1) * HALF)
            copies.store(full.at[:, lanes(part * D + section * HALF, HALF)], dpk_hbm.at[:, target])
            start = part * D + (1 - section) * HALF
            if part == 1:
                cut = QKV_SEND - HALF
                copies.store(full.at[:, lanes(start, cut)], send_hbm.at[:, HALF:])
                copies.store(full.at[:, lanes(start + cut, HALF - cut)], more_hbm.at[:, : HALF - cut])
            elif part == 0:
                copies.store(full.at[:, lanes(start, HALF)], send_hbm.at[:, :HALF])
            else:
                copies.store(full.at[:, lanes(start, HALF)], more_hbm.at[:, QKV_MORE - HALF : QKV_MORE])
        wq_copy.wait()
        dr1_copy.wait()
        if high:
            xh2_copy.wait()
        for rows in BLOCKS:
            for tile in range(3):
                cols = slice(tile * 256, (tile + 1) * 256)
                value = dr1v[rows, cols] + dot(full[rows, :], wq[cols, :], 1, 1)
                dx[rows, cols] = value.astype(BF)
            if high:
                norm_two_back(rows, dx[rows, :].astype(F32), xh[rows, :], rstd2[rows], vec, acc, dy, vgb_ref)
        copies.store(dx, dx_hbm)
        if high:
            copies.store(dy.at[:, lanes(section * HALF, HALF)], dyk_hbm)
            copies.store(dy.at[:, lanes((1 - section) * HALF, HALF)], more_hbm.at[:, QKV_MORE:])
            copies.store(dy, dy_hbm)
            copies.store(acc, dr2_hbm)
        copies.finish()

    specs = [SMEM, ANY, ANY, ANY, ANY, ANY, VMEM, ANY, ANY, ANY, ANY]
    width = QKV_MORE + (HALF if high else 0)
    outs = [
        ((T, 3 * HALF), BF, ANY), ((T, QKV_SEND), BF, ANY), ((T, width), BF, ANY), ((T, D), BF, ANY),
        ((1, GRADS * D), F32, VMEM),
    ]
    scratch = [
        pltpu.VMEM((T, D), BF), pltpu.VMEM((T, D), F32), pltpu.VMEM((T, D), BF), pltpu.VMEM((T, 3 * D), BF),
        pltpu.VMEM((D, 3 * D), BF), pltpu.VMEM((D, D), BF), pltpu.VMEM((T, D), BF), pltpu.VMEM((T, 3 * D), BF),
        pltpu.VMEM((T, D), BF), pltpu.VMEM((2, 2, T, T), BF), DMA((2,)),
    ]
    if high:
        specs += [ANY, VMEM, VMEM, VMEM]
        outs += [((T, HALF), BF, ANY), ((T, D), BF, ANY), ((T, D), F32, ANY), ((1, GRADS * D), F32, VMEM)]
        scratch += [
            pltpu.VMEM((T, D), BF), pltpu.VMEM((T, D), F32), pltpu.VMEM((T, D), F32), pltpu.VMEM((1, PARAMS * D), F32)
        ]
    return kernel_call(
        body, "low_attention_back" if low else "high_attention_back", specs,
        (scal, db, dr1, pack, qkv, a, vgin, wq_own, wq_rcv, wo_own, wo_rcv) + tuple(below),
        outs, scratch, 24, 17,
    )


class Pieces:
    def __init__(self, n, bits, my_bits, refs):
        self.n, self.bits, self.my_bits = n, bits, my_bits
        self.refs = refs

    def put(self, value, order, first, count, height, part):
        bit = self.bits[order]
        keep, send = self.refs[order]
        for kept in range(2):

            @pl.when(self.my_bits[order] == kept)
            def _():
                for block in range(count):
                    place = (block // (2 * bit)) * bit + block % bit
                    target = keep if (block // bit) % 2 == kept else send
                    target[first // 2 + place, part] = value[block * height : (block + 1) * height].astype(BF)


def weight_grads(n, bits, scal, units, plans, name, us):
    height = D // n
    widths = {"down": (FF, HALF), "up": (D, FF // 2), "attn": (D, D, 3 * HALF, HALF)}
    specs, args, scratch, counts = [SMEM], [scal], [], []
    for unit in units:
        arrays = [piece[0] for operand in unit[1:] if operand is not None for piece in operand]
        args += arrays
        specs += [ANY] * len(arrays)
        counts.append(len(arrays))
        scratch += [pltpu.VMEM((2 * T, width), BF) for width in widths[unit[0]]]
    sizes = [sum(plan.count(order) for plan in plans) for order in range(2)]
    in_use = [order for order in range(2) if sizes[order]]
    for plan in plans:
        for order in in_use:
            if order in plan:
                scratch += [pltpu.VMEM((n // 2, plan.count(order), height, HALF), BF)] * 2

    def body(copies, scal, *refs):
        refs = list(refs)
        section = scal[0]
        ins = [[refs.pop(0) for _ in range(count)] for count in counts]
        outs = {order: (refs.pop(0), refs.pop(0)) for order in in_use}
        mine = slice(0, T)
        theirs = slice(T, 2 * T)
        loaded = []
        for unit, arrays in zip(units, ins):
            arrays = list(arrays)
            buffers = [refs.pop(0) for _ in widths[unit[0]]]
            loads = []
            for which, buffer in enumerate(buffers):
                pair = unit[1 + 2 * which : 3 + 2 * which]
                if pair[1] is None:
                    array = arrays.pop(0)
                    for start, rows in ((section, mine), (1 - section, theirs)):
                        loads.append((array.at[pl.ds(pl.multiple_of(start * T, T), T)], buffer.at[rows]))
                    continue
                for operand, rows in zip(pair, (mine, theirs)):
                    filled = 0
                    for _, start, width in operand:
                        cols = lanes(section * HALF, width) if start == "half" else slice(start, start + width)
                        loads.append((arrays.pop(0).at[:, cols], buffer.at[rows, filled : filled + width]))
                        filled += width
            base = None
            if unit[0] == "down":
                waits = [copies.load(*load) for load in loads[2:]]
                base = copies.used
                for step in range(CHUNKS):
                    cols = slice(step * CHUNK, (step + 1) * CHUNK)
                    for source, target in loads[:2]:
                        copies.load(source.at[:, cols], target.at[:, cols])
            else:
                waits = [copies.load(*load) for load in loads]
            loaded.append((waits, buffers, base, loads))
        filled = [0, 0]
        for place, (unit, plan) in enumerate(zip(units, plans)):
            stages = {order: (refs.pop(0), refs.pop(0)) for order in in_use if order in plan}
            pieces = Pieces(n, bits, (scal[1], scal[2]), stages)
            slots = [plan[:part].count(plan[part]) for part in range(4)]
            waits, buffers, base, loads = loaded[place]
            for wait in waits:
                wait.wait()
            if unit[0] == "down":
                g, dy = buffers
                tall = FF // n
                count = CHUNK // tall

                def chunk(step, carry):
                    for side, (source, target) in enumerate(loads[:2]):
                        pltpu.make_async_copy(
                            source.at[:, :CHUNK], target.at[:, :CHUNK], copies.sems.at[base + 2 * step + side]
                        ).wait()
                    value = dot(g[:, lanes(step * CHUNK, CHUNK)], dy[...], 0, 0)
                    cut = value.reshape(count, 4, height, HALF)
                    for part in range(4):
                        rows = cut[:, part].reshape(count * height, HALF)
                        pieces.put(rows, plan[part], step * count, count, height, slots[part])
                    return carry

                lax.fori_loop(0, CHUNKS, chunk, 0)
            else:
                if unit[0] == "up":
                    left, right = buffers
                    terms = [(left, right, col) for col in range(4)]
                else:
                    x, o, dp, db = buffers
                    terms = [(x, dp, 0), (x, dp, 1), (x, dp, 2), (o, db, 0)]
                for part, (left, right, block) in enumerate(terms):
                    for half in range(2):
                        value = dot(
                            left[:, half * HALF : (half + 1) * HALF], right[:, block * HALF : (block + 1) * HALF], 0, 0
                        )
                        pieces.put(value, plan[part], half * (n // 2), n // 2, height, slots[part])
            for order, stage in stages.items():
                size = plan.count(order)
                for stage_ref, out in zip(stage, outs[order]):
                    copies.store(stage_ref, out.at[:, filled[order] : filled[order] + size])
                filled[order] += size
        copies.finish()

    out = [((n // 2, sizes[order], height, HALF), BF, ANY) for order in in_use for _ in range(2)]
    got = kernel_call(body, name, specs, tuple(args), out, scratch, 48, us)
    return [tuple(got[2 * place : 2 * place + 2]) for place in range(len(in_use))]


SWAP = [(0, 1), (1, 0)]


def swap(array):
    return lax.ppermute(array, "section", SWAP)


def across(array, bit, n):
    return lax.ppermute(array, "dp", [(i, i ^ bit) for i in range(n)])


def after(value, *others):
    return lax.optimization_barrier((value,) + others)[0]


class Halving:
    def __init__(self, n, index, split, bits):
        self.n, self.index, self.bits = n, index, list(bits)
        self.dims = [1 << place for place in reversed(range(n.bit_length() - 1))]
        self.tail = split[0].shape[1:]
        bit = self.bits.pop(0)
        self.dims.remove(bit)
        self.shape = (2,) * len(self.dims) + self.tail
        self.parts = [split[0].reshape(self.shape)]
        self.pending = across(split[1], bit, n).reshape(self.shape)

    def collect(self, *others):
        self.parts.append(after(self.pending, *others) if others else self.pending)

    def outgoing(self):
        bit = self.bits.pop(0)
        place = self.dims.index(bit)
        mine = (self.index // bit) % 2
        self.dims.pop(place)
        send = sum(
            lax.dynamic_index_in_dim(part, 1 - mine, place, keepdims=False).astype(F32) for part in self.parts
        ).astype(BF)
        self.parts = [lax.dynamic_index_in_dim(part, mine, place, keepdims=False) for part in self.parts]
        return send, bit

    def step(self, *others):
        self.collect(*others)
        send, bit = self.outgoing()
        self.pending = across(send, bit, self.n)
        return send

    def total(self, *others):
        self.collect(*others)
        return sum(part.astype(F32) for part in self.parts)


def step_together(chains, *others):
    if len(chains) == 1:
        return chains[0].step(*others)
    sends = []
    for chain in chains:
        chain.collect(*others)
        send, bit = chain.outgoing()
        sends.append(send)
    flat = jnp.concatenate([send.reshape((-1,) + send.shape[-2:]) for send in sends], axis=0)
    received = across(flat, bit, chains[0].n)
    start = 0
    for chain, send in zip(chains, sends):
        size = flat.shape[0] // len(chains)
        chain.pending = received[start : start + size].reshape(send.shape)
        start += size
    return flat


def per_device(
    tokens, seq_ends, qkv_weight, qv_bias, out_weight, out_bias, gain_one, shift_one, up_weight, up_bias,
    down_weight, down_bias, gain_two, shift_two, head_weight, out_cotangent, term_cotangent,
):
    n = lax.axis_size("dp")
    section = lax.axis_index("section")
    index = lax.axis_index("dp")
    is_first = section == 0
    if n == 16:
        orders = ([1, 2, 4, 8], [2, 1, 4, 8])
    else:
        ups = [1 << place for place in range(n.bit_length() - 1)]
        orders = (ups, ups[2:4] + ups[:2] + ups[4:])
    bits = (orders[0][0], orders[1][0])
    scal = jnp.stack([section, (index // bits[0]) % 2, (index // bits[1]) % 2]).astype(jnp.int32)

    wq, wo, wu, wd = qkv_weight[0], out_weight[0], up_weight[0], down_weight[0]
    wq_r = swap(wq)
    vec = pack_vectors((qv_bias, out_bias, gain_one, shift_one, down_bias, gain_two, shift_two, up_bias))
    vec_r = swap(vec)
    wo_r = swap(after(wo, vec))
    wu_r = swap(after(wu, wq_r, vec_r, wo_r))
    wd_r = swap(after(wd, wq_r, vec_r, wo_r))
    ends = seq_ends.reshape(1, 2 * T)
    termc = term_cotangent.reshape(1, 2 * T)
    head = head_weight.reshape(1, D)

    qkv1, a1, xh1_low, pack1, rstd1_low = first_attention(scal, tokens, ends, vec, vec_r, wq, wq_r, wo, wo_r)
    pack2, gp1, xh2_low, qkv2, a2, xh1_high, g2, gp2, rstd2_low, rstd1_high = middle(
        scal, pack1, xh1_low, ends, vec, vec_r, wq, wq_r, wo, wo_r, wu, wu_r, wd, wd_r
    )
    g2_r = swap(g2)
    pack2_r = swap(pack2)
    h2, dr2, dyk, dys, dy, z, vg_high = top(
        scal, g2, xh1_high, vec, vec_r, wd, wd_r, out_cotangent, ends, termc, head
    )
    dy_r = swap(dys)
    h2_r = swap(h2)

    def chain(split, which):
        return Halving(n, index, split, orders[which])

    def chains(grads):
        return [chain(split, which) for which, split in enumerate(grads)]

    def step_each(pair, *others):
        sent = step_together([pair[0]], *others)
        return step_together([pair[1]], sent)

    def col(array, start, width):
        return [(array, start, width)]

    def parts(first, second):
        rest = FF // 2 - SEND
        return [(first, 0, SEND), (second, 0, rest)], [(second, rest, HALF)]

    def qkv_parts(first, second):
        return [(first, 0, QKV_SEND), (second, 0, QKV_MORE)], [(second, QKV_MORE, HALF)]

    split, first_only, second_only = (0, 0, 1, 1), (0, 0, 0, 0), (1, 1, 1, 1)

    grads = weight_grads(
        n, bits, scal, [("down", col(g2, 0, FF), col(g2_r, 0, FF), col(dyk, 0, HALF), col(dy_r, 0, HALF))],
        [first_only], "high_down_grads", 7,
    )
    down_high = chain(grads[0], 0)
    duk, send, more, dr1, db, vg_high = mlp_backward(
        1, scal, after(dr2, grads[0][1], h2_r, pack2_r), dy, vg_high, gp2, xh1_high, rstd1_high, vec, vec_r,
        wu, wu_r, wd, wd_r,
    )
    du_r, db_high_r = parts(swap(send), swap(more))
    n_at = FF + 2 * D
    grads = weight_grads(
        n, bits, scal, [("up", col(pack2, n_at, D), col(pack2_r, n_at, D), col(duk, 0, FF // 2), du_r)],
        [second_only], "high_up_grads", 0,
    )
    sent = step_together([down_high], grads[0][1])
    pack1_r = swap(after(pack1, sent))
    up_high = chain(grads[0], 1)
    db_high = db
    dpk, send, more, d_top, vg_high, dyk, dy, dr2, vg_low = attention_back(
        False, scal, after(db, sent, grads[0][1]), dr1, pack2, FF + D, qkv2, a2, vg_high, wq, wq_r, wo, wo_r,
        (xh2_low, rstd2_low, vec, vec_r),
    )
    dp_r, dy_r = qkv_parts(swap(send), swap(more))
    d_top_r = swap(d_top)
    sent = step_together([down_high], dyk)

    duk, send, more, dr1, db, vg_low = mlp_backward(
        0, scal, after(dr2, sent, pack1_r), dy, vg_low, gp1, xh1_low, rstd1_low, vec, vec_r, wu, wu_r, wd, wd_r
    )
    send_r, more_r = swap(send), swap(more)
    du_r, db_low_r = parts(send_r, more_r)
    sent = step_together([up_high], db)
    sent = step_together([down_high], sent)
    grads = weight_grads(
        n, bits, scal,
        [(
            "attn", col(pack2, FF, D), col(pack2_r, FF, D), col(pack2, FF + D, D), col(pack2_r, FF + D, D),
            col(after(dpk, sent, d_top_r), 0, 3 * HALF), dp_r, col(db_high, "half", HALF), db_high_r,
        )],
        [split], "high_attn_grads", 9,
    )
    attn_high = chains(grads)
    sent = step_together([up_high], grads[0][1])
    z_r = swap(after(z, sent))
    grads = weight_grads(
        n, bits, scal,
        [
            (
                "down", col(pack2, 0, FF), col(pack2_r, 0, FF), col(after(dyk, sent, grads[1][1]), 0, HALF),
                dy_r,
            ),
            ("up", col(pack1, D, D), col(pack1_r, D, D), col(duk, 0, FF // 2), du_r),
        ],
        [first_only, second_only], "low_mlp_grads", 13,
    )
    mid = chains(grads)
    sent = step_each(attn_high, grads[0][1], z_r)
    sent = step_together([up_high], sent)
    dpk, send, more, d_low, vg_low = attention_back(
        True, scal, after(db, sent, grads[1][1]), dr1, pack1, 0, qkv1, a1, vg_low, wq, wq_r, wo, wo_r
    )
    dp_r, _ = qkv_parts(swap(send), swap(more))
    d_low_r = swap(d_low)
    sent = step_together(attn_high, dpk)
    grads = weight_grads(
        n, bits, scal,
        [(
            "attn", col(tokens, 0, D), None, col(pack1, 0, D), col(pack1_r, 0, D), col(after(dpk, sent), 0, 3 * HALF),
            dp_r, col(db, "half", HALF), db_low_r,
        )],
        [split], "low_attn_grads", 0,
    )
    last = chains(grads)

    vg = after(jnp.concatenate([vg_low, vg_high], axis=1), grads[0][1])
    vg = vg + swap(vg)
    vg_next = across(vg, orders[0][0], n)
    sent = step_each(mid, grads[1][1])
    sent = step_together(attn_high, sent)
    vg = vg + after(vg_next, sent)
    vg_next = across(vg, orders[0][1], n)
    sent = step_each(last, sent)
    for place in range(2, len(orders[0])):
        sent = step_together(mid, sent)
        vg = vg + after(vg_next, sent)
        vg_next = across(vg, orders[0][place], n)
        sent = step_together(last, sent)
        if place >= 4:
            for group in ([down_high], [up_high], attn_high):
                sent = step_together(group, sent)
    vg = vg + vg_next
    mid_sums = [part.total() for part in mid]
    attn_sums = [part.total() for part in attn_high]
    last_sums = [part.total() for part in last]

    def column(array, start, width):
        return array[:, start : start + width]

    h1, h1_r = column(pack2, FF, D), column(pack2_r, FF, D)

    def whole_unit(first, second):
        return jnp.concatenate([first, second], axis=0)

    low = mid_sums + [whole_unit(*last_sums)]
    high = [down_high.total(), up_high.total(), whole_unit(*attn_sums)]

    mine = jnp.where(is_first, vg[:, : GRADS * D], vg[:, GRADS * D :])
    small = D // n

    def share(place, count=1):
        width = count * small
        return lax.dynamic_slice(mine, (0, place * D + index * width), (1, width))

    head_share = lax.dynamic_slice(vg, (0, (GRADS + HD) * D + index * small), (1, small)).reshape(-1, 2)
    head_out = jnp.where(is_first, head_share[:, 0], head_share[:, 1])[:, None]

    own = [jnp.where(is_first, a, b) for a, b in zip(low, high)]
    other = [swap(jnp.where(is_first, b, a)) for a, b in zip(low, high)]
    left = [jnp.where(is_first, a, b) for a, b in zip(own, other)]
    right = [jnp.where(is_first, b, a) for a, b in zip(own, other)]
    down, up, attn = [jnp.stack([a, b]) for a, b in zip(left, right)]
    grad_down = down.transpose(1, 2, 0, 3).reshape(1, FF // n, D)
    grad_up = up.transpose(2, 0, 1, 3).reshape(1, small, FF)
    grad_qkv = attn[:, :3].transpose(2, 1, 0, 3).reshape(1, small, 3 * D)
    grad_out = attn[:, 3].transpose(1, 0, 2).reshape(1, small, D)

    def both(early, late):
        (own_low, other_low), (own_high, other_high) = early, late
        first = jnp.where(is_first, own_low, other_high)
        second = jnp.where(is_first, other_low, own_high)
        return jnp.concatenate([first, second], axis=0)[None]

    hidden = both((h1, h1_r), (h2, h2_r))
    input_out = both((d_low, d_low_r), (d_top, d_top_r))

    z_all = jnp.concatenate([jnp.where(is_first, z, z_r), jnp.where(is_first, z_r, z)], axis=1)[0]
    term = jnp.where(seq_ends > 0, jax.nn.softplus(z_all), 0.0).reshape(-1, 2)
    term_out = jnp.where(is_first, term[:, 0], term[:, 1])[:, None]

    return (
        hidden,
        term_out,
        input_out,
        grad_qkv,
        share(QB, 2),
        grad_out,
        share(OB),
        share(G1),
        share(S1),
        grad_up,
        share(UB, 4),
        grad_down,
        share(DB),
        share(G2),
        share(S2),
        head_out,
    )


def solution(mesh):
    in_specs = (
        P("dp", None),
        P("dp"),
        P("section", None, None),
        P("section", None),
        P("section", None, None),
        P("section", None),
        P("section", None),
        P("section", None),
        P("section", None, None),
        P("section", None),
        P("section", None, None),
        P("section", None),
        P("section", None),
        P("section", None),
        P(),
        P("dp", None),
        P("dp"),
    )
    out_specs = (
        P("section", "dp", None),
        P("dp", "section"),
        P("section", "dp", None),
        P("section", "dp", None),
        P("section", "dp"),
        P("section", "dp", None),
        P("section", "dp"),
        P("section", "dp"),
        P("section", "dp"),
        P("section", "dp", None),
        P("section", "dp"),
        P("section", "dp", None),
        P("section", "dp"),
        P("section", "dp"),
        P("section", "dp"),
        P("dp", "section"),
    )
    return jax.shard_map(per_device, mesh=mesh, in_specs=in_specs, out_specs=out_specs, check_vma=False)
```

time: 2190 us -> 359 us (0.16)
  waiting for transfers between devices: 1490 us -> 75.4 us
  matrix products: 424 us -> 0 us
  Pallas kernels: 0 us -> 183 us
  local copies, waits for them, and re-layouts: 115 us -> 15.2 us
  other arithmetic: 120 us -> 40 us
  starting transfers between devices: 10.5 us -> 40.3 us
    unnamed x22 -> x0, waiting for transfers between devices: 850 us -> none
    reduce_scatter x4 -> x0, waiting for transfers between devices: 640 us -> none  [per_device(): lax.psum_scatter(tuple((part[None] for part in summed)), 'dp', scatter_di...]
    dot_general x73 -> x0, matrix products: 391 us -> none  [the longest x6 90.4 us: layer_forward(): jnp.dot(active, down_weight, preferred_element_type=jnp.float32)]
    pallas_call x0 -> x13, Pallas kernels: none -> 183 us  [kernel_call(): pl.pallas_call(wrapped, in_specs=specs, out_specs=[spec for _, _, spec in...]
    ppermute x5 -> x55, waiting for transfers between devices: 2.18 us -> 75.4 us  [the longest x30 62.9 us: across(): return lax.ppermute(array, 'dp', [(i, i ^ bit) for i in range(n)])]
    unnamed x483 -> x78, local copies, waits for them, and re-layouts: 47.8 us -> 5.13 us
    reduce_sum x30 -> x0, other arithmetic: 39.1 us -> none  [the longest x3 9.99 us: layer_forward(): totals = jnp.sum(weights, axis=-1, keepdims=True)]
    convert_element_type x15 -> x0, local copies, waits for them, and re-layouts: 34.6 us -> none  [the longest x6 13.8 us: layer_forward(): (projected[:, 2 * model_width:] + qv_bias[model_width:]).astype(jnp.bfloa...]
  transfers between devices with their start and end apart: 18 -> 55, of which waited for: 12 -> 15; matrix products, arithmetic and copies ran while one was open for 13% -> 13% of each run, Pallas kernels for 0% -> 42%
where the time goes in v2:
time: 359 us; the launch traced here: 356 us
  Pallas kernels  183 us (51%)
  waiting for transfers between devices  75.4 us (21%)
  starting transfers between devices  40.3 us (11%)
  other arithmetic  40 us (11%)
  local copies, waits for them, and re-layouts  15.2 us (4%)
    pallas_call x13, Pallas kernels, kernel_call(): pl.pallas_call(wrapped, in_specs=specs, out_specs=[spec for _, _, spec in...  183 us
    ppermute x30, waiting for transfers between devices, across(): return lax.ppermute(array, 'dp', [(i, i ^ bit) for i in range(n)])  62.9 us
    ppermute x30, starting transfers between devices, across(): return lax.ppermute(array, 'dp', [(i, i ^ bit) for i in range(n)])  34.1 us
    convert_element_type x24, other arithmetic, outgoing(): send = sum((lax.dynamic_index_in_dim(part, 1 - mine, place, keepdims=Fals...  19.8 us
    ppermute x25, waiting for transfers between devices, swap(): return lax.ppermute(array, 'section', SWAP)  12.5 us
  transfers between devices with their start and end apart: 55, of which 15 were waited for; matrix products, arithmetic and copies ran while one was open for 13% of the time, Pallas kernels for 42%

profile of v2, /device:TPU:0, one launch (start us, length us, event | category | flops | bytes accessed | tf_op | source)
XLA Modules:
  0.0 355.6 jit_solution(11292175666809057886)
XLA Ops:
  3.2 4.1 %collective-permute-done.refs_4_.refs_5_.refs_8_.refs_14_ = f32[1,9216]{1,0:T(1,128)S(1)} collective-permute-done((f32[1,9216]{1,0:T(1,128)}, f32[1,9216]{1,0:T(1,128)S(1)}, u32[]{:S(2)}, u32[]{:S(2)}) %collective-permute-start) | collective-permute-done | bytes 36896 | tf_op jit(solution)/shard_map/ppermute | solution.py:879
  9.9 17.4 %first_attention.1 = (bf16[512,2304]{1,0:T(8,128)(2,1)}, bf16[12,512,512]{2,1,0:T(8,128)(2,1)}, f32[512,768]{1,0:T(8,128)}, bf16[512,1536]{1,0:T(8,128)(2,1)}, f32[1,512]{1,0:T(1,128)}) custom-call(s32[3]{0:T(128)} %pad_add_fusion.refs_0_, bf16[1024,768]{1,0:T(8,128)(2,1)} %refs_1_.5, s32[1,1024]{1,0:T(1,128)} %bitcast.322, ...), custom_call_target="tpu_custom_call" | custom-call | flops 15000000512 | bytes 30001000 | tf_op jit(solution)/shard_map/first_attention/pallas_call | solution.py:120
  27.3 34.7 %middle.1 = (bf16[512,5376]{1,0:T(8,128)(2,1)}, bf16[512,3072]{1,0:T(8,128)(2,1)}, f32[512,768]{1,0:T(8,128)}, bf16[512,2304]{1,0:T(8,128)(2,1)}, bf16[12,512,51...) custom-call(s32[3]{0:T(128)} %pad_add_fusion.refs_0_, ...), custom_call_target="tpu_custom_call" | custom-call | flops 30000001024 | bytes 60001000 | tf_op jit(solution)/shard_map/middle/pallas_call | solution.py:120
  63.2 10.7 %top.1 = (bf16[512,768]{1,0:T(8,128)(2,1)}, f32[512,768]{1,0:T(8,128)}, bf16[512,384]{1,0:T(8,128)(2,1)}, bf16[512,384]{1,0:T(8,128)(2,1)}, bf16[512,768]{1,0:T(...) custom-call(s32[3]{0:T(128)} %pad_add_fusion.refs_0_, bf16[512,3072]{1,0:T(8,128)(2,1)} %get-tuple-element.126.refs_1_, ...), custom_call_target="tpu_custom_call" | custom-call | flops 10000001024 | bytes 20001000 | tf_op jit(solution)/shard_map/top/pallas_call | solution.py:120
  74.4 2.0 collective-permute-done.8.refs_4_
  78.8 8.6 %high_down_grads.1 = (bf16[8,4,48,384]{3,2,1,0:T(8,128)(2,1)}, bf16[8,4,48,384]{3,2,1,0:T(8,128)(2,1)}) custom-call(s32[3]{0:T(128)} %pad_add_fusion.refs_0_, bf16[512,3072]{1,0:T(8,128)(2,1)} %get-tuple-element.126.refs_1_, bf16[512,3072]{1,0:T(8,128)(2,1)} %copy-done.33, bf16[512,384]{1,0:T(8,128)(2,1)} %get-tuple-element.131.refs_3_, ...), custom_call_target="tpu_custom_call" | custom-call | flops 7000001024 | bytes 14001000 | tf_op jit(solution)/shard_map/high_down_grads/pallas_call | solution.py:120
  87.4 2.9 collective-permute-start.12
  90.4 13.8 %mlp_backward.2 = (bf16[512,1536]{1,0:T(8,128)(2,1)}, bf16[512,1024]{1,0:T(8,128)(2,1)}, bf16[512,896]{1,0:T(8,128)(2,1)}, f32[512,768]{1,0:T(8,128)}, bf16[512,768]{1,0:T(8,128)(2,1)}, /*index=5*/f32[1,9984]{1,0:T(1,128)}) custom-call(s32[3]{0:T(128)} %pad_add_fusion.refs_0_, f32[512,768]{1,0:T(8,128)} %get-tuple-element.134.refs_1_, ...), custom_call_target="tpu_custom_call" | custom-call | flops 13000000512 | bytes 26001000 | tf_op jit(solution)/shard_map/mlp_backward/pallas_call | solution.py:120
  104.8 3.7 %collective-permute-done.10.refs_5_.refs_9_ = bf16[512,896]{1,0:T(8,128)(2,1)S(1)} collective-permute-done((bf16[512,896]{1,0:T(8,128)(2,1)}, bf16[512,896]{1,0:T(8,128)(2,1)S(1)}, u32[]{:S(2)}, u32[]{:S(2)}) %collective-permute-start.10) | collective-permute-done | bytes 917536 | tf_op jit(solution)/shard_map/ppermute | solution.py:879
  109.7 10.2 %high_up_grads.1 = (bf16[8,4,48,384]{3,2,1,0:T(8,128)(2,1)}, bf16[8,4,48,384]{3,2,1,0:T(8,128)(2,1)}) custom-call(s32[3]{0:T(128)} %pad_add_fusion.refs_0_, bf16[512,5376]{1,0:T(8,128)(2,1)} %get-tuple-element.125.refs_1_.refs_3_, bf16[512,5376]{1,0:T(8,128)(2,1)} %collective-permute-done.6.refs_2_.refs_4_, bf16[512,1536]{1,0:T(8,128)(2,1)} %get-tuple-element.139.refs_3_, ...), custom_call_target="tpu_custom_call" | custom-call | flops 1000 | bytes 1000 | tf_op jit(solution)/shard_map/high_up_grads/pallas_call | solution.py:120
  119.9 2.1 fusion
  124.1 19.3 %high_attention_back.1 = (bf16[512,1152]{1,0:T(8,128)(2,1)}, bf16[512,640]{1,0:T(8,128)(2,1)}, bf16[512,896]{1,0:T(8,128)(2,1)}, bf16[512,768]{1,0:T(8,128)(2,1)...) custom-call(s32[3]{0:T(128)} %pad_add_fusion.refs_0_, ...), custom_call_target="tpu_custom_call" | custom-call | flops 17000000512 | bytes 34001000 | tf_op jit(solution)/shard_map/high_attention_back/pallas_call | solution.py:120
  145.6 2.0 fusion.7
  150.4 13.8 %mlp_backward.3 = (bf16[512,1536]{1,0:T(8,128)(2,1)}, bf16[512,1024]{1,0:T(8,128)(2,1)}, bf16[512,896]{1,0:T(8,128)(2,1)}, f32[512,768]{1,0:T(8,128)}, bf16[512,768]{1,0:T(8,128)(2,1)}, /*index=5*/f32[1,9984]{1,0:T(1,128)}) custom-call(s32[3]{0:T(128)} %pad_add_fusion.refs_0_, f32[512,768]{1,0:T(8,128)} %get-tuple-element.158.refs_1_, ...), custom_call_target="tpu_custom_call" | custom-call | flops 1000 | bytes 1000 | tf_op jit(solution)/shard_map/mlp_backward/pallas_call | solution.py:120
  164.3 2.0 fusion.1
  166.9 1.9 fusion.25
  169.3 10.5 %high_attn_grads.1 = (bf16[8,2,48,384]{3,2,1,0:T(8,128)(2,1)}, bf16[8,2,48,384]{3,2,1,0:T(8,128)(2,1)}, bf16[8,2,48,384]{3,2,1,0:T(8,128)(2,1)}, bf16[8,2,48,384]{3,2,1,0:T(8,128)(2,1)}) custom-call(s32[3]{0:T(128)} %pad_add_fusion.refs_0_, bf16[512,5376]{1,0:T(8,128)(2,1)} %get-tuple-element.125.refs_1_.refs_3_, ...), custom_call_target="tpu_custom_call" | custom-call | flops 9000000512 | bytes 18001000 | tf_op jit(solution)/shard_map/high_attn_grads/pallas_call | solution.py:120
  179.8 2.0 collective-permute-done.15
  188.0 13.9 %low_mlp_grads.1 = (bf16[8,4,48,384]{3,2,1,0:T(8,128)(2,1)}, bf16[8,4,48,384]{3,2,1,0:T(8,128)(2,1)}, bf16[8,4,48,384]{3,2,1,0:T(8,128)(2,1)}, bf16[8,4,48,384]{3,2,1,0:T(8,128)(2,1)}) custom-call(s32[3]{0:T(128)} %pad_add_fusion.refs_0_, bf16[512,5376]{1,0:T(8,128)(2,1)} %get-tuple-element.125.refs_1_.refs_3_, ...), custom_call_target="tpu_custom_call" | custom-call | flops 13000000512 | bytes 26001000 | tf_op jit(solution)/shard_map/low_mlp_grads/pallas_call | solution.py:120
  211.4 17.7 %low_attention_back.1 = (bf16[512,1152]{1,0:T(8,128)(2,1)}, bf16[512,640]{1,0:T(8,128)(2,1)}, bf16[512,512]{1,0:T(8,128)(2,1)}, bf16[512,768]{1,0:T(8,128)(2,1)}, f32[1,9984]{1,0:T(1,128)}) custom-call(s32[3]{0:T(128)} %pad_add_fusion.refs_0_, bf16[512,768]{1,0:T(8,128)(2,1)} %get-tuple-element.186.refs_1_.refs_7_, f32[512,768]{1,0:T(8,128)} %get-tuple-element.187.refs_2_, ...), custom_call_target="tpu_custom_call" | custom-call | flops 17000000512 | bytes 34001000 | tf_op jit(solution)/shard_map/low_attention_back/pallas_call | solution.py:120
  231.3 4.8 %collective-permute-done.28 = bf16[2,2,2,48,384]{4,3,2,1,0:T(8,128)(2,1)} collective-permute-done((bf16[2,2,2,48,384]{4,3,2,1,0:T(8,128)(2,1)}, bf16[2,2,2,48,384]{4,3,2,1,0:T(8,128)(2,1)}, u32[]{:S(2)}, u32[]{:S(2)}) %collective-permute-start.28) | collective-permute-done | bytes 294944 | tf_op jit(solution)/shard_map/ppermute | solution.py:883
  242.3 2.7 collective-permute-start.53
  245.0 10.6 %low_attn_grads.1 = (bf16[8,2,48,384]{3,2,1,0:T(8,128)(2,1)}, bf16[8,2,48,384]{3,2,1,0:T(8,128)(2,1)}, bf16[8,2,48,384]{3,2,1,0:T(8,128)(2,1)}, bf16[8,2,48,384]{3,2,1,0:T(8,128)(2,1)}) custom-call(s32[3]{0:T(128)} %pad_add_fusion.refs_0_, bf16[1024,768]{1,0:T(8,128)(2,1)} %refs_1_.5, bf16[512,1536]{1,0:T(8,128)(2,1)} %get-tuple-element.157.refs_1_.refs_5_.refs_3_.refs_2_, ...), custom_call_target="tpu_custom_call" | custom-call | flops 1000 | bytes 1000 | tf_op jit(solution)/shard_map/low_attn_grads/pallas_call | solution.py:120
  267.2 6.1 %collective-permute-done.31 = bf16[8,2,48,384]{3,2,1,0:T(8,128)(2,1)S(1)} collective-permute-done((bf16[8,2,48,384]{3,2,1,0:T(8,128)(2,1)}, bf16[8,2,48,384]{3,2,1,0:T(8,128)(2,1)S(1)}, u32[]{:S(2)}, u32[]{:S(2)}) %collective-permute-start.31) | collective-permute-done | bytes 589856 | tf_op jit(solution)/shard_map/ppermute | solution.py:883
  275.8 10.8 %collective-permute-done.36 = bf16[2,2,4,48,384]{4,3,2,1,0:T(8,128)(2,1)S(1)} collective-permute-done((bf16[2,2,4,48,384]{4,3,2,1,0:T(8,128)(2,1)S(1)}, bf16[2,2,4,48,384]{4,3,2,1,0:T(8,128)(2,1)S(1)}, u32[]{:S(2)}, u32[]{:S(2)}) %collective-permute-start.36) | collective-permute-done | bytes 589856 | tf_op jit(solution)/shard_map/ppermute | solution.py:883
  289.0 5.5 %collective-permute-done.39 = bf16[2,2,2,48,384]{4,3,2,1,0:T(8,128)(2,1)S(1)} collective-permute-done((bf16[2,2,2,48,384]{4,3,2,1,0:T(8,128)(2,1)S(1)}, bf16[2,2,2,48,384]{4,3,2,1,0:T(8,128)(2,1)S(1)}, u32[]{:S(2)}, u32[]{:S(2)}) %collective-permute-start.39) | collective-permute-done | bytes 294944 | tf_op jit(solution)/shard_map/ppermute | solution.py:883
  298.1 1.9 collective-permute-start.51
  301.9 2.7 collective-permute-done.47
  306.3 11.9 %collective-permute-done.40 = bf16[8,48,384]{2,1,0:T(8,128)(2,1)S(1)} collective-permute-done((bf16[8,48,384]{2,1,0:T(8,128)(2,1)S(1)}, bf16[8,48,384]{2,1,0:T(8,128)(2,1)S(1)}, u32[]{:S(2)}, u32[]{:S(2)}) %collective-permute-start.40) | collective-permute-done | bytes 294944 | tf_op jit(solution)/shard_map/ppermute | solution.py:883
  320.4 2.4 collective-permute-start.49
  323.5 16.7 %collective-permute-done.49 = f32[1,19968]{1,0:T(1,128)S(1)} collective-permute-done((f32[1,19968]{1,0:T(1,128)S(1)}, f32[1,19968]{1,0:T(1,128)S(1)}, u32[]{:S(2)}, u32[]{:S(2)}) %collective-permute-start.49) | collective-permute-done | bytes 79904 | tf_op jit(solution)/shard_map/ppermute | solution.py:883
  346.4 2.1 broadcast_select_fusion.4
  (259 shorter events, 82.0 us)
Async XLA Ops:
  8.8 18.5 %collective-permute-start.3 = (bf16[768,3072]{1,0:T(8,128)(2,1)}, bf16[768,3072]{1,0:T(8,128)(2,1)}, u32[]{:S(2)}, u32[]{:S(2)}) collective-permute-start(bf16[768,3072]{1,0:T(8,128)(2,1)} %bitcast.256), channel_id=1, source_target_pairs={{0,16},{16,0},{1,17},{17,1},{2,18},{18,2},{3,19},{19,3},{4,20},{20... | collective-permute-start | bytes 14155784 | tf_op jit(solution)/shard_map/ppermute | solution.py:879
  9.1 18.1 %collective-permute-start.4 = (bf16[3072,768]{1,0:T(8,128)(2,1)}, bf16[3072,768]{1,0:T(8,128)(2,1)}, u32[]{:S(2)}, u32[]{:S(2)}) collective-permute-start(bf16[3072,768]{1,0:T(8,128)(2,1)} %bitcast.260), channel_id=1, source_target_pairs={{0,16},{16,0},{1,17},{17,1},{2,18},{18,2},{3,19},{19,3},{4,20},{20... | collective-permute-start | bytes 14155784 | tf_op jit(solution)/shard_map/ppermute | solution.py:879
  62.0 28.3 %collective-permute-start.6 = (bf16[512,5376]{1,0:T(8,128)(2,1)}, bf16[512,5376]{1,0:T(8,128)(2,1)}, u32[]{:S(2)}, u32[]{:S(2)}) collective-permute-start(bf16[512,5376]{1,0:T(8,128)(2,1)} %get-tuple-element.125.refs_1_.refs_3_), channel_id=1, source_target_pairs={{0,16},{16,0},{1,17},{17,1},{2,18},{18,2},{3,19},{19,3},{4,20},{20... | collective-permute-start | bytes 16515080 | tf_op jit(solution)/shard_map/ppermute | solution.py:879
  87.4 32.5 %collective-permute-start.12 = (bf16[8,4,48,384]{3,2,1,0:T(8,128)(2,1)}, bf16[8,4,48,384]{3,2,1,0:T(8,128)(2,1)}, u32[]{:S(2)}, u32[]{:S(2)}) collective-permute-start(bf16[8,4,48,384]{3,2,1,0:T(8,128)(2,1)} %get-tuple-element.133), channel_id=1, source_target_pairs={{0,1},{1,0},{2,3},{3,2},{4,5},{5,4},{6,7},{7,6},{8,9},{9,8},{10,11... | collective-permute-start | bytes 3538952 | tf_op jit(solution)/shard_map/ppermute | solution.py:883
  122.1 23.2 %collective-permute-start.13 = (bf16[2,2,4,48,384]{4,3,2,1,0:T(8,128)(2,1)}, bf16[2,2,4,48,384]{4,3,2,1,0:T(8,128)(2,1)}, u32[]{:S(2)}, u32[]{:S(2)}) collective-permute-start(bf16[2,2,4,48,384]{4,3,2,1,0:T(8,128)(2,1)} %fusion), channel_id=1, source_target_pairs={{0,2},{1,3},{2,0},{3,1},{4,6},{5,7},{6,4},{7,5},{8,10},{9,11},{10,... | collective-permute-start | bytes 1769480 | tf_op jit(solution)/shard_map/ppermute | solution.py:883
  123.6 40.6 %collective-permute-start.11 = (bf16[8,4,48,384]{3,2,1,0:T(8,128)(2,1)}, bf16[8,4,48,384]{3,2,1,0:T(8,128)(2,1)}, u32[]{:S(2)}, u32[]{:S(2)}) collective-permute-start(bf16[8,4,48,384]{3,2,1,0:T(8,128)(2,1)} %get-tuple-element.143), channel_id=1, source_target_pairs={{0,2},{1,3},{2,0},{3,1},{4,6},{5,7},{6,4},{7,5},{8,10},{9,11},{10,... | collective-permute-start | bytes 3538952 | tf_op jit(solution)/shard_map/ppermute | solution.py:883
  124.1 23.5 %collective-permute-start.14 = (bf16[512,1536]{1,0:T(8,128)(2,1)S(1)}, bf16[512,1536]{1,0:T(8,128)(2,1)}, u32[]{:S(2)}, u32[]{:S(2)}) collective-permute-start(bf16[512,1536]{1,0:T(8,128)(2,1)S(1)} %copy-done), channel_id=1, source_target_pairs={{0,16},{16,0},{1,17},{17,1},{2,18},{18,2},{3,19},{19,3},{4,20},{20... | collective-permute-start | bytes 4718600 | tf_op jit(solution)/shard_map/ppermute | solution.py:879
  143.4 25.3 %collective-permute-start.17 = (bf16[512,768]{1,0:T(8,128)(2,1)}, bf16[512,768]{1,0:T(8,128)(2,1)S(1)}, u32[]{:S(2)}, u32[]{:S(2)}) collective-permute-start(bf16[512,768]{1,0:T(8,128)(2,1)} %get-tuple-element.167), channel_id=1, source_target_pairs={{0,16},{16,0},{1,17},{17,1},{2,18},{18,2},{3,19},{19,3},{4,20},{20... | collective-permute-start | bytes 2359304 | tf_op jit(solution)/shard_map/ppermute | solution.py:879
  143.8 25.5 %collective-permute-start.19 = (bf16[512,896]{1,0:T(8,128)(2,1)}, bf16[512,896]{1,0:T(8,128)(2,1)}, u32[]{:S(2)}, u32[]{:S(2)}) collective-permute-start(bf16[512,896]{1,0:T(8,128)(2,1)} %get-tuple-element.170), channel_id=1, source_target_pairs={{0,16},{16,0},{1,17},{17,1},{2,18},{18,2},{3,19},{19,3},{4,20},{20... | collective-permute-start | bytes 2752520 | tf_op jit(solution)/shard_map/ppermute | solution.py:879
  145.3 24.0 %collective-permute-start.18 = (bf16[512,640]{1,0:T(8,128)(2,1)}, bf16[512,640]{1,0:T(8,128)(2,1)}, u32[]{:S(2)}, u32[]{:S(2)}) collective-permute-start(bf16[512,640]{1,0:T(8,128)(2,1)} %get-tuple-element.169), channel_id=1, source_target_pairs={{0,16},{16,0},{1,17},{17,1},{2,18},{18,2},{3,19},{19,3},{4,20},{20... | collective-permute-start | bytes 1966088 | tf_op jit(solution)/shard_map/ppermute | solution.py:879
  147.6 19.3 %collective-permute-start.16 = (bf16[2,4,48,384]{3,2,1,0:T(8,128)(2,1)}, bf16[2,4,48,384]{3,2,1,0:T(8,128)(2,1)S(1)}, u32[]{:S(2)}, u32[]{:S(2)}) collective-permute-start(bf16[2,4,48,384]{3,2,1,0:T(8,128)(2,1)} %fusion.7), channel_id=1, source_target_pairs={{0,4},{1,5},{2,6},{3,7},{4,0},{5,1},{6,2},{7,3},{8,12},{9,13},{10,... | collective-permute-start | bytes 884744 | tf_op jit(solution)/shard_map/ppermute | solution.py:883
  168.8 19.2 %collective-permute-start.25 = (bf16[512,896]{1,0:T(8,128)(2,1)}, bf16[512,896]{1,0:T(8,128)(2,1)}, u32[]{:S(2)}, u32[]{:S(2)}) collective-permute-start(bf16[512,896]{1,0:T(8,128)(2,1)} %get-tuple-element.180), channel_id=1, source_target_pairs={{0,16},{16,0},{1,17},{17,1},{2,18},{18,2},{3,19},{19,3},{4,20},{20... | collective-permute-start | bytes 2752520 | tf_op jit(solution)/shard_map/ppermute | solution.py:879
  168.8 19.2 %collective-permute-start.24 = (bf16[512,1024]{1,0:T(8,128)(2,1)}, bf16[512,1024]{1,0:T(8,128)(2,1)}, u32[]{:S(2)}, u32[]{:S(2)}) collective-permute-start(bf16[512,1024]{1,0:T(8,128)(2,1)} %get-tuple-element.179), channel_id=1, source_target_pairs={{0,16},{16,0},{1,17},{17,1},{2,18},{18,2},{3,19},{19,3},{4,20},{20... | collective-permute-start | bytes 3145736 | tf_op jit(solution)/shard_map/ppermute | solution.py:879
  184.3 19.1 %collective-permute-start.23 = (bf16[8,2,48,384]{3,2,1,0:T(8,128)(2,1)}, bf16[8,2,48,384]{3,2,1,0:T(8,128)(2,1)}, u32[]{:S(2)}, u32[]{:S(2)}) collective-permute-start(bf16[8,2,48,384]{3,2,1,0:T(8,128)(2,1)} %get-tuple-element.171), channel_id=1, source_target_pairs={{0,1},{1,0},{2,3},{3,2},{4,5},{5,4},{6,7},{7,6},{8,9},{9,8},{10,11... | collective-permute-start | bytes 1769480 | tf_op jit(solution)/shard_map/ppermute | solution.py:883
  184.9 20.8 %collective-permute-start.22 = (bf16[8,2,48,384]{3,2,1,0:T(8,128)(2,1)}, bf16[8,2,48,384]{3,2,1,0:T(8,128)(2,1)}, u32[]{:S(2)}, u32[]{:S(2)}) collective-permute-start(bf16[8,2,48,384]{3,2,1,0:T(8,128)(2,1)} %get-tuple-element.175), channel_id=1, source_target_pairs={{0,2},{1,3},{2,0},{3,1},{4,6},{5,7},{6,4},{7,5},{8,10},{9,11},{10,... | collective-permute-start | bytes 1769480 | tf_op jit(solution)/shard_map/ppermute | solution.py:883
  186.4 21.5 %collective-permute-start.21 = (bf16[2,4,48,384]{3,2,1,0:T(8,128)(2,1)S(1)}, bf16[2,4,48,384]{3,2,1,0:T(8,128)(2,1)S(1)}, u32[]{:S(2)}, u32[]{:S(2)}) collective-permute-start(bf16[2,4,48,384]{3,2,1,0:T(8,128)(2,1)S(1)} %fusion.6), channel_id=1, source_target_pairs={{0,4},{1,5},{2,6},{3,7},{4,0},{5,1},{6,2},{7,3},{8,12},{9,13},{10,... | collective-permute-start | bytes 884744 | tf_op jit(solution)/shard_map/ppermute | solution.py:883
  201.9 58.5 %collective-permute-start.34 = (bf16[8,4,48,384]{3,2,1,0:T(8,128)(2,1)}, bf16[8,4,48,384]{3,2,1,0:T(8,128)(2,1)S(1)}, u32[]{:S(2)}, u32[]{:S(2)}) collective-permute-start(bf16[8,4,48,384]{3,2,1,0:T(8,128)(2,1)} %get-tuple-element.181), channel_id=1, source_target_pairs={{0,1},{1,0},{2,3},{3,2},{4,5},{5,4},{6,7},{7,6},{8,9},{9,8},{10,11... | collective-permute-start | bytes 3538952 | tf_op jit(solution)/shard_map/ppermute | solution.py:883
  205.2 31.9 %collective-permute-start.27 = (bf16[2,2,2,48,384]{4,3,2,1,0:T(8,128)(2,1)}, bf16[2,2,2,48,384]{4,3,2,1,0:T(8,128)(2,1)}, u32[]{:S(2)}, u32[]{:S(2)}) collective-permute-start(bf16[2,2,2,48,384]{4,3,2,1,0:T(8,128)(2,1)} %fusion.10), channel_id=1, source_target_pairs={{0,2},{1,3},{2,0},{3,1},{4,6},{5,7},{6,4},{7,5},{8,10},{9,11},{10,... | collective-permute-start | bytes 884744 | tf_op jit(solution)/shard_map/ppermute | solution.py:883
  207.5 28.5 %collective-permute-start.28 = (bf16[2,2,2,48,384]{4,3,2,1,0:T(8,128)(2,1)}, bf16[2,2,2,48,384]{4,3,2,1,0:T(8,128)(2,1)}, u32[]{:S(2)}, u32[]{:S(2)}) collective-permute-start(bf16[2,2,2,48,384]{4,3,2,1,0:T(8,128)(2,1)} %fusion.11), channel_id=1, source_target_pairs={{0,1},{1,0},{2,3},{3,2},{4,5},{5,4},{6,7},{7,6},{8,9},{9,8},{10,11... | collective-permute-start | bytes 884744 | tf_op jit(solution)/shard_map/ppermute | solution.py:883
  209.7 51.4 %collective-permute-start.33 = (bf16[8,4,48,384]{3,2,1,0:T(8,128)(2,1)}, bf16[8,4,48,384]{3,2,1,0:T(8,128)(2,1)}, u32[]{:S(2)}, u32[]{:S(2)}) collective-permute-start(bf16[8,4,48,384]{3,2,1,0:T(8,128)(2,1)} %get-tuple-element.185), channel_id=1, source_target_pairs={{0,2},{1,3},{2,0},{3,1},{4,6},{5,7},{6,4},{7,5},{8,10},{9,11},{10,... | collective-permute-start | bytes 3538952 | tf_op jit(solution)/shard_map/ppermute | solution.py:883
  237.1 21.4 %collective-permute-start.26 = (bf16[512,768]{1,0:T(8,128)(2,1)}, bf16[512,768]{1,0:T(8,128)(2,1)}, u32[]{:S(2)}, u32[]{:S(2)}) collective-permute-start(bf16[512,768]{1,0:T(8,128)(2,1)} %get-tuple-element.191), channel_id=1, source_target_pairs={{0,16},{16,0},{1,17},{17,1},{2,18},{18,2},{3,19},{19,3},{4,20},{20... | collective-permute-start | bytes 2359304 | tf_op jit(solution)/shard_map/ppermute | solution.py:879
  242.3 102.0 %collective-permute-start.53 = (bf16[4,48,384]{2,1,0:T(8,128)(2,1)}, bf16[4,48,384]{2,1,0:T(8,128)(2,1)}, u32[]{:S(2)}, u32[]{:S(2)}) collective-permute-start(bf16[4,48,384]{2,1,0:T(8,128)(2,1)} %fusion.25), channel_id=1, source_target_pairs={{0,8},{1,9},{2,10},{3,11},{4,12},{5,13},{6,14},{7,15},{8,0},{9,1},... | collective-permute-start | bytes 442376 | tf_op jit(solution)/shard_map/ppermute | solution.py:883
  258.6 16.5 %collective-permute-start.37 = (bf16[8,2,48,384]{3,2,1,0:T(8,128)(2,1)}, bf16[8,2,48,384]{3,2,1,0:T(8,128)(2,1)S(1)}, u32[]{:S(2)}, u32[]{:S(2)}) collective-permute-start(bf16[8,2,48,384]{3,2,1,0:T(8,128)(2,1)} %get-tuple-element.202), channel_id=1, source_target_pairs={{0,2},{1,3},{2,0},{3,1},{4,6},{5,7},{6,4},{7,5},{8,10},{9,11},{10,... | collective-permute-start | bytes 1769480 | tf_op jit(solution)/shard_map/ppermute | solution.py:883
  260.4 37.7 %collective-permute-start.46 = (f32[1,19968]{1,0:T(1,128)S(1)}, f32[1,19968]{1,0:T(1,128)S(1)}, u32[]{:S(2)}, u32[]{:S(2)}) collective-permute-start(f32[1,19968]{1,0:T(1,128)S(1)} %add.1164), channel_id=1, source_target_pairs={{0,1},{1,0},{2,3},{3,2},{4,5},{5,4},{6,7},{7,6},{8,9},{9,8},{10,11... | collective-permute-start | bytes 239624 | tf_op jit(solution)/shard_map/ppermute | solution.py:883
  261.2 25.4 %collective-permute-start.36 = (bf16[2,2,4,48,384]{4,3,2,1,0:T(8,128)(2,1)S(1)}, bf16[2,2,4,48,384]{4,3,2,1,0:T(8,128)(2,1)S(1)}, u32[]{:S(2)}, u32[]{:S(2)}) collective-permute-start(bf16[2,2,4,48,384]{4,3,2,1,0:T(8,128)(2,1)S(1)} %fusion.2), channel_id=1, source_target_pairs={{0,2},{1,3},{2,0},{3,1},{4,6},{5,7},{6,4},{7,5},{8,10},{9,11},{10,... | collective-permute-start | bytes 1769480 | tf_op jit(solution)/shard_map/ppermute | solution.py:883
  273.3 26.7 %collective-permute-start.43 = (bf16[4,48,384]{2,1,0:T(8,128)(2,1)S(1)}, bf16[4,48,384]{2,1,0:T(8,128)(2,1)S(1)}, u32[]{:S(2)}, u32[]{:S(2)}) collective-permute-start(bf16[4,48,384]{2,1,0:T(8,128)(2,1)S(1)} %pad_maximum_fusion.7), channel_id=1, source_target_pairs={{0,8},{1,9},{2,10},{3,11},{4,12},{5,13},{6,14},{7,15},{8,0},{9,1},... | collective-permute-start | bytes 442376 | tf_op jit(solution)/shard_map/ppermute | solution.py:883
  294.5 23.7 %collective-permute-start.41 = (bf16[16,48,384]{2,1,0:T(8,128)(2,1)S(1)}, bf16[16,48,384]{2,1,0:T(8,128)(2,1)S(1)}, u32[]{:S(2)}, u32[]{:S(2)}) collective-permute-start(bf16[16,48,384]{2,1,0:T(8,128)(2,1)S(1)} %pad_maximum_fusion), channel_id=1, source_target_pairs={{0,4},{1,5},{2,6},{3,7},{4,0},{5,1},{6,2},{7,3},{8,12},{9,13},{10,... | collective-permute-start | bytes 1769480 | tf_op jit(solution)/shard_map/ppermute | solution.py:883
  295.2 23.0 %collective-permute-start.40 = (bf16[8,48,384]{2,1,0:T(8,128)(2,1)S(1)}, bf16[8,48,384]{2,1,0:T(8,128)(2,1)S(1)}, u32[]{:S(2)}, u32[]{:S(2)}) collective-permute-start(bf16[8,48,384]{2,1,0:T(8,128)(2,1)S(1)} %pad_maximum_fusion.2), channel_id=1, source_target_pairs={{0,4},{1,5},{2,6},{3,7},{4,0},{5,1},{6,2},{7,3},{8,12},{9,13},{10,... | collective-permute-start | bytes 884744 | tf_op jit(solution)/shard_map/ppermute | solution.py:883
  298.1 48.3 %collective-permute-start.51 = (bf16[4,48,384]{2,1,0:T(8,128)(2,1)}, bf16[4,48,384]{2,1,0:T(8,128)(2,1)}, u32[]{:S(2)}, u32[]{:S(2)}) collective-permute-start(bf16[4,48,384]{2,1,0:T(8,128)(2,1)} %fusion.24), channel_id=1, source_target_pairs={{0,8},{1,9},{2,10},{3,11},{4,12},{5,13},{6,14},{7,15},{8,0},{9,1},... | collective-permute-start | bytes 442376 | tf_op jit(solution)/shard_map/ppermute | solution.py:883
  319.5 24.8 %collective-permute-start.50 = (bf16[8,48,384]{2,1,0:T(8,128)(2,1)S(1)}, bf16[8,48,384]{2,1,0:T(8,128)(2,1)S(1)}, u32[]{:S(2)}, u32[]{:S(2)}) collective-permute-start(bf16[8,48,384]{2,1,0:T(8,128)(2,1)S(1)} %pad_maximum_fusion.3), channel_id=1, source_target_pairs={{0,8},{1,9},{2,10},{3,11},{4,12},{5,13},{6,14},{7,15},{8,0},{9,1},... | collective-permute-start | bytes 884744 | tf_op jit(solution)/shard_map/ppermute | solution.py:883
  320.4 19.7 %collective-permute-start.49 = (f32[1,19968]{1,0:T(1,128)S(1)}, f32[1,19968]{1,0:T(1,128)S(1)}, u32[]{:S(2)}, u32[]{:S(2)}) collective-permute-start(f32[1,19968]{1,0:T(1,128)S(1)} %add.1167), channel_id=1, source_target_pairs={{0,8},{1,9},{2,10},{3,11},{4,12},{5,13},{6,14},{7,15},{8,0},{9,1},... | collective-permute-start | bytes 239624 | tf_op jit(solution)/shard_map/ppermute | solution.py:883
  322.9 20.1 %collective-permute-start.42 = (bf16[4,48,384]{2,1,0:T(8,128)(2,1)S(1)}, bf16[4,48,384]{2,1,0:T(8,128)(2,1)S(1)}, u32[]{:S(2)}, u32[]{:S(2)}) collective-permute-start(bf16[4,48,384]{2,1,0:T(8,128)(2,1)S(1)} %pad_maximum_fusion.8), channel_id=1, source_target_pairs={{0,8},{1,9},{2,10},{3,11},{4,12},{5,13},{6,14},{7,15},{8,0},{9,1},... | collective-permute-start | bytes 442376 | tf_op jit(solution)/shard_map/ppermute | solution.py:883
  (61 other events, 685.5 us)

commit v3 on v2

--- a/solution.py
+++ b/solution.py
@@ -30,9 +30,7 @@
 PARAMS = 12
 GRADS = 13
 SEND = 1024
-MORE = FF // 2 + HALF - SEND
-QKV_SEND = 640
-QKV_MORE = 3 * HALF - QKV_SEND
+TILE = 16
 
 ANY = pl.BlockSpec(memory_space=pl.ANY)
 VMEM = pl.BlockSpec(memory_space=pltpu.VMEM)
@@ -225,7 +223,14 @@
     return value, cdf + u * bell * 0.3989422804014327
 
 
-def mlp(n1_ref, wu, wu_copies, wd, wd_copies, vec, g_hbm, gp_hbm, g_slots, gp_slots, g_sems, acc):
+def in_two(body, hook):
+    lax.fori_loop(0, 1, body, 0)
+    if hook is not None:
+        hook()
+    lax.fori_loop(1, CHUNKS, body, 0)
+
+
+def mlp(n1_ref, wu, wu_copies, wd, wd_copies, vec, g_hbm, gp_hbm, g_slots, gp_slots, g_sems, acc, hook=None):
     def chunk(step, carry):
         slot = lax.rem(step, 2)
         cols = lanes(step * CHUNK, CHUNK)
@@ -253,7 +258,7 @@
         slope_out.start()
         return carry
 
-    lax.fori_loop(0, CHUNKS, chunk, 0)
+    in_two(chunk, hook)
 
 
 def mlp_end(g_hbm, gp_hbm, g_slots, gp_slots, g_sems):
@@ -284,10 +289,11 @@
     vg_ref[at(DB)] += col_sum(low.astype(F32))
 
 
-def mlp_back(dy_ref, gp, wu, wu_copies, wd, wd_copies, acc, du, vg_ref):
+def mlp_back(dy_ref, gp, gp_copies, wu, wu_copies, wd, wd_copies, acc, du, vg_ref, hook=None):
     def chunk(step, carry):
         cols = lanes(step * CHUNK, CHUNK)
         wd_copies(step).wait()
+        gp_copies(step).wait()
         wu_copies(step).wait()
         total = None
         for rows in BLOCKS:
@@ -300,7 +306,7 @@
         vg_ref[0:1, lanes(UB * D + step * CHUNK, CHUNK)] = total
         return carry
 
-    lax.fori_loop(0, CHUNKS, chunk, 0)
+    in_two(chunk, hook)
 
 
 def norm_one_back(acc, xh_ref, rstd, vec, dr1_ref, db_ref, vg_ref):
@@ -354,8 +360,9 @@
         d_q = jnp.concatenate(d_q, axis=0).astype(BF) * jnp.asarray(SCALE, BF)
         d_k = d_k.astype(BF)
         d_v = d_v.astype(BF)
-        vg_ref[0:1, lanes(QB * D + off, PAIR)] = col_sum(d_q.astype(F32))
-        vg_ref[0:1, lanes(VB * D + off, PAIR)] = col_sum(d_v.astype(F32))
+        if vg_ref is not None:
+            vg_ref[0:1, lanes(QB * D + off, PAIR)] = col_sum(d_q.astype(F32))
+            vg_ref[0:1, lanes(VB * D + off, PAIR)] = col_sum(d_v.astype(F32))
         for part, value in enumerate((d_q, d_k, d_v)):
             full[:, lanes(part * D + off, PAIR)] = value
 
@@ -366,15 +373,6 @@
         return carry
 
     lax.fori_loop(0, PAIRS, pair, 0)
-
-
-def split_store(copies, section, source, keep, send, parts=1):
-    width = source.shape[1] // parts
-    half = width // 2
-    for part in range(parts):
-        target = slice(part * half, (part + 1) * half)
-        copies.store(source.at[:, lanes(part * width + section * half, half)], keep.at[:, target])
-        copies.store(source.at[:, lanes(part * width + (1 - section) * half, half)], send.at[:, target])
 
 
 def first_attention(scal, tokens, ends, vec_own, vec_rcv, wq_own, wq_rcv, wo_own, wo_rcv):
@@ -443,20 +441,27 @@
     return chunk_copy
 
 
-def pick_both(copies, is_own, wu_own, wu_rcv, wu, wd_own, wd_rcv, wd):
+def pick_both(copies, is_own, wu_own, wu_rcv, wu, wd_own, wd_rcv, wd, gp_hbm=None, gp=None):
     base = copies.used
+    kinds = 2 if gp is None else 3
     for step in range(CHUNKS):
         cols = pl.ds(step * CHUNK, CHUNK)
         copies.pick(is_own, wu_own.at[:, cols], wu_rcv.at[:, cols], wu.at[step])
         copies.pick(is_own, wd_own.at[cols], wd_rcv.at[cols], wd.at[step])
+        if gp is not None:
+            copies.load(gp_hbm.at[:, cols], gp.at[:, cols])
+    first = pl.ds(0, CHUNK)
 
     def wu_copy(step):
-        return pltpu.make_async_copy(wu_own.at[:, pl.ds(0, CHUNK)], wu.at[step], copies.sems.at[base + 2 * step])
+        return pltpu.make_async_copy(wu_own.at[:, first], wu.at[step], copies.sems.at[base + kinds * step])
 
     def wd_copy(step):
-        return pltpu.make_async_copy(wd_own.at[pl.ds(0, CHUNK)], wd.at[step], copies.sems.at[base + 2 * step + 1])
-
-    return wu_copy, wd_copy
+        return pltpu.make_async_copy(wd_own.at[first], wd.at[step], copies.sems.at[base + kinds * step + 1])
+
+    def gp_copy(step):
+        return pltpu.make_async_copy(gp_hbm.at[:, first], gp.at[:, first], copies.sems.at[base + kinds * step + 2])
+
+    return (wu_copy, wd_copy) if gp is None else (wu_copy, wd_copy, gp_copy)
 
 
 def middle(scal, pack, xh1, ends, vec_own, vec_rcv, wq_own, wq_rcv, wo_own, wo_rcv, wu_own, wu_rcv, wd_own, wd_rcv):
@@ -474,19 +479,23 @@
         n1_copy = copies.load(pack_hbm.at[:, D:], n1)
         xh_copy = copies.load(xh1_hbm, xh)
         wu_copies, wd_copies = pick_both(copies, low, wu_own, wu_rcv, wu, wd_own, wd_rcv, wd)
-        wq_copies = [
-            copies.pick(high, wq_own.at[:, cols], wq_rcv.at[:, cols], wq.at[:, cols])
-            for cols in (slice(part * D, (part + 1) * D) for part in range(3))
-        ]
-        wo_copy = copies.pick(high, wo_own, wo_rcv, wo)
-        wub_copies = pick_chunks(copies, high, wu_own, wu_rcv, wub, False)
+        later = {}
+
+        def more_loads():
+            later["wq"] = [
+                copies.pick(high, wq_own.at[:, cols], wq_rcv.at[:, cols], wq.at[:, cols])
+                for cols in (slice(part * D, (part + 1) * D) for part in range(3))
+            ]
+            later["wo"] = copies.pick(high, wo_own, wo_rcv, wo)
+            later["wu"] = pick_chunks(copies, high, wu_own, wu_rcv, wub, False)
+
         vec[...] = jnp.where(low, vec_own[...], vec_rcv[...])
         vecb[...] = jnp.where(high, vec_own[...], vec_rcv[...])
         make_bias(section, ends_ref, bias)
         xh_copy.wait()
         acc[...] = xh[...] * vec[at(G1)] + (vec[at(S1)] + vec[at(DB)])
         n1_copy.wait()
-        mlp(n1, wu, wu_copies, wd, wd_copies, vec, g_hbm, gp_hbm, g_slots, gp_slots, g_sems, acc)
+        mlp(n1, wu, wu_copies, wd, wd_copies, vec, g_hbm, gp_hbm, g_slots, gp_slots, g_sems, acc, more_loads)
         rstds = []
         for rows in BLOCKS:
             normed, rstd, output = norm_two(rows, acc[rows, :], vec)
@@ -496,16 +505,16 @@
         rstd2_ref[...] = as_row(jnp.concatenate(rstds, axis=0))
         copies.store(xh, xh2_hbm)
         copies.store(h, out_hbm.at[:, FF : FF + D])
-        project(h, wq, wq_copies, vecb, qkv)
+        project(h, wq, later["wq"], vecb, qkv)
         copies.store(qkv, qkv_hbm)
         attend(qkv, bias, a_slots, a_hbm, a_sems, o)
         copies.store(o, out_hbm.at[:, FF + D : FF + 2 * D])
-        wo_copy.wait()
+        later["wo"].wait()
         rstd1_ref[...] = norm_one(h, o, wo, vecb, xhb, n1b)
         copies.store(xhb, xh1b_hbm)
         copies.store(n1b, out_hbm.at[:, FF + 2 * D :])
         mlp_end(g_hbm, gp_hbm, g_slots, gp_slots, g_sems)
-        mlp(n1b, wub, wub_copies, None, None, vecb, gb_hbm, gpb_hbm, g_slots, gp_slots, g_sems, None)
+        mlp(n1b, wub, later["wu"], None, None, vecb, gb_hbm, gpb_hbm, g_slots, gp_slots, g_sems, None)
         attend_end(a_slots, a_hbm, a_sems)
         mlp_end(gb_hbm, gpb_hbm, g_slots, gp_slots, g_sems)
         copies.finish()
@@ -578,7 +587,8 @@
             vg_ref[at(HD)] += col_sum(slope * output)
             norm_two_back(rows, cotangent, normed, rstd, vec, dr2, dy, vg_ref)
         z_ref[...] = as_row(jnp.concatenate(zs, axis=0))
-        split_store(copies, section, dy, dyk_hbm, dys_hbm)
+        copies.store(dy.at[:, lanes(section * HALF, HALF)], dyk_hbm)
+        copies.store(dy.at[:, lanes((1 - section) * HALF, HALF)], dys_hbm)
         copies.store(dy, dy_hbm)
         copies.store(dr2, dr2_hbm)
         copies.store(h, h_hbm)
@@ -600,14 +610,53 @@
     )
 
 
-def back_outputs():
-    return [
-        ((T, FF // 2), BF, ANY), ((T, SEND), BF, ANY), ((T, MORE), BF, ANY), ((T, D), F32, ANY), ((T, D), BF, ANY),
-        ((1, GRADS * D), F32, VMEM),
+class AttentionBack:
+    scratch = [
+        pltpu.VMEM((T, D), BF), pltpu.VMEM((T, 3 * D), BF), pltpu.VMEM((D, 3 * D), BF), pltpu.VMEM((D, D), BF),
+        pltpu.VMEM((T, D), BF), pltpu.VMEM((T, 3 * D), BF), pltpu.VMEM((T, D), BF), pltpu.VMEM((2, 2, T, T), BF),
+        DMA((2,)),
     ]
 
-
-def back_scratch():
+    def __init__(self, copies, section, is_own, refs):
+        self.copies, self.section, self.is_own = copies, section, is_own
+        self.o, self.qkv, self.wq, self.wo, self.dmix, self.full, self.dx, self.a_slots, self.a_sems = refs
+
+    def load(self, pack_hbm, o_at, qkv_hbm, a_hbm, wq_own, wq_rcv, wo_own, wo_rcv):
+        copies = self.copies
+        self.a_hbm = a_hbm
+        self.first = [
+            copies.pick(self.is_own, wo_own, wo_rcv, self.wo), copies.load(qkv_hbm, self.qkv),
+            copies.load(pack_hbm.at[:, o_at : o_at + D], self.o),
+        ]
+        for slot in range(2):
+            pltpu.make_async_copy(a_hbm.at[pl.ds(2 * slot, 2)], self.a_slots.at[slot], self.a_sems.at[slot]).start()
+        self.wq_copy = copies.pick(self.is_own, wq_own, wq_rcv, self.wq)
+
+    def heads(self, db, vg_ref):
+        for copy in self.first:
+            copy.wait()
+        for tile in range(3):
+            cols = slice(tile * 256, (tile + 1) * 256)
+            self.dmix[:, cols] = dot(db[...], self.wo[cols, :], 1, 1).astype(BF)
+        attend_back(self.qkv, self.a_hbm, self.a_slots, self.a_sems, self.o, self.dmix, self.full, vg_ref)
+
+    def half(self, part, whose, start, width):
+        return self.full.at[:, lanes(part * D + whose * HALF + start, width)]
+
+    def store(self, dpk_hbm, targets):
+        for part in range(3):
+            self.copies.store(self.half(part, self.section, 0, HALF), dpk_hbm.at[:, part * HALF : (part + 1) * HALF])
+        for part, start, width, ref in targets:
+            self.copies.store(self.half(part, 1 - self.section, start, width), ref)
+
+    def to_input(self, rows, dr1):
+        for tile in range(3):
+            cols = slice(tile * 256, (tile + 1) * 256)
+            value = dr1[rows, cols] + dot(self.full[rows, :], self.wq[cols, :], 1, 1)
+            self.dx[rows, cols] = value.astype(BF)
+
+
+def mlp_back_scratch():
     return [
         pltpu.VMEM((T, D), BF), pltpu.VMEM((T, FF), BF), pltpu.VMEM((T, D), F32),
         pltpu.VMEM((CHUNKS, D, CHUNK), BF), pltpu.VMEM((CHUNKS, CHUNK, D), BF),
@@ -616,146 +665,102 @@
     ]
 
 
-def mlp_backward(layer, scal, dr2, dy, vgin, gp, xh1, rstd1, vec_own, vec_rcv, wu_own, wu_rcv, wd_own, wd_rcv):
+def layer_backward(
+    layer, scal, dr2, dy, vgin, gp, xh1, rstd1, vec_own, vec_rcv, wu_own, wu_rcv, wd_own, wd_rcv,
+    pack, o_at, qkv, a, wq_own, wq_rcv, wo_own, wo_rcv, below=(),
+):
     def body(
         copies, scal, dr2_hbm, dy_hbm, vgin_ref, gp_hbm, xh1_hbm, rstd1_ref, vec_own, vec_rcv,
-        wu_own, wu_rcv, wd_own, wd_rcv, *refs,
+        wu_own, wu_rcv, wd_own, wd_rcv, pack_hbm, qkv_hbm, a_hbm, wq_own, wq_rcv, wo_own, wo_rcv, *refs,
     ):
-        duk_hbm, send_hbm, more_hbm, dr1_hbm, db_hbm, vg_ref, dy, gp, acc, wu, wd, vec, xh, du, dr1, db = refs
+        if layer:
+            xh2_hbm, rstd2_ref, *refs = refs
+        duk_hbm, db_hbm, dpk_hbm, send_a, send_b, send_c, dx_hbm, vg_ref, *refs = refs
+        if layer:
+            dys_hbm, dyk_hbm, dylow_hbm, dr2low_hbm, vglow_ref, *refs = refs
+        dy, gp, acc, wu, wd, vec, xh, du, dr1, db, *refs = refs
         section = scal[0]
         is_own = section == layer
+        other = 1 - section
+        attn = AttentionBack(copies, section, is_own, refs)
         dy_copy = copies.load(dy_hbm, dy)
+        wu_copies, wd_copies, gp_copies = pick_both(
+            copies, is_own, wu_own, wu_rcv, wu, wd_own, wd_rcv, wd, gp_hbm, gp
+        )
         acc_copy = copies.load(dr2_hbm, acc)
-        gp_copy = copies.load(gp_hbm, gp)
-        wu_copies, wd_copies = pick_both(copies, is_own, wu_own, wu_rcv, wu, wd_own, wd_rcv, wd)
         xh_copy = copies.load(xh1_hbm, xh)
         vec[...] = jnp.where(is_own, vec_own[...], vec_rcv[...])
         vg_ref[...] = vgin_ref[...]
         rstd = as_column(rstd1_ref[...])
+        if layer:
+            vglow_ref[...] = jnp.zeros((1, GRADS * D), F32)
+            rstd2 = as_column(rstd2_ref[...])
         dy_copy.wait()
         acc_copy.wait()
-        gp_copy.wait()
-        mlp_back(dy, gp, wu, wu_copies, wd, wd_copies, acc, du, vg_ref)
+        mlp_back(
+            dy, gp, gp_copies, wu, wu_copies, wd, wd_copies, acc, du, vg_ref,
+            lambda: attn.load(pack_hbm, o_at, qkv_hbm, a_hbm, wq_own, wq_rcv, wo_own, wo_rcv),
+        )
         half = FF // 2
         copies.store(du.at[:, lanes(section * half, half)], duk_hbm)
-        copies.store(du.at[:, lanes((1 - section) * half, SEND)], send_hbm)
-        copies.store(du.at[:, lanes((1 - section) * half + SEND, half - SEND)], more_hbm.at[:, : half - SEND])
+        copies.store(du.at[:, lanes(other * half, SEND)], send_a)
+        copies.store(du.at[:, lanes(other * half + SEND, half - SEND)], send_b.at[:, : half - SEND])
         xh_copy.wait()
         norm_one_back(acc, xh, rstd, vec, dr1, db, vg_ref)
+        if layer:
+            xh2_copy = copies.load(xh2_hbm, xh)
         copies.store(db, db_hbm)
-        copies.store(db.at[:, lanes((1 - section) * HALF, HALF)], more_hbm.at[:, half - SEND :])
-        copies.store(dr1, dr1_hbm)
-        copies.finish()
-
-    return kernel_call(
-        body, "mlp_backward", [SMEM, ANY, ANY, VMEM, ANY, ANY, VMEM, VMEM, VMEM] + [ANY] * 4,
-        (scal, dr2, dy, vgin, gp, xh1, rstd1, vec_own, vec_rcv, wu_own, wu_rcv, wd_own, wd_rcv),
-        back_outputs(), back_scratch(), 24, 13 * layer,
-    )
-
-
-def attention_back(
-    low, scal, db, dr1, pack, o_at, qkv, a, vgin, wq_own, wq_rcv, wo_own, wo_rcv, below=()
-):
-    high = not low
-
-    def body(
-        copies, scal, db_hbm, dr1_hbm, pack_hbm, qkv_hbm, a_hbm, vgin_ref, wq_own, wq_rcv, wo_own, wo_rcv, *refs
-    ):
-        if high:
-            (
-                xh2_hbm, rstd2_ref, vec_own, vec_rcv,
-                dpk_hbm, send_hbm, more_hbm, dx_hbm, vg_ref, dyk_hbm, dy_hbm, dr2_hbm, vgb_ref,
-                dbv, dr1v, ov, qkvv, wq, wo, dmix, full, dx, a_slots, a_sems, dy, acc, xh, vec,
-            ) = refs
-        else:
-            dpk_hbm, send_hbm, more_hbm, dx_hbm, vg_ref, *refs = refs
-            dbv, dr1v, ov, qkvv, wq, wo, dmix, full, dx, a_slots, a_sems = refs
-        section = scal[0]
-        is_own = section == (0 if low else 1)
-        db_copy = copies.load(db_hbm, dbv)
-        wo_copy = copies.pick(is_own, wo_own, wo_rcv, wo)
-        qkv_copy = copies.load(qkv_hbm, qkvv)
-        o_copy = copies.load(pack_hbm.at[:, o_at : o_at + D], ov)
-        for slot in range(2):
-            pltpu.make_async_copy(a_hbm.at[pl.ds(2 * slot, 2)], a_slots.at[slot], a_sems.at[slot]).start()
-        wq_copy = copies.pick(is_own, wq_own, wq_rcv, wq)
-        dr1_copy = copies.load(dr1_hbm, dr1v)
-        if high:
-            xh2_copy = copies.load(xh2_hbm, xh)
-            vec[...] = jnp.where(section == 0, vec_own[...], vec_rcv[...])
-            vgb_ref[...] = jnp.zeros((1, GRADS * D), F32)
-            rstd2 = as_column(rstd2_ref[...])
-        vg_ref[...] = vgin_ref[...]
-        db_copy.wait()
-        wo_copy.wait()
-        for tile in range(3):
-            cols = slice(tile * 256, (tile + 1) * 256)
-            dmix[:, cols] = dot(dbv[...], wo[cols, :], 1, 1).astype(BF)
-        qkv_copy.wait()
-        o_copy.wait()
-        attend_back(qkvv, a_hbm, a_slots, a_sems, ov, dmix, full, vg_ref)
-        for part in range(3):
-            target = slice(part * HALF, (part + 1) * HALF)
-            copies.store(full.at[:, lanes(part * D + section * HALF, HALF)], dpk_hbm.at[:, target])
-            start = part * D + (1 - section) * HALF
-            if part == 1:
-                cut = QKV_SEND - HALF
-                copies.store(full.at[:, lanes(start, cut)], send_hbm.at[:, HALF:])
-                copies.store(full.at[:, lanes(start + cut, HALF - cut)], more_hbm.at[:, : HALF - cut])
-            elif part == 0:
-                copies.store(full.at[:, lanes(start, HALF)], send_hbm.at[:, :HALF])
-            else:
-                copies.store(full.at[:, lanes(start, HALF)], more_hbm.at[:, QKV_MORE - HALF : QKV_MORE])
-        wq_copy.wait()
-        dr1_copy.wait()
-        if high:
+        copies.store(db.at[:, lanes(other * HALF, HALF)], send_b.at[:, half - SEND : half - SEND + HALF])
+        attn.heads(db, vg_ref if layer else None)
+        attn.store(
+            dpk_hbm,
+            [(0, 0, 128, send_b.at[:, half - SEND + HALF :]), (0, 128, HALF - 128, send_c.at[:, : HALF - 128])]
+            + [(part, 0, HALF, send_c.at[:, part * HALF - 128 : (part + 1) * HALF - 128]) for part in (1, 2)],
+        )
+        attn.wq_copy.wait()
+        if layer:
+            vec[...] = jnp.where(is_own, vec_rcv[...], vec_own[...])
             xh2_copy.wait()
         for rows in BLOCKS:
-            for tile in range(3):
-                cols = slice(tile * 256, (tile + 1) * 256)
-                value = dr1v[rows, cols] + dot(full[rows, :], wq[cols, :], 1, 1)
-                dx[rows, cols] = value.astype(BF)
-            if high:
-                norm_two_back(rows, dx[rows, :].astype(F32), xh[rows, :], rstd2[rows], vec, acc, dy, vgb_ref)
-        copies.store(dx, dx_hbm)
-        if high:
+            attn.to_input(rows, dr1)
+            if layer:
+                norm_two_back(rows, attn.dx[rows, :].astype(F32), xh[rows, :], rstd2[rows], vec, acc, dy, vglow_ref)
+        copies.store(attn.dx, dx_hbm)
+        if layer:
             copies.store(dy.at[:, lanes(section * HALF, HALF)], dyk_hbm)
-            copies.store(dy.at[:, lanes((1 - section) * HALF, HALF)], more_hbm.at[:, QKV_MORE:])
-            copies.store(dy, dy_hbm)
-            copies.store(acc, dr2_hbm)
+            copies.store(dy.at[:, lanes(other * HALF, HALF)], dys_hbm)
+            copies.store(dy, dylow_hbm)
+            copies.store(acc, dr2low_hbm)
         copies.finish()
 
-    specs = [SMEM, ANY, ANY, ANY, ANY, ANY, VMEM, ANY, ANY, ANY, ANY]
-    width = QKV_MORE + (HALF if high else 0)
-    outs = [
-        ((T, 3 * HALF), BF, ANY), ((T, QKV_SEND), BF, ANY), ((T, width), BF, ANY), ((T, D), BF, ANY),
-        ((1, GRADS * D), F32, VMEM),
-    ]
-    scratch = [
-        pltpu.VMEM((T, D), BF), pltpu.VMEM((T, D), F32), pltpu.VMEM((T, D), BF), pltpu.VMEM((T, 3 * D), BF),
-        pltpu.VMEM((D, 3 * D), BF), pltpu.VMEM((D, D), BF), pltpu.VMEM((T, D), BF), pltpu.VMEM((T, 3 * D), BF),
-        pltpu.VMEM((T, D), BF), pltpu.VMEM((2, 2, T, T), BF), DMA((2,)),
-    ]
-    if high:
-        specs += [ANY, VMEM, VMEM, VMEM]
-        outs += [((T, HALF), BF, ANY), ((T, D), BF, ANY), ((T, D), F32, ANY), ((1, GRADS * D), F32, VMEM)]
-        scratch += [
-            pltpu.VMEM((T, D), BF), pltpu.VMEM((T, D), F32), pltpu.VMEM((T, D), F32), pltpu.VMEM((1, PARAMS * D), F32)
-        ]
+    act, f_act, grad = ((T, D), BF, ANY), ((T, D), F32, ANY), ((1, GRADS * D), F32, VMEM)
+    send, half = ((T, SEND), BF, ANY), ((T, HALF), BF, ANY)
+    outs = [((T, FF // 2), BF, ANY), act, ((T, 3 * HALF), BF, ANY), send, send, send]
+    outs += [act, grad, half, half, act, f_act, grad] if layer else [act, grad]
     return kernel_call(
-        body, "low_attention_back" if low else "high_attention_back", specs,
-        (scal, db, dr1, pack, qkv, a, vgin, wq_own, wq_rcv, wo_own, wo_rcv) + tuple(below),
-        outs, scratch, 24, 17,
-    )
+        body, "layer_backward",
+        [SMEM, ANY, ANY, VMEM, ANY, ANY, VMEM, VMEM, VMEM] + [ANY] * 4 + [ANY] * 7 + ([ANY, VMEM] if layer else []),
+        (
+            scal, dr2, dy, vgin, gp, xh1, rstd1, vec_own, vec_rcv, wu_own, wu_rcv, wd_own, wd_rcv,
+            pack, qkv, a, wq_own, wq_rcv, wo_own, wo_rcv,
+        )
+        + tuple(below),
+        outs, mlp_back_scratch() + AttentionBack.scratch, 48, 25 * layer,
+    )
+
+
+def pitch(n):
+    return -(-(D // n) // 16) * 16
 
 
 class Pieces:
     def __init__(self, n, bits, my_bits, refs):
         self.n, self.bits, self.my_bits = n, bits, my_bits
+        self.height, self.pitch = D // n, pitch(n)
         self.refs = refs
 
-    def put(self, value, order, first, count, height, part):
+    def put(self, value, order, first, count, part):
+        height, top = self.height, part * self.pitch
         bit = self.bits[order]
         keep, send = self.refs[order]
         for kept in range(2):
@@ -765,11 +770,13 @@
                 for block in range(count):
                     place = (block // (2 * bit)) * bit + block % bit
                     target = keep if (block // bit) % 2 == kept else send
-                    target[first // 2 + place, part] = value[block * height : (block + 1) * height].astype(BF)
-
-
-def weight_grads(n, bits, scal, units, plans, name, us):
+                    rows = value[block * height : (block + 1) * height].astype(BF)
+                    target[first // 2 + place, top : top + height, :] = rows
+
+
+def weight_grads(n, bits, scal, units, plans, name, us, with_bias=False):
     height = D // n
+    tall_part = pitch(n)
     widths = {"down": (FF, HALF), "up": (D, FF // 2), "attn": (D, D, 3 * HALF, HALF)}
     specs, args, scratch, counts = [SMEM], [scal], [], []
     for unit in units:
@@ -780,10 +787,11 @@
         scratch += [pltpu.VMEM((2 * T, width), BF) for width in widths[unit[0]]]
     sizes = [sum(plan.count(order) for plan in plans) for order in range(2)]
     in_use = [order for order in range(2) if sizes[order]]
-    for plan in plans:
+    for place, plan in enumerate(plans):
         for order in in_use:
             if order in plan:
-                scratch += [pltpu.VMEM((n // 2, plan.count(order), height, HALF), BF)] * 2
+                extra = TILE if with_bias and order == 0 and place == len(plans) - 1 else 0
+                scratch += [pltpu.VMEM((n // 2, plan.count(order) * tall_part + extra, HALF), BF)] * 2
 
     def body(copies, scal, *refs):
         refs = list(refs)
@@ -843,7 +851,7 @@
                     cut = value.reshape(count, 4, height, HALF)
                     for part in range(4):
                         rows = cut[:, part].reshape(count * height, HALF)
-                        pieces.put(rows, plan[part], step * count, count, height, slots[part])
+                        pieces.put(rows, plan[part], step * count, count, slots[part])
                     return carry
 
                 lax.fori_loop(0, CHUNKS, chunk, 0)
@@ -859,19 +867,76 @@
                         value = dot(
                             left[:, half * HALF : (half + 1) * HALF], right[:, block * HALF : (block + 1) * HALF], 0, 0
                         )
-                        pieces.put(value, plan[part], half * (n // 2), n // 2, height, slots[part])
+                        pieces.put(value, plan[part], half * (n // 2), n // 2, slots[part])
+            if with_bias and unit[0] == "attn":
+                sums = [col_sum(dp[:, col * HALF : (col + 1) * HALF].astype(F32)) for col in range(3)]
+                tile = jnp.concatenate(sums + [jnp.zeros((TILE - 3, HALF), F32)], axis=0).astype(BF)
+                for stage_ref in stages[0]:
+                    for block in range(n // 2):
+                        stage_ref[block, stage_ref.shape[1] - TILE :, :] = tile
             for order, stage in stages.items():
-                size = plan.count(order)
+                size = stage[0].shape[1]
                 for stage_ref, out in zip(stage, outs[order]):
                     copies.store(stage_ref, out.at[:, filled[order] : filled[order] + size])
                 filled[order] += size
         copies.finish()
 
-    out = [((n // 2, sizes[order], height, HALF), BF, ANY) for order in in_use for _ in range(2)]
+    rows = [size * tall_part for size in sizes]
+    rows[0] += TILE if with_bias else 0
+    out = [((n // 2, rows[order], HALF), BF, ANY) for order in in_use for _ in range(2)]
     got = kernel_call(body, name, specs, tuple(args), out, scratch, 48, us)
     return [tuple(got[2 * place : 2 * place + 2]) for place in range(len(in_use))]
 
 
+def finish_pieces(scal, high, low_base, low_end):
+    def body(copies, scal, high_p, high_q, base_p, base_q, end_p, end_q, send, own):
+        is_first = scal[0] == 0
+        start = 0
+        for high, base, end in ((high_p, base_p, end_p), (high_q, base_q, end_q)):
+            size = high.shape[0]
+            low = base[:size, :] + end[:size, :].astype(F32)
+            rows = slice(start, start + size)
+            send[rows, :] = jnp.where(is_first, high[...], low)
+            own[rows, :] = jnp.where(is_first, low, high[...])
+            start += size
+        size = high_p.shape[0]
+        tile = base_p[size:, :] + end_p[size:, :].astype(F32)
+        send[start:, :] = tile
+        own[start:, :] = tile
+
+    rows = high[0].shape[0] + low_base[0].shape[0]
+    out = ((rows, HALF), F32, VMEM)
+    return kernel_call(
+        body, "finish_pieces", [SMEM] + [VMEM] * 6, (scal, *high, *low_base, *low_end), [out, out], [], 1, 2
+    )
+
+
+def place_pieces(small, tall, scal, own, other):
+    def body(copies, scal, own, other, up, qkv, out, rows):
+        is_first = scal[0] == 0
+        for side in range(2):
+
+            def part(number, size):
+                start = number * tall
+                mine, theirs = own[start : start + size, :], other[start : start + size, :]
+                return jnp.where(is_first, mine, theirs) if side == 0 else jnp.where(is_first, theirs, mine)
+
+            for col, number in enumerate((0, 1, 4, 5)):
+                start = side * 4 * HALF + col * HALF
+                up[:, start : start + HALF] = part(number, small)
+            for col, number in enumerate((2, 3, 6)):
+                start = col * D + side * HALF
+                qkv[:, start : start + HALF] = part(number, small)
+            cols = slice(side * HALF, (side + 1) * HALF)
+            out[:, cols] = part(7, small)
+            rows[:, cols] = part(8, 8)
+
+    return kernel_call(
+        body, "place_pieces", [SMEM, VMEM, VMEM], (scal, own, other),
+        [((small, width), F32, VMEM) for width in (FF, 3 * D, D)] + [((8, D), F32, VMEM)], [], 1, 2,
+    )
+
+
 SWAP = [(0, 1), (1, 0)]
 
 
@@ -887,8 +952,12 @@
     return lax.optimization_barrier((value,) + others)[0]
 
 
+def isolated(value):
+    return lax.optimization_barrier(value)
+
+
 class Halving:
-    def __init__(self, n, index, split, bits):
+    def __init__(self, n, index, split, bits, *others):
         self.n, self.index, self.bits = n, index, list(bits)
         self.dims = [1 << place for place in reversed(range(n.bit_length() - 1))]
         self.tail = split[0].shape[1:]
@@ -896,7 +965,7 @@
         self.dims.remove(bit)
         self.shape = (2,) * len(self.dims) + self.tail
         self.parts = [split[0].reshape(self.shape)]
-        self.pending = across(split[1], bit, n).reshape(self.shape)
+        self.pending = across(after(split[1], *others) if others else split[1], bit, n).reshape(self.shape)
 
     def collect(self, *others):
         self.parts.append(after(self.pending, *others) if others else self.pending)
@@ -912,32 +981,29 @@
         self.parts = [lax.dynamic_index_in_dim(part, mine, place, keepdims=False) for part in self.parts]
         return send, bit
 
-    def step(self, *others):
-        self.collect(*others)
-        send, bit = self.outgoing()
-        self.pending = across(send, bit, self.n)
-        return send
+    def base(self):
+        return isolated(sum(part.astype(F32) for part in self.parts))
 
     def total(self, *others):
         self.collect(*others)
         return sum(part.astype(F32) for part in self.parts)
 
 
-def step_together(chains, *others):
-    if len(chains) == 1:
-        return chains[0].step(*others)
+def step_together(chains, *others, gate=()):
     sends = []
     for chain in chains:
         chain.collect(*others)
         send, bit = chain.outgoing()
         sends.append(send)
-    flat = jnp.concatenate([send.reshape((-1,) + send.shape[-2:]) for send in sends], axis=0)
-    received = across(flat, bit, chains[0].n)
+    joined = jnp.concatenate(sends, axis=-2) if len(sends) > 1 else sends[0]
+    flat = joined.reshape(-1, joined.shape[-1])
+    if gate:
+        flat = after(flat, *gate)
+    received = across(flat, bit, chains[0].n).reshape(joined.shape)
     start = 0
     for chain, send in zip(chains, sends):
-        size = flat.shape[0] // len(chains)
-        chain.pending = received[start : start + size].reshape(send.shape)
-        start += size
+        chain.pending = lax.slice_in_dim(received, start, start + send.shape[-2], axis=received.ndim - 2)
+        start += send.shape[-2]
     return flat
 
 
@@ -980,11 +1046,11 @@
     dy_r = swap(dys)
     h2_r = swap(h2)
 
-    def chain(split, which):
-        return Halving(n, index, split, orders[which])
-
-    def chains(grads):
-        return [chain(split, which) for which, split in enumerate(grads)]
+    def chain(split, which, *others):
+        return Halving(n, index, split, orders[which], *others)
+
+    def chains(grads, *others):
+        return [chain(split, which, *others) for which, split in enumerate(grads)]
 
     def step_each(pair, *others):
         sent = step_together([pair[0]], *others)
@@ -993,124 +1059,109 @@
     def col(array, start, width):
         return [(array, start, width)]
 
-    def parts(first, second):
-        rest = FF // 2 - SEND
-        return [(first, 0, SEND), (second, 0, rest)], [(second, rest, HALF)]
-
-    def qkv_parts(first, second):
-        return [(first, 0, QKV_SEND), (second, 0, QKV_MORE)], [(second, QKV_MORE, HALF)]
-
     split, first_only, second_only = (0, 0, 1, 1), (0, 0, 0, 0), (1, 1, 1, 1)
+    rest = FF // 2 - SEND
 
     grads = weight_grads(
         n, bits, scal, [("down", col(g2, 0, FF), col(g2_r, 0, FF), col(dyk, 0, HALF), col(dy_r, 0, HALF))],
         [first_only], "high_down_grads", 7,
     )
     down_high = chain(grads[0], 0)
-    duk, send, more, dr1, db, vg_high = mlp_backward(
+    (
+        duk, db_high, dpk, send_a, send_b, send_c, d_top, vg_high, dys, dyk, dy, dr2, vg_low
+    ) = layer_backward(
         1, scal, after(dr2, grads[0][1], h2_r, pack2_r), dy, vg_high, gp2, xh1_high, rstd1_high, vec, vec_r,
-        wu, wu_r, wd, wd_r,
-    )
-    du_r, db_high_r = parts(swap(send), swap(more))
+        wu, wu_r, wd, wd_r, pack2, FF + D, qkv2, a2, wq, wq_r, wo, wo_r, (xh2_low, rstd2_low),
+    )
+    a_r, b_r, c_r, dy_r = swap(send_a), swap(send_b), swap(send_c), swap(dys)
+    sent = step_together([down_high], db_high)
+    pack1_r = swap(after(pack1, sent))
+    z_r = swap(after(z, sent))
     n_at = FF + 2 * D
-    grads = weight_grads(
-        n, bits, scal, [("up", col(pack2, n_at, D), col(pack2_r, n_at, D), col(duk, 0, FF // 2), du_r)],
-        [second_only], "high_up_grads", 0,
-    )
-    sent = step_together([down_high], grads[0][1])
-    pack1_r = swap(after(pack1, sent))
-    up_high = chain(grads[0], 1)
-    db_high = db
-    dpk, send, more, d_top, vg_high, dyk, dy, dr2, vg_low = attention_back(
-        False, scal, after(db, sent, grads[0][1]), dr1, pack2, FF + D, qkv2, a2, vg_high, wq, wq_r, wo, wo_r,
-        (xh2_low, rstd2_low, vec, vec_r),
-    )
-    dp_r, dy_r = qkv_parts(swap(send), swap(more))
-    d_top_r = swap(d_top)
-    sent = step_together([down_high], dyk)
-
-    duk, send, more, dr1, db, vg_low = mlp_backward(
-        0, scal, after(dr2, sent, pack1_r), dy, vg_low, gp1, xh1_low, rstd1_low, vec, vec_r, wu, wu_r, wd, wd_r
-    )
-    send_r, more_r = swap(send), swap(more)
-    du_r, db_low_r = parts(send_r, more_r)
-    sent = step_together([up_high], db)
-    sent = step_together([down_high], sent)
-    grads = weight_grads(
-        n, bits, scal,
-        [(
-            "attn", col(pack2, FF, D), col(pack2_r, FF, D), col(pack2, FF + D, D), col(pack2_r, FF + D, D),
-            col(after(dpk, sent, d_top_r), 0, 3 * HALF), dp_r, col(db_high, "half", HALF), db_high_r,
-        )],
-        [split], "high_attn_grads", 9,
-    )
-    attn_high = chains(grads)
-    sent = step_together([up_high], grads[0][1])
-    z_r = swap(after(z, sent))
     grads = weight_grads(
         n, bits, scal,
         [
             (
-                "down", col(pack2, 0, FF), col(pack2_r, 0, FF), col(after(dyk, sent, grads[1][1]), 0, HALF),
-                dy_r,
+                "up", col(pack2, n_at, D), col(pack2_r, n_at, D), col(after(duk, sent), 0, FF // 2),
+                [(a_r, 0, SEND), (b_r, 0, rest)],
             ),
-            ("up", col(pack1, D, D), col(pack1_r, D, D), col(duk, 0, FF // 2), du_r),
+            (
+                "attn", col(pack2, FF, D), col(pack2_r, FF, D), col(pack2, FF + D, D), col(pack2_r, FF + D, D),
+                col(dpk, 0, 3 * HALF), [(b_r, rest + HALF, 128), (c_r, 0, SEND)],
+                col(db_high, "half", HALF), col(b_r, rest, HALF),
+            ),
+            ("down", col(pack2, 0, FF), col(pack2_r, 0, FF), col(dyk, 0, HALF), col(dy_r, 0, HALF)),
         ],
-        [first_only, second_only], "low_mlp_grads", 13,
-    )
-    mid = chains(grads)
-    sent = step_each(attn_high, grads[0][1], z_r)
-    sent = step_together([up_high], sent)
-    dpk, send, more, d_low, vg_low = attention_back(
-        True, scal, after(db, sent, grads[1][1]), dr1, pack1, 0, qkv1, a1, vg_low, wq, wq_r, wo, wo_r
-    )
-    dp_r, _ = qkv_parts(swap(send), swap(more))
-    d_low_r = swap(d_low)
-    sent = step_together(attn_high, dpk)
+        [split, split, split], "high_grads", 0,
+    )
+    high = chains(grads)
+    sent = step_together([down_high], grads[0][1])
+    d_top_r = swap(after(d_top, sent))
+
+    duk, db, dpk, send_a, send_b, send_c, d_low, vg_low = layer_backward(
+        0, scal, after(dr2, sent, grads[0][1], grads[1][1], pack1_r, z_r), dy, vg_low, gp1, xh1_low, rstd1_low, vec, vec_r,
+        wu, wu_r, wd, wd_r, pack1, 0, qkv1, a1, wq, wq_r, wo, wo_r,
+    )
+    vg = jnp.concatenate([vg_low, vg_high], axis=1)
+    vg = vg + swap(vg)
+    a_r, b_r, c_r = swap(send_a), swap(send_b), swap(send_c)
+    sent = step_each(high, db, d_top_r)
+    vg_next = across(after(vg, sent), 4, n)
+    sent = step_together([down_high], sent)
     grads = weight_grads(
         n, bits, scal,
-        [(
-            "attn", col(tokens, 0, D), None, col(pack1, 0, D), col(pack1_r, 0, D), col(after(dpk, sent), 0, 3 * HALF),
-            dp_r, col(db, "half", HALF), db_low_r,
-        )],
-        [split], "low_attn_grads", 0,
-    )
+        [
+            (
+                "up", col(pack1, D, D), col(pack1_r, D, D), col(after(duk, sent), 0, FF // 2),
+                [(a_r, 0, SEND), (b_r, 0, rest)],
+            ),
+            (
+                "attn", col(tokens, 0, D), None, col(pack1, 0, D), col(pack1_r, 0, D),
+                col(dpk, 0, 3 * HALF), [(b_r, rest + HALF, 128), (c_r, 0, SEND)],
+                col(db, "half", HALF), col(b_r, rest, HALF),
+            ),
+        ],
+        [split, split], "low_grads", 0, True,
+    )
+
     last = chains(grads)
-
-    vg = after(jnp.concatenate([vg_low, vg_high], axis=1), grads[0][1])
-    vg = vg + swap(vg)
-    vg_next = across(vg, orders[0][0], n)
-    sent = step_each(mid, grads[1][1])
-    sent = step_together(attn_high, sent)
+    vg = vg + after(vg_next, grads[0][1])
+    vg_next = across(vg, 8, n)
+    vg = vg + vg_next
+    sent = step_together(high, grads[0][1], grads[1][1], vg)
+    vg_next = across(vg, 1, n)
+    d_low_r = swap(after(d_low, sent))
+    sent = step_together(high, sent)
+    sent = step_each(last, sent)
     vg = vg + after(vg_next, sent)
-    vg_next = across(vg, orders[0][1], n)
-    sent = step_each(last, sent)
-    for place in range(2, len(orders[0])):
-        sent = step_together(mid, sent)
-        vg = vg + after(vg_next, sent)
-        vg_next = across(vg, orders[0][place], n)
-        sent = step_together(last, sent)
-        if place >= 4:
-            for group in ([down_high], [up_high], attn_high):
-                sent = step_together(group, sent)
-    vg = vg + vg_next
-    mid_sums = [part.total() for part in mid]
-    attn_sums = [part.total() for part in attn_high]
-    last_sums = [part.total() for part in last]
+    vg_next = across(vg, 2, n)
+    sent = step_together(last, sent, d_low_r, *[part.pending for part in high])
+    vg = vg + after(vg_next, sent)
+    sent = step_together(last, sent)
+    for bit in orders[0][4:]:
+        vg = vg + across(vg, bit, n)
+        for group in ([down_high], high, last):
+            sent = step_together(group, sent)
+
+    small = D // n
+    tall = pitch(n)
+
+    def rows_of(total, start, count):
+        return total.reshape(-1, HALF)[start * tall : (start + count) * tall]
+
+    high_p, high_q = [part.total() for part in high]
+    down_high = rows_of(down_high.total(), 0, 4)
+    down_low = jnp.concatenate([rows_of(high_p, 4, 2), rows_of(high_q, 4, 2)], axis=0)
+    high = [rows_of(high_p, 0, 4), rows_of(high_q, 0, 4)]
+    low_base = [part.base().reshape(-1, HALF) for part in last]
+    low_end = [part.pending.reshape(-1, HALF) for part in last]
 
     def column(array, start, width):
         return array[:, start : start + width]
 
     h1, h1_r = column(pack2, FF, D), column(pack2_r, FF, D)
 
-    def whole_unit(first, second):
-        return jnp.concatenate([first, second], axis=0)
-
-    low = mid_sums + [whole_unit(*last_sums)]
-    high = [down_high.total(), up_high.total(), whole_unit(*attn_sums)]
-
     mine = jnp.where(is_first, vg[:, : GRADS * D], vg[:, GRADS * D :])
-    small = D // n
 
     def share(place, count=1):
         width = count * small
@@ -1119,15 +1170,17 @@
     head_share = lax.dynamic_slice(vg, (0, (GRADS + HD) * D + index * small), (1, small)).reshape(-1, 2)
     head_out = jnp.where(is_first, head_share[:, 0], head_share[:, 1])[:, None]
 
-    own = [jnp.where(is_first, a, b) for a, b in zip(low, high)]
-    other = [swap(jnp.where(is_first, b, a)) for a, b in zip(low, high)]
-    left = [jnp.where(is_first, a, b) for a, b in zip(own, other)]
-    right = [jnp.where(is_first, b, a) for a, b in zip(own, other)]
-    down, up, attn = [jnp.stack([a, b]) for a, b in zip(left, right)]
-    grad_down = down.transpose(1, 2, 0, 3).reshape(1, FF // n, D)
-    grad_up = up.transpose(2, 0, 1, 3).reshape(1, small, FF)
-    grad_qkv = attn[:, :3].transpose(2, 1, 0, 3).reshape(1, small, 3 * D)
-    grad_out = attn[:, 3].transpose(1, 0, 2).reshape(1, small, D)
+    def halves(low, high):
+        own = jnp.where(is_first, low, high)
+        other = swap(jnp.where(is_first, high, low))
+        return jnp.where(is_first, own, other), jnp.where(is_first, other, own)
+
+    left, right = [half.reshape(4, tall, HALF)[:, :small].reshape(4 * small, HALF) for half in halves(down_low, down_high)]
+    grad_down = jnp.concatenate([left, right], axis=1)[None]
+    send, own = finish_pieces(scal, high, low_base, low_end)
+    grad_up, grad_qkv, grad_out, rows = place_pieces(small, tall, scal, own, swap(send))
+    low_qv = lax.dynamic_slice(jnp.concatenate([rows[0], rows[2]]), (index * 2 * small,), (2 * small,))[None]
+    grad_qv = jnp.where(is_first, low_qv, share(QB, 2))
 
     def both(early, late):
         (own_low, other_low), (own_high, other_high) = early, late
@@ -1146,13 +1199,13 @@
         hidden,
         term_out,
         input_out,
-        grad_qkv,
-        share(QB, 2),
-        grad_out,
+        grad_qkv[None],
+        grad_qv,
+        grad_out[None],
         share(OB),
         share(G1),
         share(S1),
-        grad_up,
+        grad_up[None],
         share(UB, 4),
         grad_down,
         share(DB),

time: 359 us -> 330 us (0.919)
  starting transfers between devices: 40.3 us -> 28 us
  Pallas kernels: 183 us -> 171 us
  other arithmetic: 40 us -> 30.9 us
    pallas_call x13 -> x11, Pallas kernels: 183 us -> 171 us  [kernel_call(): pl.pallas_call(wrapped, in_specs=specs, out_specs=[spec for _, _, spec in...]
    ppermute x30 -> x20, starting transfers between devices: 34.1 us -> 22.8 us  [across(): return lax.ppermute(array, 'dp', [(i, i ^ bit) for i in range(n)])]
    unnamed x78 -> x73, local copies, waits for them, and re-layouts: 5.13 us -> 11.3 us
    slice x3 -> x10, local copies, waits for them, and re-layouts: 0.12 us -> 4.97 us  [the longest x5 2.65 us: step_together(): lax.slice_in_dim(received, start, start + send.shape[-2], axis=received.n...]
    reshape x4 -> x0, local copies, waits for them, and re-layouts: 4.24 us -> none  [the longest x1 1.29 us: per_device(): grad_down = down.transpose(1, 2, 0, 3).reshape(1, FF // n, D)]
    ppermute x30 -> x20, waiting for transfers between devices: 62.9 us -> 66.5 us  [across(): return lax.ppermute(array, 'dp', [(i, i ^ bit) for i in range(n)])]
    convert_element_type x24 -> x14, other arithmetic: 19.8 us -> 16.6 us  [outgoing(): send = sum((lax.dynamic_index_in_dim(part, 1 - mine, place, keepdims=Fals...]
    ppermute x25 -> x23, waiting for transfers between devices: 12.5 us -> 10.5 us  [swap(): return lax.ppermute(array, 'section', SWAP)]
  transfers between devices with their start and end apart: 55 -> 43, of which waited for: 15 -> 10; matrix products, arithmetic and copies ran while one was open for 13% -> 11% of each run, Pallas kernels for 42% -> 41%
where the time goes in v3:
time: 330 us; the launch traced here: 327 us
  Pallas kernels  171 us (52%)
  waiting for transfers between devices  77 us (23%)
  other arithmetic  30.9 us (9%)
  starting transfers between devices  28 us (8%)
  local copies, waits for them, and re-layouts  18.5 us (6%)
    pallas_call x11, Pallas kernels, kernel_call(): pl.pallas_call(wrapped, in_specs=specs, out_specs=[spec for _, _, spec in...  171 us
    ppermute x20, waiting for transfers between devices, across(): return lax.ppermute(array, 'dp', [(i, i ^ bit) for i in range(n)])  66.5 us
    ppermute x20, starting transfers between devices, across(): return lax.ppermute(array, 'dp', [(i, i ^ bit) for i in range(n)])  22.8 us
    convert_element_type x14, other arithmetic, outgoing(): send = sum((lax.dynamic_index_in_dim(part, 1 - mine, place, keepdims=Fals...  16.6 us
    unnamed x73, local copies, waits for them, and re-layouts  11.3 us
    ppermute x23, waiting for transfers between devices, swap(): return lax.ppermute(array, 'section', SWAP)  10.5 us
  transfers between devices with their start and end apart: 43, of which 10 were waited for; matrix products, arithmetic and copies ran while one was open for 11% of the time, Pallas kernels for 41%

profile of v3, /device:TPU:0, one launch (start us, length us, event | category | flops | bytes accessed | tf_op | source)
XLA Modules:
  0.0 326.8 jit_solution(3171273539555581426)
XLA Ops:
  3.2 5.8 %collective-permute-done.refs_4_.refs_5_.refs_8_ = f32[1,9216]{1,0:T(1,128)S(1)} collective-permute-done((f32[1,9216]{1,0:T(1,128)}, f32[1,9216]{1,0:T(1,128)S(1)}, u32[]{:S(2)}, u32[]{:S(2)}) %collective-permute-start) | collective-permute-done | bytes 36896 | tf_op jit(solution)/shard_map/ppermute | solution.py:944
  11.8 17.3 %first_attention.1 = (bf16[512,2304]{1,0:T(8,128)(2,1)}, bf16[12,512,512]{2,1,0:T(8,128)(2,1)}, f32[512,768]{1,0:T(8,128)}, bf16[512,1536]{1,0:T(8,128)(2,1)}, f32[1,512]{1,0:T(1,128)}) custom-call(s32[3]{0:T(128)} %pad_add_fusion.refs_0_, bf16[1024,768]{1,0:T(8,128)(2,1)} %refs_6_.3, s32[1,1024]{1,0:T(1,128)} %bitcast.223, ...), custom_call_target="tpu_custom_call" | custom-call | flops 15000000512 | bytes 30001000 | tf_op jit(solution)/shard_map/first_attention/pallas_call | solution.py:118
  29.1 34.9 %middle.1 = (bf16[512,5376]{1,0:T(8,128)(2,1)}, bf16[512,3072]{1,0:T(8,128)(2,1)}, f32[512,768]{1,0:T(8,128)}, bf16[512,2304]{1,0:T(8,128)(2,1)}, bf16[12,512,51...) custom-call(s32[3]{0:T(128)} %pad_add_fusion.refs_0_, ...), custom_call_target="tpu_custom_call" | custom-call | flops 30000001024 | bytes 60001000 | tf_op jit(solution)/shard_map/middle/pallas_call | solution.py:118
  65.2 10.7 %top.1 = (bf16[512,768]{1,0:T(8,128)(2,1)}, f32[512,768]{1,0:T(8,128)}, bf16[512,384]{1,0:T(8,128)(2,1)}, bf16[512,384]{1,0:T(8,128)(2,1)}, bf16[512,768]{1,0:T(...) custom-call(s32[3]{0:T(128)} %pad_add_fusion.refs_0_, bf16[512,3072]{1,0:T(8,128)(2,1)} %get-tuple-element.111.refs_1_, ...), custom_call_target="tpu_custom_call" | custom-call | flops 10000001024 | bytes 20001000 | tf_op jit(solution)/shard_map/top/pallas_call | solution.py:118
  76.5 1.9 collective-permute-done.8.refs_4_
  79.1 8.6 %high_down_grads.1 = (bf16[8,192,384]{2,1,0:T(8,128)(2,1)}, bf16[8,192,384]{2,1,0:T(8,128)(2,1)}) custom-call(s32[3]{0:T(128)} %pad_add_fusion.refs_0_, bf16[512,3072]{1,0:T(8,128)(2,1)} %get-tuple-element.111.refs_1_, bf16[512,3072]{1,0:T(8,128)(2,1)} %collective-permute-done.7.refs_2_, bf16[512,384]{1,0:T(8,128)(2,1)} %get-tuple-element.115.refs_3_, ...), custom_call_target="tpu_custom_call" | custom-call | flops 7000001024 | bytes 14001000 | tf_op jit(solution)/shard_map/high_down_grads/pallas_call | solution.py:118
  87.7 2.9 collective-permute-start.9
  91.5 29.6 %layer_backward.2 = (bf16[512,1536]{1,0:T(8,128)(2,1)}, bf16[512,768]{1,0:T(8,128)(2,1)}, bf16[512,1152]{1,0:T(8,128)(2,1)}, bf16[512,1024]{1,0:T(8,128)(2,1)}, ...) custom-call(s32[3]{0:T(128)} %pad_add_fusion.refs_0_, ...), custom_call_target="tpu_custom_call" | custom-call | flops 25000001536 | bytes 50001000 | tf_op jit(solution)/shard_map/layer_backward/pallas_call | solution.py:118
  122.7 2.2 add_convert_fusion.4
  125.5 2.8 collective-permute-done.15.refs_18_
  132.1 19.8 %high_grads.1 = (bf16[8,288,384]{2,1,0:T(8,128)(2,1)}, bf16[8,288,384]{2,1,0:T(8,128)(2,1)}, bf16[8,288,384]{2,1,0:T(8,128)(2,1)}, bf16[8,288,384]{2,1,0:T(8,128)(2,1)}) custom-call(s32[3]{0:T(128)} %pad_add_fusion.refs_0_, bf16[512,5376]{1,0:T(8,128)(2,1)} %get-tuple-element.110.refs_13_.refs_1_.refs_6_.refs_8_.refs_15_, ...), custom_call_target="tpu_custom_call" | custom-call | flops 1000 | bytes 1000 | tf_op jit(solution)/shard_map/high_grads/pallas_call | solution.py:118
  154.7 2.0 collective-permute-start.20
  156.7 28.0 %layer_backward.3 = (bf16[512,1536]{1,0:T(8,128)(2,1)}, bf16[512,768]{1,0:T(8,128)(2,1)}, bf16[512,1152]{1,0:T(8,128)(2,1)}, bf16[512,1024]{1,0:T(8,128)(2,1)}, ...) custom-call(s32[3]{0:T(128)} %pad_add_fusion.refs_0_, ...), custom_call_target="tpu_custom_call" | custom-call | flops 1000 | bytes 1000 | tf_op jit(solution)/shard_map/layer_backward/pallas_call | solution.py:118
  186.2 6.5 %collective-permute-done.18 = bf16[8,288,384]{2,1,0:T(8,128)(2,1)} collective-permute-done((bf16[8,288,384]{2,1,0:T(8,128)(2,1)}, bf16[8,288,384]{2,1,0:T(8,128)(2,1)}, u32[]{:S(2)}, u32[]{:S(2)}) %collective-permute-start.18) | collective-permute-done | bytes 1769504 | tf_op jit(solution)/shard_map/ppermute | solution.py:948
  192.7 2.4 add_convert_fusion.1
  196.1 2.3 add_convert_fusion
  201.5 1.6 collective-permute-start.26
  203.1 1.8 fusion.12
  205.9 15.7 %low_grads.1 = (bf16[8,208,384]{2,1,0:T(8,128)(2,1)}, bf16[8,208,384]{2,1,0:T(8,128)(2,1)}, bf16[8,192,384]{2,1,0:T(8,128)(2,1)}, bf16[8,192,384]{2,1,0:T(8,128)(2,1)}) custom-call(s32[3]{0:T(128)} %pad_add_fusion.refs_0_, bf16[512,1536]{1,0:T(8,128)(2,1)} %get-tuple-element.144.refs_1_.refs_13_.refs_7_, ...), custom_call_target="tpu_custom_call" | custom-call | flops 1000 | bytes 1000 | tf_op jit(solution)/shard_map/low_grads/pallas_call | solution.py:118
  221.7 2.7 collective-permute-start.27
  225.6 2.6 collective-permute-done.27
  228.3 2.2 fusion
  233.4 1.6 collective-permute-start.34
  236.1 16.8 %collective-permute-done.30 = bf16[1152,384]{1,0:T(8,128)(2,1)} collective-permute-done((bf16[1152,384]{1,0:T(8,128)(2,1)}, bf16[1152,384]{1,0:T(8,128)(2,1)}, u32[]{:S(2)}, u32[]{:S(2)}) %collective-permute-start.30) | collective-permute-done | bytes 884768 | tf_op jit(solution)/shard_map/ppermute | solution.py:948
  257.3 5.2 %collective-permute-done.32 = bf16[8,208,384]{2,1,0:T(8,128)(2,1)S(1)} collective-permute-done((bf16[8,208,384]{2,1,0:T(8,128)(2,1)}, bf16[8,208,384]{2,1,0:T(8,128)(2,1)S(1)}, u32[]{:S(2)}, u32[]{:S(2)}) %collective-permute-start.32) | collective-permute-done | bytes 1277984 | tf_op jit(solution)/shard_map/ppermute | solution.py:948
  263.8 1.6 collective-permute-start.41
  268.3 12.9 %collective-permute-done.31 = bf16[576,384]{1,0:T(8,128)(2,1)S(1)} collective-permute-done((bf16[576,384]{1,0:T(8,128)(2,1)S(1)}, bf16[576,384]{1,0:T(8,128)(2,1)S(1)}, u32[]{:S(2)}, u32[]{:S(2)}) %collective-permute-start.31) | collective-permute-done | bytes 442400 | tf_op jit(solution)/shard_map/ppermute | solution.py:948
  285.1 1.6 fusion.5
  289.5 7.9 %collective-permute-done.36 = bf16[800,384]{1,0:T(8,128)(2,1)S(1)} collective-permute-done((bf16[800,384]{1,0:T(8,128)(2,1)S(1)}, bf16[800,384]{1,0:T(8,128)(2,1)S(1)}, u32[]{:S(2)}, u32[]{:S(2)}) %collective-permute-start.36) | collective-permute-done | bytes 614432 | tf_op jit(solution)/shard_map/ppermute | solution.py:948
  299.6 14.5 %collective-permute-done.37 = bf16[400,384]{1,0:T(8,128)(2,1)S(1)} collective-permute-done((bf16[400,384]{1,0:T(8,128)(2,1)S(1)}, bf16[400,384]{1,0:T(8,128)(2,1)S(1)}, u32[]{:S(2)}, u32[]{:S(2)}) %collective-permute-start.37) | collective-permute-done | bytes 307232 | tf_op jit(solution)/shard_map/ppermute | solution.py:948
  315.5 2.6 finish_pieces.1
  322.8 2.3 place_pieces.1
  (198 shorter events, 54.1 us)
Async XLA Ops:
  10.0 19.1 %collective-permute-start.3 = (bf16[768,3072]{1,0:T(8,128)(2,1)}, bf16[768,3072]{1,0:T(8,128)(2,1)}, u32[]{:S(2)}, u32[]{:S(2)}) collective-permute-start(bf16[768,3072]{1,0:T(8,128)(2,1)} %bitcast.158), channel_id=1, source_target_pairs={{0,16},{16,0},{1,17},{17,1},{2,18},{18,2},{3,19},{19,3},{4,20},{20... | collective-permute-start | bytes 14155784 | tf_op jit(solution)/shard_map/ppermute | solution.py:944
  10.4 18.7 %collective-permute-start.4 = (bf16[3072,768]{1,0:T(8,128)(2,1)}, bf16[3072,768]{1,0:T(8,128)(2,1)}, u32[]{:S(2)}, u32[]{:S(2)}) collective-permute-start(bf16[3072,768]{1,0:T(8,128)(2,1)} %bitcast.162), channel_id=1, source_target_pairs={{0,16},{16,0},{1,17},{17,1},{2,18},{18,2},{3,19},{19,3},{4,20},{20... | collective-permute-start | bytes 14155784 | tf_op jit(solution)/shard_map/ppermute | solution.py:944
  64.0 26.6 %collective-permute-start.6 = (bf16[512,5376]{1,0:T(8,128)(2,1)}, bf16[512,5376]{1,0:T(8,128)(2,1)}, u32[]{:S(2)}, u32[]{:S(2)}) collective-permute-start(bf16[512,5376]{1,0:T(8,128)(2,1)} %get-tuple-element.110.refs_13_.refs_1_.refs_6_.refs_8_.refs_15_), channel_id=1, source_target_pairs={{0,16},{16,0},{1,17},{17,1},{2,18},{18,2},{3,19},{19,3},{4,20},{20... | collective-permute-start | bytes 16515080 | tf_op jit(solution)/shard_map/ppermute | solution.py:944
  64.4 13.9 %collective-permute-start.7 = (bf16[512,3072]{1,0:T(8,128)(2,1)}, bf16[512,3072]{1,0:T(8,128)(2,1)}, u32[]{:S(2)}, u32[]{:S(2)}) collective-permute-start(bf16[512,3072]{1,0:T(8,128)(2,1)} %get-tuple-element.111.refs_1_), channel_id=1, source_target_pairs={{0,16},{16,0},{1,17},{17,1},{2,18},{18,2},{3,19},{19,3},{4,20},{20... | collective-permute-start | bytes 9437192 | tf_op jit(solution)/shard_map/ppermute | solution.py:944
  76.4 14.3 %collective-permute-start.5 = (bf16[512,768]{1,0:T(8,128)(2,1)}, bf16[512,768]{1,0:T(8,128)(2,1)S(1)}, u32[]{:S(2)}, u32[]{:S(2)}) collective-permute-start(bf16[512,768]{1,0:T(8,128)(2,1)} %get-tuple-element.113), channel_id=1, source_target_pairs={{0,16},{16,0},{1,17},{17,1},{2,18},{18,2},{3,19},{19,3},{4,20},{20... | collective-permute-start | bytes 2359304 | tf_op jit(solution)/shard_map/ppermute | solution.py:944
  87.7 33.5 %collective-permute-start.9 = (bf16[8,192,384]{2,1,0:T(8,128)(2,1)}, bf16[8,192,384]{2,1,0:T(8,128)(2,1)S(1)}, u32[]{:S(2)}, u32[]{:S(2)}) collective-permute-start(bf16[8,192,384]{2,1,0:T(8,128)(2,1)} %get-tuple-element.118), channel_id=1, source_target_pairs={{0,1},{1,0},{2,3},{3,2},{4,5},{5,4},{6,7},{7,6},{8,9},{9,8},{10,11... | collective-permute-start | bytes 3538952 | tf_op jit(solution)/shard_map/ppermute | solution.py:948
  121.2 8.6 %collective-permute-start.12 = (bf16[512,1024]{1,0:T(8,128)(2,1)}, bf16[512,1024]{1,0:T(8,128)(2,1)S(1)}, u32[]{:S(2)}, u32[]{:S(2)}) collective-permute-start(bf16[512,1024]{1,0:T(8,128)(2,1)} %get-tuple-element.135), channel_id=1, source_target_pairs={{0,16},{16,0},{1,17},{17,1},{2,18},{18,2},{3,19},{19,3},{4,20},{20... | collective-permute-start | bytes 3145736 | tf_op jit(solution)/shard_map/ppermute | solution.py:944
  122.2 8.5 %collective-permute-start.14 = (bf16[512,1024]{1,0:T(8,128)(2,1)}, bf16[512,1024]{1,0:T(8,128)(2,1)S(1)}, u32[]{:S(2)}, u32[]{:S(2)}) collective-permute-start(bf16[512,1024]{1,0:T(8,128)(2,1)} %get-tuple-element.138), channel_id=1, source_target_pairs={{0,16},{16,0},{1,17},{17,1},{2,18},{18,2},{3,19},{19,3},{4,20},{20... | collective-permute-start | bytes 3145736 | tf_op jit(solution)/shard_map/ppermute | solution.py:944
  124.9 31.7 %collective-permute-start.16 = (bf16[512,1536]{1,0:T(8,128)(2,1)S(1)}, bf16[512,1536]{1,0:T(8,128)(2,1)}, u32[]{:S(2)}, u32[]{:S(2)}) collective-permute-start(bf16[512,1536]{1,0:T(8,128)(2,1)S(1)} %copy-done), channel_id=1, source_target_pairs={{0,16},{16,0},{1,17},{17,1},{2,18},{18,2},{3,19},{19,3},{4,20},{20... | collective-permute-start | bytes 4718600 | tf_op jit(solution)/shard_map/ppermute | solution.py:944
  128.3 25.3 %collective-permute-start.11 = (bf16[768,384]{1,0:T(8,128)(2,1)}, bf16[768,384]{1,0:T(8,128)(2,1)S(1)}, u32[]{:S(2)}, u32[]{:S(2)}) collective-permute-start(bf16[768,384]{1,0:T(8,128)(2,1)} %bitcast.12), channel_id=1, source_target_pairs={{0,2},{1,3},{2,0},{3,1},{4,6},{5,7},{6,4},{7,5},{8,10},{9,11},{10,... | collective-permute-start | bytes 1769480 | tf_op jit(solution)/shard_map/ppermute | solution.py:948
  151.9 40.8 %collective-permute-start.18 = (bf16[8,288,384]{2,1,0:T(8,128)(2,1)}, bf16[8,288,384]{2,1,0:T(8,128)(2,1)}, u32[]{:S(2)}, u32[]{:S(2)}) collective-permute-start(bf16[8,288,384]{2,1,0:T(8,128)(2,1)} %get-tuple-element.141), channel_id=1, source_target_pairs={{0,1},{1,0},{2,3},{3,2},{4,5},{5,4},{6,7},{7,6},{8,9},{9,8},{10,11... | collective-permute-start | bytes 5308424 | tf_op jit(solution)/shard_map/ppermute | solution.py:948
  153.6 41.4 %collective-permute-start.21 = (bf16[8,288,384]{2,1,0:T(8,128)(2,1)}, bf16[8,288,384]{2,1,0:T(8,128)(2,1)}, u32[]{:S(2)}, u32[]{:S(2)}) collective-permute-start(bf16[8,288,384]{2,1,0:T(8,128)(2,1)} %get-tuple-element.143), channel_id=1, source_target_pairs={{0,2},{1,3},{2,0},{3,1},{4,6},{5,7},{6,4},{7,5},{8,10},{9,11},{10,... | collective-permute-start | bytes 5308424 | tf_op jit(solution)/shard_map/ppermute | solution.py:948
  154.7 40.9 %collective-permute-start.20 = (bf16[384,384]{1,0:T(8,128)(2,1)}, bf16[384,384]{1,0:T(8,128)(2,1)S(1)}, u32[]{:S(2)}, u32[]{:S(2)}) collective-permute-start(bf16[384,384]{1,0:T(8,128)(2,1)} %fusion.4), channel_id=1, source_target_pairs={{0,4},{1,5},{2,6},{3,7},{4,0},{5,1},{6,2},{7,3},{8,12},{9,13},{10,... | collective-permute-start | bytes 884744 | tf_op jit(solution)/shard_map/ppermute | solution.py:948
  156.6 29.4 %collective-permute-start.17 = (bf16[512,768]{1,0:T(8,128)(2,1)}, bf16[512,768]{1,0:T(8,128)(2,1)}, u32[]{:S(2)}, u32[]{:S(2)}) collective-permute-start(bf16[512,768]{1,0:T(8,128)(2,1)} %get-tuple-element.154), channel_id=1, source_target_pairs={{0,16},{16,0},{1,17},{17,1},{2,18},{18,2},{3,19},{19,3},{4,20},{20... | collective-permute-start | bytes 2359304 | tf_op jit(solution)/shard_map/ppermute | solution.py:944
  184.7 16.7 %collective-permute-start.22 = (bf16[512,1024]{1,0:T(8,128)(2,1)}, bf16[512,1024]{1,0:T(8,128)(2,1)}, u32[]{:S(2)}, u32[]{:S(2)}) collective-permute-start(bf16[512,1024]{1,0:T(8,128)(2,1)} %get-tuple-element.163), channel_id=1, source_target_pairs={{0,16},{16,0},{1,17},{17,1},{2,18},{18,2},{3,19},{19,3},{4,20},{20... | collective-permute-start | bytes 3145736 | tf_op jit(solution)/shard_map/ppermute | solution.py:944
  186.0 18.9 %collective-permute-start.23 = (bf16[512,1024]{1,0:T(8,128)(2,1)}, bf16[512,1024]{1,0:T(8,128)(2,1)S(1)}, u32[]{:S(2)}, u32[]{:S(2)}) collective-permute-start(bf16[512,1024]{1,0:T(8,128)(2,1)} %get-tuple-element.164), channel_id=1, source_target_pairs={{0,16},{16,0},{1,17},{17,1},{2,18},{18,2},{3,19},{19,3},{4,20},{20... | collective-permute-start | bytes 3145736 | tf_op jit(solution)/shard_map/ppermute | solution.py:944
  192.6 12.3 %collective-permute-start.24 = (bf16[512,1024]{1,0:T(8,128)(2,1)}, bf16[512,1024]{1,0:T(8,128)(2,1)}, u32[]{:S(2)}, u32[]{:S(2)}) collective-permute-start(bf16[512,1024]{1,0:T(8,128)(2,1)} %get-tuple-element.166), channel_id=1, source_target_pairs={{0,16},{16,0},{1,17},{17,1},{2,18},{18,2},{3,19},{19,3},{4,20},{20... | collective-permute-start | bytes 3145736 | tf_op jit(solution)/shard_map/ppermute | solution.py:944
  195.6 32.7 %collective-permute-start.19 = (bf16[1152,384]{1,0:T(8,128)(2,1)}, bf16[1152,384]{1,0:T(8,128)(2,1)S(1)}, u32[]{:S(2)}, u32[]{:S(2)}) collective-permute-start(bf16[1152,384]{1,0:T(8,128)(2,1)} %bitcast.20), channel_id=1, source_target_pairs={{0,2},{1,3},{2,0},{3,1},{4,6},{5,7},{6,4},{7,5},{8,10},{9,11},{10,... | collective-permute-start | bytes 2654216 | tf_op jit(solution)/shard_map/ppermute | solution.py:948
  199.0 29.2 %collective-permute-start.28 = (bf16[1152,384]{1,0:T(8,128)(2,1)}, bf16[1152,384]{1,0:T(8,128)(2,1)}, u32[]{:S(2)}, u32[]{:S(2)}) collective-permute-start(bf16[1152,384]{1,0:T(8,128)(2,1)} %bitcast.27), channel_id=1, source_target_pairs={{0,1},{1,0},{2,3},{3,2},{4,5},{5,4},{6,7},{7,6},{8,9},{9,8},{10,11... | collective-permute-start | bytes 2654216 | tf_op jit(solution)/shard_map/ppermute | solution.py:948
  201.5 20.1 %collective-permute-start.26 = (f32[1,19968]{1,0:T(1,128)S(1)}, f32[1,19968]{1,0:T(1,128)S(1)}, u32[]{:S(2)}, u32[]{:S(2)}) collective-permute-start(f32[1,19968]{1,0:T(1,128)S(1)} %add.681), channel_id=1, source_target_pairs={{0,4},{1,5},{2,6},{3,7},{4,0},{5,1},{6,2},{7,3},{8,12},{9,13},{10,... | collective-permute-start | bytes 239624 | tf_op jit(solution)/shard_map/ppermute | solution.py:948
  231.5 21.4 %collective-permute-start.30 = (bf16[1152,384]{1,0:T(8,128)(2,1)}, bf16[1152,384]{1,0:T(8,128)(2,1)}, u32[]{:S(2)}, u32[]{:S(2)}) collective-permute-start(bf16[1152,384]{1,0:T(8,128)(2,1)} %bitcast.33), channel_id=1, source_target_pairs={{0,4},{1,5},{2,6},{3,7},{4,0},{5,1},{6,2},{7,3},{8,12},{9,13},{10,... | collective-permute-start | bytes 2654216 | tf_op jit(solution)/shard_map/ppermute | solution.py:948
  232.7 29.7 %collective-permute-start.32 = (bf16[8,208,384]{2,1,0:T(8,128)(2,1)}, bf16[8,208,384]{2,1,0:T(8,128)(2,1)S(1)}, u32[]{:S(2)}, u32[]{:S(2)}) collective-permute-start(bf16[8,208,384]{2,1,0:T(8,128)(2,1)} %get-tuple-element.167), channel_id=1, source_target_pairs={{0,1},{1,0},{2,3},{3,2},{4,5},{5,4},{6,7},{7,6},{8,9},{9,8},{10,11... | collective-permute-start | bytes 3833864 | tf_op jit(solution)/shard_map/ppermute | solution.py:948
  233.4 29.2 %collective-permute-start.34 = (bf16[8,192,384]{2,1,0:T(8,128)(2,1)}, bf16[8,192,384]{2,1,0:T(8,128)(2,1)S(1)}, u32[]{:S(2)}, u32[]{:S(2)}) collective-permute-start(bf16[8,192,384]{2,1,0:T(8,128)(2,1)} %get-tuple-element.168), channel_id=1, source_target_pairs={{0,2},{1,3},{2,0},{3,1},{4,6},{5,7},{6,4},{7,5},{8,10},{9,11},{10,... | collective-permute-start | bytes 3538952 | tf_op jit(solution)/shard_map/ppermute | solution.py:948
  236.1 30.6 %collective-permute-start.29 = (bf16[512,768]{1,0:T(8,128)(2,1)}, bf16[512,768]{1,0:T(8,128)(2,1)S(1)}, u32[]{:S(2)}, u32[]{:S(2)}) collective-permute-start(bf16[512,768]{1,0:T(8,128)(2,1)} %get-tuple-element.175), channel_id=1, source_target_pairs={{0,16},{16,0},{1,17},{17,1},{2,18},{18,2},{3,19},{19,3},{4,20},{20... | collective-permute-start | bytes 2359304 | tf_op jit(solution)/shard_map/ppermute | solution.py:944
  256.8 24.5 %collective-permute-start.31 = (bf16[576,384]{1,0:T(8,128)(2,1)S(1)}, bf16[576,384]{1,0:T(8,128)(2,1)S(1)}, u32[]{:S(2)}, u32[]{:S(2)}) collective-permute-start(bf16[576,384]{1,0:T(8,128)(2,1)S(1)} %pad_maximum_fusion.2), channel_id=1, source_target_pairs={{0,8},{1,9},{2,10},{3,11},{4,12},{5,13},{6,14},{7,15},{8,0},{9,1},... | collective-permute-start | bytes 1327112 | tf_op jit(solution)/shard_map/ppermute | solution.py:948
  262.8 18.4 %collective-permute-start.35 = (bf16[768,384]{1,0:T(8,128)(2,1)S(1)}, bf16[768,384]{1,0:T(8,128)(2,1)S(1)}, u32[]{:S(2)}, u32[]{:S(2)}) collective-permute-start(bf16[768,384]{1,0:T(8,128)(2,1)S(1)} %bitcast.219), channel_id=1, source_target_pairs={{0,1},{1,0},{2,3},{3,2},{4,5},{5,4},{6,7},{7,6},{8,9},{9,8},{10,11... | collective-permute-start | bytes 1769480 | tf_op jit(solution)/shard_map/ppermute | solution.py:948
  263.8 22.9 %collective-permute-start.41 = (bf16[192,384]{1,0:T(8,128)(2,1)S(1)}, bf16[192,384]{1,0:T(8,128)(2,1)S(1)}, u32[]{:S(2)}, u32[]{:S(2)}) collective-permute-start(bf16[192,384]{1,0:T(8,128)(2,1)S(1)} %copy-done.25), channel_id=1, source_target_pairs={{0,8},{1,9},{2,10},{3,11},{4,12},{5,13},{6,14},{7,15},{8,0},{9,1},... | collective-permute-start | bytes 442376 | tf_op jit(solution)/shard_map/ppermute | solution.py:948
  265.4 18.3 %collective-permute-start.39 = (f32[1,19968]{1,0:T(1,128)S(1)}, f32[1,19968]{1,0:T(1,128)S(1)}, u32[]{:S(2)}, u32[]{:S(2)}) collective-permute-start(f32[1,19968]{1,0:T(1,128)S(1)} %add.683), channel_id=1, source_target_pairs={{0,1},{1,0},{2,3},{3,2},{4,5},{5,4},{6,7},{7,6},{8,9},{9,8},{10,11... | collective-permute-start | bytes 239624 | tf_op jit(solution)/shard_map/ppermute | solution.py:948
  266.7 14.7 %collective-permute-start.33 = (bf16[832,384]{1,0:T(8,128)(2,1)S(1)}, bf16[832,384]{1,0:T(8,128)(2,1)S(1)}, u32[]{:S(2)}, u32[]{:S(2)}) collective-permute-start(bf16[832,384]{1,0:T(8,128)(2,1)S(1)} %bitcast.208), channel_id=1, source_target_pairs={{0,2},{1,3},{2,0},{3,1},{4,6},{5,7},{6,4},{7,5},{8,10},{9,11},{10,... | collective-permute-start | bytes 1916936 | tf_op jit(solution)/shard_map/ppermute | solution.py:948
  281.6 15.9 %collective-permute-start.36 = (bf16[800,384]{1,0:T(8,128)(2,1)S(1)}, bf16[800,384]{1,0:T(8,128)(2,1)S(1)}, u32[]{:S(2)}, u32[]{:S(2)}) collective-permute-start(bf16[800,384]{1,0:T(8,128)(2,1)S(1)} %bitcast.213), channel_id=1, source_target_pairs={{0,4},{1,5},{2,6},{3,7},{4,0},{5,1},{6,2},{7,3},{8,12},{9,13},{10,... | collective-permute-start | bytes 1843208 | tf_op jit(solution)/shard_map/ppermute | solution.py:948
  289.4 30.7 %collective-permute-start.42 = (f32[192,384]{1,0:T(8,128)S(1)}, f32[192,384]{1,0:T(8,128)}, u32[]{:S(2)}, u32[]{:S(2)}) collective-permute-start(f32[192,384]{1,0:T(8,128)S(1)} %get-tuple-element.260), channel_id=1, source_target_pairs={{0,16},{16,0},{1,17},{17,1},{2,18},{18,2},{3,19},{19,3},{4,20},{20... | collective-permute-start | bytes 884744 | tf_op jit(solution)/shard_map/ppermute | solution.py:944
  299.3 14.9 %collective-permute-start.37 = (bf16[400,384]{1,0:T(8,128)(2,1)S(1)}, bf16[400,384]{1,0:T(8,128)(2,1)S(1)}, u32[]{:S(2)}, u32[]{:S(2)}) collective-permute-start(bf16[400,384]{1,0:T(8,128)(2,1)S(1)} %pad_maximum_fusion.3), channel_id=1, source_target_pairs={{0,8},{1,9},{2,10},{3,11},{4,12},{5,13},{6,14},{7,15},{8,0},{9,1},... | collective-permute-start | bytes 921608 | tf_op jit(solution)/shard_map/ppermute | solution.py:948
  (46 other events, 301.7 us)

commit v4 on v3

--- a/solution.py
+++ b/solution.py
@@ -207,20 +207,9 @@
     return as_row(jnp.concatenate(rstds, axis=0))
 
 
-def erf_tail(magnitude, bell):
-    t = 1.0 / (1.0 + (0.3275911 * 0.7071067811865476) * magnitude)
-    poly = 0.5 * 1.061405429
-    for factor in (-1.453152027, 1.421413741, -0.284496736, 0.254829592):
-        poly = poly * t + 0.5 * factor
-    return poly * t * bell
-
-
 def gelu_and_slope(u):
-    bell = jnp.exp(u * u * -0.5)
-    tail = erf_tail(jnp.abs(u), bell)
-    cdf = jnp.where(u < 0.0, tail, 1.0 - tail)
-    value = u * cdf
-    return value, cdf + u * bell * 0.3989422804014327
+    cdf = 0.5 + 0.5 * lax.erf(u * 0.7071067811865476)
+    return u * cdf, cdf + u * jnp.exp(u * u * -0.5) * 0.3989422804014327
 
 
 def in_two(body, hook):
@@ -800,7 +789,7 @@
         outs = {order: (refs.pop(0), refs.pop(0)) for order in in_use}
         mine = slice(0, T)
         theirs = slice(T, 2 * T)
-        loaded = []
+        plans_of_loads = []
         for unit, arrays in zip(units, ins):
             arrays = list(arrays)
             buffers = [refs.pop(0) for _ in widths[unit[0]]]
@@ -818,8 +807,12 @@
                         cols = lanes(section * HALF, width) if start == "half" else slice(start, start + width)
                         loads.append((arrays.pop(0).at[:, cols], buffer.at[rows, filled : filled + width]))
                         filled += width
+            plans_of_loads.append((buffers, loads))
+
+        def start_loads(place):
+            buffers, loads = plans_of_loads[place]
             base = None
-            if unit[0] == "down":
+            if units[place][0] == "down":
                 waits = [copies.load(*load) for load in loads[2:]]
                 base = copies.used
                 for step in range(CHUNKS):
@@ -828,7 +821,9 @@
                         copies.load(source.at[:, cols], target.at[:, cols])
             else:
                 waits = [copies.load(*load) for load in loads]
-            loaded.append((waits, buffers, base, loads))
+            return waits, buffers, base, loads
+
+        loaded = {0: start_loads(0)}
         filled = [0, 0]
         for place, (unit, plan) in enumerate(zip(units, plans)):
             stages = {order: (refs.pop(0), refs.pop(0)) for order in in_use if order in plan}
@@ -837,6 +832,8 @@
             waits, buffers, base, loads = loaded[place]
             for wait in waits:
                 wait.wait()
+            if place + 1 < len(units):
+                loaded[place + 1] = start_loads(place + 1)
             if unit[0] == "down":
                 g, dy = buffers
                 tall = FF // n
@@ -1126,18 +1123,18 @@
 
     last = chains(grads)
     vg = vg + after(vg_next, grads[0][1])
-    vg_next = across(vg, 8, n)
-    vg = vg + vg_next
-    sent = step_together(high, grads[0][1], grads[1][1], vg)
+    sent = step_together(high, grads[0][1], grads[1][1])
+    vg_next = across(after(vg, sent), 8, n)
+    d_low_r = swap(after(d_low, sent))
+    sent = step_each(last, sent)
+    sent = step_together(high, sent)
+    vg = vg + after(vg_next, sent)
     vg_next = across(vg, 1, n)
-    d_low_r = swap(after(d_low, sent))
-    sent = step_together(high, sent)
-    sent = step_each(last, sent)
+    sent = step_together(last, sent, d_low_r)
     vg = vg + after(vg_next, sent)
     vg_next = across(vg, 2, n)
-    sent = step_together(last, sent, d_low_r, *[part.pending for part in high])
+    sent = step_together(last, sent)
     vg = vg + after(vg_next, sent)
-    sent = step_together(last, sent)
     for bit in orders[0][4:]:
         vg = vg + across(vg, bit, n)
         for group in ([down_high], high, last):
@@ -1177,10 +1174,11 @@
 
     left, right = [half.reshape(4, tall, HALF)[:, :small].reshape(4 * small, HALF) for half in halves(down_low, down_high)]
     grad_down = jnp.concatenate([left, right], axis=1)[None]
+    shares = [share(*where) for where in ((OB,), (G1,), (S1,), (UB, 4), (DB,), (G2,), (S2,), (QB, 2))]
     send, own = finish_pieces(scal, high, low_base, low_end)
     grad_up, grad_qkv, grad_out, rows = place_pieces(small, tall, scal, own, swap(send))
     low_qv = lax.dynamic_slice(jnp.concatenate([rows[0], rows[2]]), (index * 2 * small,), (2 * small,))[None]
-    grad_qv = jnp.where(is_first, low_qv, share(QB, 2))
+    grad_qv = jnp.where(is_first, low_qv, shares[7])
 
     def both(early, late):
         (own_low, other_low), (own_high, other_high) = early, late
@@ -1202,15 +1200,15 @@
         grad_qkv[None],
         grad_qv,
         grad_out[None],
-        share(OB),
-        share(G1),
-        share(S1),
+        shares[0],
+        shares[1],
+        shares[2],
         grad_up[None],
-        share(UB, 4),
+        shares[3],
         grad_down,
-        share(DB),
-        share(G2),
-        share(S2),
+        shares[4],
+        shares[5],
+        shares[6],
         head_out,
     )
 

time: 330 us -> 320 us (0.970)
  waiting for transfers between devices: 77 us -> 59.5 us
  starting transfers between devices: 28 us -> 36.7 us
  Pallas kernels: 171 us -> 165 us
  other arithmetic: 30.9 us -> 34.9 us
    ppermute x20, waiting for transfers between devices: 66.5 us -> 49.8 us  [across(): return lax.ppermute(array, 'dp', [(i, i ^ bit) for i in range(n)])]
    ppermute x20, starting transfers between devices: 22.8 us -> 31 us  [across(): return lax.ppermute(array, 'dp', [(i, i ^ bit) for i in range(n)])]
    pallas_call x11, Pallas kernels: 171 us -> 165 us  [kernel_call(): pl.pallas_call(wrapped, in_specs=specs, out_specs=[spec for _, _, spec in...]
    unnamed x73 -> x49, local copies, waits for them, and re-layouts: 11.3 us -> 8.48 us
  transfers between devices with their start and end apart: 43 -> 43, of which waited for: 10 -> 10; matrix products, arithmetic and copies ran while one was open for 11% -> 13% of each run, Pallas kernels for 41% -> 41%
where the time goes in v4:
time: 320 us; the launch traced here: 315 us
  Pallas kernels  165 us (52%)
  waiting for transfers between devices  59.5 us (19%)
  starting transfers between devices  36.7 us (11%)
  other arithmetic  34.9 us (11%)
  local copies, waits for them, and re-layouts  16.7 us (5%)
    pallas_call x11, Pallas kernels, kernel_call(): pl.pallas_call(wrapped, in_specs=specs, out_specs=[spec for _, _, spec in...  165 us
    ppermute x20, waiting for transfers between devices, across(): return lax.ppermute(array, 'dp', [(i, i ^ bit) for i in range(n)])  49.8 us
    ppermute x20, starting transfers between devices, across(): return lax.ppermute(array, 'dp', [(i, i ^ bit) for i in range(n)])  31 us
    convert_element_type x14, other arithmetic, outgoing(): send = sum((lax.dynamic_index_in_dim(part, 1 - mine, place, keepdims=Fals...  19.1 us
    ppermute x23, waiting for transfers between devices, swap(): return lax.ppermute(array, 'section', SWAP)  9.69 us
    unnamed x49, local copies, waits for them, and re-layouts  8.48 us
  transfers between devices with their start and end apart: 43, of which 10 were waited for; matrix products, arithmetic and copies ran while one was open for 13% of the time, Pallas kernels for 41%

profile of v4, /device:TPU:0, one launch (start us, length us, event | category | flops | bytes accessed | tf_op | source)
XLA Modules:
  0.0 315.0 jit_solution(2672908770792513087)
XLA Ops:
  3.2 5.8 %collective-permute-done.refs_4_.refs_5_.refs_8_ = f32[1,9216]{1,0:T(1,128)S(1)} collective-permute-done((f32[1,9216]{1,0:T(1,128)}, f32[1,9216]{1,0:T(1,128)S(1)}, u32[]{:S(2)}, u32[]{:S(2)}) %collective-permute-start) | collective-permute-done | bytes 36896 | tf_op jit(solution)/shard_map/ppermute | solution.py:941
  11.8 17.4 %first_attention.1 = (bf16[512,2304]{1,0:T(8,128)(2,1)}, bf16[12,512,512]{2,1,0:T(8,128)(2,1)}, f32[512,768]{1,0:T(8,128)}, bf16[512,1536]{1,0:T(8,128)(2,1)}, f32[1,512]{1,0:T(1,128)}) custom-call(s32[3]{0:T(128)} %pad_add_fusion.refs_0_, bf16[1024,768]{1,0:T(8,128)(2,1)} %refs_6_.3, s32[1,1024]{1,0:T(1,128)} %bitcast.208, ...), custom_call_target="tpu_custom_call" | custom-call | flops 15000000512 | bytes 30001000 | tf_op jit(solution)/shard_map/first_attention/pallas_call | solution.py:118
  29.3 30.2 %middle.1 = (bf16[512,5376]{1,0:T(8,128)(2,1)}, bf16[512,3072]{1,0:T(8,128)(2,1)}, f32[512,768]{1,0:T(8,128)}, bf16[512,2304]{1,0:T(8,128)(2,1)}, bf16[12,512,51...) custom-call(s32[3]{0:T(128)} %pad_add_fusion.refs_0_, ...), custom_call_target="tpu_custom_call" | custom-call | flops 30000001024 | bytes 60001000 | tf_op jit(solution)/shard_map/middle/pallas_call | solution.py:118
  60.6 10.7 %top.1 = (bf16[512,768]{1,0:T(8,128)(2,1)}, f32[512,768]{1,0:T(8,128)}, bf16[512,384]{1,0:T(8,128)(2,1)}, bf16[512,384]{1,0:T(8,128)(2,1)}, bf16[512,768]{1,0:T(...) custom-call(s32[3]{0:T(128)} %pad_add_fusion.refs_0_, bf16[512,3072]{1,0:T(8,128)(2,1)} %get-tuple-element.113.refs_1_, ...), custom_call_target="tpu_custom_call" | custom-call | flops 10000001024 | bytes 20001000 | tf_op jit(solution)/shard_map/top/pallas_call | solution.py:118
  71.8 2.0 collective-permute-done.8.refs_4_
  76.2 8.6 %high_down_grads.1 = (bf16[8,192,384]{2,1,0:T(8,128)(2,1)}, bf16[8,192,384]{2,1,0:T(8,128)(2,1)}) custom-call(s32[3]{0:T(128)} %pad_add_fusion.refs_0_, bf16[512,3072]{1,0:T(8,128)(2,1)} %get-tuple-element.113.refs_1_, bf16[512,3072]{1,0:T(8,128)(2,1)} %copy-done.20, bf16[512,384]{1,0:T(8,128)(2,1)} %get-tuple-element.117.refs_3_, bf16[512,384]{1,0:T(8,128)(2,1)} %copy-done.22), custom_call_target="tpu_custom_call" | custom-call | flops 7000001024 | bytes 14001000 | tf_op jit(solution)/shard_map/high_down_grads/pallas_call | solution.py:118
  84.7 2.9 collective-permute-start.9
  87.7 29.3 %layer_backward.2 = (bf16[512,1536]{1,0:T(8,128)(2,1)}, bf16[512,768]{1,0:T(8,128)(2,1)}, bf16[512,1152]{1,0:T(8,128)(2,1)}, bf16[512,1024]{1,0:T(8,128)(2,1)}, ...) custom-call(s32[3]{0:T(128)} %pad_add_fusion.refs_0_, ...), custom_call_target="tpu_custom_call" | custom-call | flops 25000001536 | bytes 50001000 | tf_op jit(solution)/shard_map/layer_backward/pallas_call | solution.py:118
  118.1 2.2 add_convert_fusion.4
  121.8 1.8 collective-permute-done.15.refs_18_
  124.8 19.7 %high_grads.1 = (bf16[8,288,384]{2,1,0:T(8,128)(2,1)}, bf16[8,288,384]{2,1,0:T(8,128)(2,1)}, bf16[8,288,384]{2,1,0:T(8,128)(2,1)}, bf16[8,288,384]{2,1,0:T(8,128)(2,1)}) custom-call(s32[3]{0:T(128)} %pad_add_fusion.refs_0_, bf16[512,5376]{1,0:T(8,128)(2,1)} %get-tuple-element.112.refs_13_.refs_1_.refs_6_.refs_8_.refs_15_, ...), custom_call_target="tpu_custom_call" | custom-call | flops 1000 | bytes 1000 | tf_op jit(solution)/shard_map/high_grads/pallas_call | solution.py:118
  155.8 27.8 %layer_backward.3 = (bf16[512,1536]{1,0:T(8,128)(2,1)}, bf16[512,768]{1,0:T(8,128)(2,1)}, bf16[512,1152]{1,0:T(8,128)(2,1)}, bf16[512,1024]{1,0:T(8,128)(2,1)}, ...) custom-call(s32[3]{0:T(128)} %pad_add_fusion.refs_0_, ...), custom_call_target="tpu_custom_call" | custom-call | flops 1000 | bytes 1000 | tf_op jit(solution)/shard_map/layer_backward/pallas_call | solution.py:118
  184.2 2.7 collective-permute-done.18
  186.9 2.6 add_convert_fusion.1
  190.0 2.3 add_convert_fusion
  195.6 15.6 %low_grads.1 = (bf16[8,208,384]{2,1,0:T(8,128)(2,1)}, bf16[8,208,384]{2,1,0:T(8,128)(2,1)}, bf16[8,192,384]{2,1,0:T(8,128)(2,1)}, bf16[8,192,384]{2,1,0:T(8,128)(2,1)}) custom-call(s32[3]{0:T(128)} %pad_add_fusion.refs_0_, bf16[512,1536]{1,0:T(8,128)(2,1)} %get-tuple-element.146.refs_1_.refs_13_.refs_7_, ...), custom_call_target="tpu_custom_call" | custom-call | flops 1000 | bytes 1000 | tf_op jit(solution)/shard_map/low_grads/pallas_call | solution.py:118
  211.2 1.7 collective-permute-start.28
  214.5 2.0 fusion
  222.7 18.9 %collective-permute-done.37 = f32[1,19968]{1,0:T(1,128)S(1)} collective-permute-done((f32[1,19968]{1,0:T(1,128)S(1)}, f32[1,19968]{1,0:T(1,128)S(1)}, u32[]{:S(2)}, u32[]{:S(2)}) %collective-permute-start.37) | collective-permute-done | bytes 79904 | tf_op jit(solution)/shard_map/ppermute | solution.py:945
  241.7 2.6 collective-permute-start.41
  254.0 2.1 collective-permute-start.30
  257.8 4.6 %collective-permute-done.32 = bf16[768,384]{1,0:T(8,128)(2,1)S(1)} collective-permute-done((bf16[768,384]{1,0:T(8,128)(2,1)S(1)}, bf16[768,384]{1,0:T(8,128)(2,1)S(1)}, u32[]{:S(2)}, u32[]{:S(2)}) %collective-permute-start.32) | collective-permute-done | bytes 589856 | tf_op jit(solution)/shard_map/ppermute | solution.py:945
  263.7 1.6 collective-permute-start.33
  266.7 2.3 collective-permute-start.40
  269.0 4.5 %collective-permute-done.30 = bf16[576,384]{1,0:T(8,128)(2,1)S(1)} collective-permute-done((bf16[576,384]{1,0:T(8,128)(2,1)S(1)}, bf16[576,384]{1,0:T(8,128)(2,1)S(1)}, u32[]{:S(2)}, u32[]{:S(2)}) %collective-permute-start.30) | collective-permute-done | bytes 442400 | tf_op jit(solution)/shard_map/ppermute | solution.py:945
  273.5 1.7 fusion.5
  278.0 6.6 %collective-permute-done.33 = bf16[800,384]{1,0:T(8,128)(2,1)S(1)} collective-permute-done((bf16[800,384]{1,0:T(8,128)(2,1)S(1)}, bf16[800,384]{1,0:T(8,128)(2,1)S(1)}, u32[]{:S(2)}, u32[]{:S(2)}) %collective-permute-start.33) | collective-permute-done | bytes 614432 | tf_op jit(solution)/shard_map/ppermute | solution.py:945
  284.6 1.9 fusion.11
  287.5 2.9 collective-permute-start.34
  291.4 12.4 %collective-permute-done.34 = bf16[400,384]{1,0:T(8,128)(2,1)S(1)} collective-permute-done((bf16[400,384]{1,0:T(8,128)(2,1)S(1)}, bf16[400,384]{1,0:T(8,128)(2,1)S(1)}, u32[]{:S(2)}, u32[]{:S(2)}) %collective-permute-start.34) | collective-permute-done | bytes 307232 | tf_op jit(solution)/shard_map/ppermute | solution.py:945
  305.1 2.5 finish_pieces.1
  310.8 2.3 place_pieces.1
  (174 shorter events, 61.1 us)
Async XLA Ops:
  0.6 8.3 %collective-permute-start.1 = (bf16[768,2304]{1,0:T(8,128)(2,1)}, bf16[768,2304]{1,0:T(8,128)(2,1)S(1)}, u32[]{:S(2)}, u32[]{:S(2)}) collective-permute-start(bf16[768,2304]{1,0:T(8,128)(2,1)} %bitcast.167), channel_id=1, source_target_pairs={{0,16},{16,0},{1,17},{17,1},{2,18},{18,2},{3,19},{19,3},{4,20},{20... | collective-permute-start | bytes 10616840 | tf_op jit(solution)/shard_map/ppermute | solution.py:941
  10.0 19.2 %collective-permute-start.3 = (bf16[768,3072]{1,0:T(8,128)(2,1)}, bf16[768,3072]{1,0:T(8,128)(2,1)}, u32[]{:S(2)}, u32[]{:S(2)}) collective-permute-start(bf16[768,3072]{1,0:T(8,128)(2,1)} %bitcast.158), channel_id=1, source_target_pairs={{0,16},{16,0},{1,17},{17,1},{2,18},{18,2},{3,19},{19,3},{4,20},{20... | collective-permute-start | bytes 14155784 | tf_op jit(solution)/shard_map/ppermute | solution.py:941
  10.4 18.9 %collective-permute-start.4 = (bf16[3072,768]{1,0:T(8,128)(2,1)}, bf16[3072,768]{1,0:T(8,128)(2,1)}, u32[]{:S(2)}, u32[]{:S(2)}) collective-permute-start(bf16[3072,768]{1,0:T(8,128)(2,1)} %bitcast.162), channel_id=1, source_target_pairs={{0,16},{16,0},{1,17},{17,1},{2,18},{18,2},{3,19},{19,3},{4,20},{20... | collective-permute-start | bytes 14155784 | tf_op jit(solution)/shard_map/ppermute | solution.py:941
  59.4 28.2 %collective-permute-start.6 = (bf16[512,5376]{1,0:T(8,128)(2,1)}, bf16[512,5376]{1,0:T(8,128)(2,1)}, u32[]{:S(2)}, u32[]{:S(2)}) collective-permute-start(bf16[512,5376]{1,0:T(8,128)(2,1)} %get-tuple-element.112.refs_13_.refs_1_.refs_6_.refs_8_.refs_15_), channel_id=1, source_target_pairs={{0,16},{16,0},{1,17},{17,1},{2,18},{18,2},{3,19},{19,3},{4,20},{20... | collective-permute-start | bytes 16515080 | tf_op jit(solution)/shard_map/ppermute | solution.py:941
  59.9 13.9 %collective-permute-start.7 = (bf16[512,3072]{1,0:T(8,128)(2,1)}, bf16[512,3072]{1,0:T(8,128)(2,1)S(1)}, u32[]{:S(2)}, u32[]{:S(2)}) collective-permute-start(bf16[512,3072]{1,0:T(8,128)(2,1)} %get-tuple-element.113.refs_1_), channel_id=1, source_target_pairs={{0,16},{16,0},{1,17},{17,1},{2,18},{18,2},{3,19},{19,3},{4,20},{20... | collective-permute-start | bytes 9437192 | tf_op jit(solution)/shard_map/ppermute | solution.py:941
  71.7 16.0 %collective-permute-start.5 = (bf16[512,768]{1,0:T(8,128)(2,1)}, bf16[512,768]{1,0:T(8,128)(2,1)S(1)}, u32[]{:S(2)}, u32[]{:S(2)}) collective-permute-start(bf16[512,768]{1,0:T(8,128)(2,1)} %get-tuple-element.115), channel_id=1, source_target_pairs={{0,16},{16,0},{1,17},{17,1},{2,18},{18,2},{3,19},{19,3},{4,20},{20... | collective-permute-start | bytes 2359304 | tf_op jit(solution)/shard_map/ppermute | solution.py:941
  84.7 33.4 %collective-permute-start.9 = (bf16[8,192,384]{2,1,0:T(8,128)(2,1)}, bf16[8,192,384]{2,1,0:T(8,128)(2,1)}, u32[]{:S(2)}, u32[]{:S(2)}) collective-permute-start(bf16[8,192,384]{2,1,0:T(8,128)(2,1)} %get-tuple-element.120), channel_id=1, source_target_pairs={{0,1},{1,0},{2,3},{3,2},{4,5},{5,4},{6,7},{7,6},{8,9},{9,8},{10,11... | collective-permute-start | bytes 3538952 | tf_op jit(solution)/shard_map/ppermute | solution.py:945
  120.3 28.8 %collective-permute-start.11 = (bf16[768,384]{1,0:T(8,128)(2,1)}, bf16[768,384]{1,0:T(8,128)(2,1)}, u32[]{:S(2)}, u32[]{:S(2)}) collective-permute-start(bf16[768,384]{1,0:T(8,128)(2,1)} %bitcast.12), channel_id=1, source_target_pairs={{0,2},{1,3},{2,0},{3,1},{4,6},{5,7},{6,4},{7,5},{8,10},{9,11},{10,... | collective-permute-start | bytes 1769480 | tf_op jit(solution)/shard_map/ppermute | solution.py:945
  123.6 32.1 %collective-permute-start.16 = (bf16[512,1536]{1,0:T(8,128)(2,1)S(1)}, bf16[512,1536]{1,0:T(8,128)(2,1)}, u32[]{:S(2)}, u32[]{:S(2)}) collective-permute-start(bf16[512,1536]{1,0:T(8,128)(2,1)S(1)} %copy-done), channel_id=1, source_target_pairs={{0,16},{16,0},{1,17},{17,1},{2,18},{18,2},{3,19},{19,3},{4,20},{20... | collective-permute-start | bytes 4718600 | tf_op jit(solution)/shard_map/ppermute | solution.py:941
  144.4 45.1 %collective-permute-start.21 = (bf16[8,288,384]{2,1,0:T(8,128)(2,1)}, bf16[8,288,384]{2,1,0:T(8,128)(2,1)}, u32[]{:S(2)}, u32[]{:S(2)}) collective-permute-start(bf16[8,288,384]{2,1,0:T(8,128)(2,1)} %get-tuple-element.145), channel_id=1, source_target_pairs={{0,2},{1,3},{2,0},{3,1},{4,6},{5,7},{6,4},{7,5},{8,10},{9,11},{10,... | collective-permute-start | bytes 5308424 | tf_op jit(solution)/shard_map/ppermute | solution.py:945
  146.0 40.9 %collective-permute-start.18 = (bf16[8,288,384]{2,1,0:T(8,128)(2,1)}, bf16[8,288,384]{2,1,0:T(8,128)(2,1)}, u32[]{:S(2)}, u32[]{:S(2)}) collective-permute-start(bf16[8,288,384]{2,1,0:T(8,128)(2,1)} %get-tuple-element.143), channel_id=1, source_target_pairs={{0,1},{1,0},{2,3},{3,2},{4,5},{5,4},{6,7},{7,6},{8,9},{9,8},{10,11... | collective-permute-start | bytes 5308424 | tf_op jit(solution)/shard_map/ppermute | solution.py:945
  151.0 32.7 %collective-permute-start.17 = (bf16[512,768]{1,0:T(8,128)(2,1)S(1)}, bf16[512,768]{1,0:T(8,128)(2,1)S(1)}, u32[]{:S(2)}, u32[]{:S(2)}) collective-permute-start(bf16[512,768]{1,0:T(8,128)(2,1)S(1)} %copy-done.10), channel_id=1, source_target_pairs={{0,16},{16,0},{1,17},{17,1},{2,18},{18,2},{3,19},{19,3},{4,20},{20... | collective-permute-start | bytes 2359304 | tf_op jit(solution)/shard_map/ppermute | solution.py:941
  153.9 38.5 %collective-permute-start.20 = (bf16[384,384]{1,0:T(8,128)(2,1)}, bf16[384,384]{1,0:T(8,128)(2,1)}, u32[]{:S(2)}, u32[]{:S(2)}) collective-permute-start(bf16[384,384]{1,0:T(8,128)(2,1)} %fusion.4), channel_id=1, source_target_pairs={{0,4},{1,5},{2,6},{3,7},{4,0},{5,1},{6,2},{7,3},{8,12},{9,13},{10,... | collective-permute-start | bytes 884744 | tf_op jit(solution)/shard_map/ppermute | solution.py:945
  183.6 10.4 %collective-permute-start.22 = (bf16[512,1024]{1,0:T(8,128)(2,1)}, bf16[512,1024]{1,0:T(8,128)(2,1)S(1)}, u32[]{:S(2)}, u32[]{:S(2)}) collective-permute-start(bf16[512,1024]{1,0:T(8,128)(2,1)} %get-tuple-element.165), channel_id=1, source_target_pairs={{0,16},{16,0},{1,17},{17,1},{2,18},{18,2},{3,19},{19,3},{4,20},{20... | collective-permute-start | bytes 3145736 | tf_op jit(solution)/shard_map/ppermute | solution.py:941
  183.7 10.3 %collective-permute-start.23 = (bf16[512,1024]{1,0:T(8,128)(2,1)}, bf16[512,1024]{1,0:T(8,128)(2,1)S(1)}, u32[]{:S(2)}, u32[]{:S(2)}) collective-permute-start(bf16[512,1024]{1,0:T(8,128)(2,1)} %get-tuple-element.166), channel_id=1, source_target_pairs={{0,16},{16,0},{1,17},{17,1},{2,18},{18,2},{3,19},{19,3},{4,20},{20... | collective-permute-start | bytes 3145736 | tf_op jit(solution)/shard_map/ppermute | solution.py:941
  189.5 24.9 %collective-permute-start.19 = (bf16[1152,384]{1,0:T(8,128)(2,1)}, bf16[1152,384]{1,0:T(8,128)(2,1)}, u32[]{:S(2)}, u32[]{:S(2)}) collective-permute-start(bf16[1152,384]{1,0:T(8,128)(2,1)} %bitcast.20), channel_id=1, source_target_pairs={{0,2},{1,3},{2,0},{3,1},{4,6},{5,7},{6,4},{7,5},{8,10},{9,11},{10,... | collective-permute-start | bytes 2654216 | tf_op jit(solution)/shard_map/ppermute | solution.py:945
  192.4 22.1 %collective-permute-start.25 = (bf16[1152,384]{1,0:T(8,128)(2,1)}, bf16[1152,384]{1,0:T(8,128)(2,1)}, u32[]{:S(2)}, u32[]{:S(2)}) collective-permute-start(bf16[1152,384]{1,0:T(8,128)(2,1)} %bitcast.27), channel_id=1, source_target_pairs={{0,1},{1,0},{2,3},{3,2},{4,5},{5,4},{6,7},{7,6},{8,9},{9,8},{10,11... | collective-permute-start | bytes 2654216 | tf_op jit(solution)/shard_map/ppermute | solution.py:945
  211.2 34.4 %collective-permute-start.28 = (bf16[8,192,384]{2,1,0:T(8,128)(2,1)}, bf16[8,192,384]{2,1,0:T(8,128)(2,1)}, u32[]{:S(2)}, u32[]{:S(2)}) collective-permute-start(bf16[8,192,384]{2,1,0:T(8,128)(2,1)} %get-tuple-element.170), channel_id=1, source_target_pairs={{0,2},{1,3},{2,0},{3,1},{4,6},{5,7},{6,4},{7,5},{8,10},{9,11},{10,... | collective-permute-start | bytes 3538952 | tf_op jit(solution)/shard_map/ppermute | solution.py:945
  213.0 31.4 %collective-permute-start.29 = (bf16[8,208,384]{2,1,0:T(8,128)(2,1)}, bf16[8,208,384]{2,1,0:T(8,128)(2,1)S(1)}, u32[]{:S(2)}, u32[]{:S(2)}) collective-permute-start(bf16[8,208,384]{2,1,0:T(8,128)(2,1)} %get-tuple-element.169), channel_id=1, source_target_pairs={{0,1},{1,0},{2,3},{3,2},{4,5},{5,4},{6,7},{7,6},{8,9},{9,8},{10,11... | collective-permute-start | bytes 3833864 | tf_op jit(solution)/shard_map/ppermute | solution.py:945
  217.5 30.2 %collective-permute-start.26 = (bf16[512,768]{1,0:T(8,128)(2,1)}, bf16[512,768]{1,0:T(8,128)(2,1)}, u32[]{:S(2)}, u32[]{:S(2)}) collective-permute-start(bf16[512,768]{1,0:T(8,128)(2,1)} %get-tuple-element.173), channel_id=1, source_target_pairs={{0,16},{16,0},{1,17},{17,1},{2,18},{18,2},{3,19},{19,3},{4,20},{20... | collective-permute-start | bytes 2359304 | tf_op jit(solution)/shard_map/ppermute | solution.py:941
  218.1 32.1 %collective-permute-start.27 = (bf16[1152,384]{1,0:T(8,128)(2,1)}, bf16[1152,384]{1,0:T(8,128)(2,1)}, u32[]{:S(2)}, u32[]{:S(2)}) collective-permute-start(bf16[1152,384]{1,0:T(8,128)(2,1)} %bitcast.33), channel_id=1, source_target_pairs={{0,4},{1,5},{2,6},{3,7},{4,0},{5,1},{6,2},{7,3},{8,12},{9,13},{10,... | collective-permute-start | bytes 2654216 | tf_op jit(solution)/shard_map/ppermute | solution.py:945
  220.6 21.0 %collective-permute-start.37 = (f32[1,19968]{1,0:T(1,128)S(1)}, f32[1,19968]{1,0:T(1,128)S(1)}, u32[]{:S(2)}, u32[]{:S(2)}) collective-permute-start(f32[1,19968]{1,0:T(1,128)S(1)} %add.730), channel_id=1, source_target_pairs={{0,4},{1,5},{2,6},{3,7},{4,0},{5,1},{6,2},{7,3},{8,12},{9,13},{10,... | collective-permute-start | bytes 239624 | tf_op jit(solution)/shard_map/ppermute | solution.py:945
  241.7 35.0 %collective-permute-start.41 = (bf16[192,384]{1,0:T(8,128)(2,1)S(1)}, bf16[192,384]{1,0:T(8,128)(2,1)S(1)}, u32[]{:S(2)}, u32[]{:S(2)}) collective-permute-start(bf16[192,384]{1,0:T(8,128)(2,1)S(1)} %fusion.12), channel_id=1, source_target_pairs={{0,8},{1,9},{2,10},{3,11},{4,12},{5,13},{6,14},{7,15},{8,0},{9,1},... | collective-permute-start | bytes 442376 | tf_op jit(solution)/shard_map/ppermute | solution.py:945
  244.4 11.8 %collective-permute-start.38 = (f32[1,19968]{1,0:T(1,128)S(1)}, f32[1,19968]{1,0:T(1,128)S(1)}, u32[]{:S(2)}, u32[]{:S(2)}) collective-permute-start(f32[1,19968]{1,0:T(1,128)S(1)} %add.731), channel_id=1, source_target_pairs={{0,8},{1,9},{2,10},{3,11},{4,12},{5,13},{6,14},{7,15},{8,0},{9,1},... | collective-permute-start | bytes 239624 | tf_op jit(solution)/shard_map/ppermute | solution.py:945
  245.6 17.9 %collective-permute-start.31 = (bf16[832,384]{1,0:T(8,128)(2,1)S(1)}, bf16[832,384]{1,0:T(8,128)(2,1)S(1)}, u32[]{:S(2)}, u32[]{:S(2)}) collective-permute-start(bf16[832,384]{1,0:T(8,128)(2,1)S(1)} %bitcast.198), channel_id=1, source_target_pairs={{0,2},{1,3},{2,0},{3,1},{4,6},{5,7},{6,4},{7,5},{8,10},{9,11},{10,... | collective-permute-start | bytes 1916936 | tf_op jit(solution)/shard_map/ppermute | solution.py:945
  247.7 14.7 %collective-permute-start.32 = (bf16[768,384]{1,0:T(8,128)(2,1)S(1)}, bf16[768,384]{1,0:T(8,128)(2,1)S(1)}, u32[]{:S(2)}, u32[]{:S(2)}) collective-permute-start(bf16[768,384]{1,0:T(8,128)(2,1)S(1)} %bitcast.206), channel_id=1, source_target_pairs={{0,1},{1,0},{2,3},{3,2},{4,5},{5,4},{6,7},{7,6},{8,9},{9,8},{10,11... | collective-permute-start | bytes 1769480 | tf_op jit(solution)/shard_map/ppermute | solution.py:945
  254.0 19.4 %collective-permute-start.30 = (bf16[576,384]{1,0:T(8,128)(2,1)S(1)}, bf16[576,384]{1,0:T(8,128)(2,1)S(1)}, u32[]{:S(2)}, u32[]{:S(2)}) collective-permute-start(bf16[576,384]{1,0:T(8,128)(2,1)S(1)} %pad_maximum_fusion.2), channel_id=1, source_target_pairs={{0,8},{1,9},{2,10},{3,11},{4,12},{5,13},{6,14},{7,15},{8,0},{9,1},... | collective-permute-start | bytes 1327112 | tf_op jit(solution)/shard_map/ppermute | solution.py:945
  256.2 10.4 %collective-permute-start.39 = (f32[1,19968]{1,0:T(1,128)S(1)}, f32[1,19968]{1,0:T(1,128)S(1)}, u32[]{:S(2)}, u32[]{:S(2)}) collective-permute-start(f32[1,19968]{1,0:T(1,128)S(1)} %add.732), channel_id=1, source_target_pairs={{0,1},{1,0},{2,3},{3,2},{4,5},{5,4},{6,7},{7,6},{8,9},{9,8},{10,11... | collective-permute-start | bytes 239624 | tf_op jit(solution)/shard_map/ppermute | solution.py:945
  263.7 20.9 %collective-permute-start.33 = (bf16[800,384]{1,0:T(8,128)(2,1)S(1)}, bf16[800,384]{1,0:T(8,128)(2,1)S(1)}, u32[]{:S(2)}, u32[]{:S(2)}) collective-permute-start(bf16[800,384]{1,0:T(8,128)(2,1)S(1)} %bitcast.203), channel_id=1, source_target_pairs={{0,4},{1,5},{2,6},{3,7},{4,0},{5,1},{6,2},{7,3},{8,12},{9,13},{10,... | collective-permute-start | bytes 1843208 | tf_op jit(solution)/shard_map/ppermute | solution.py:945
  266.7 24.6 %collective-permute-start.40 = (f32[1,19968]{1,0:T(1,128)S(1)}, f32[1,19968]{1,0:T(1,128)S(1)}, u32[]{:S(2)}, u32[]{:S(2)}) collective-permute-start(f32[1,19968]{1,0:T(1,128)S(1)} %add.733), channel_id=1, source_target_pairs={{0,2},{1,3},{2,0},{3,1},{4,6},{5,7},{6,4},{7,5},{8,10},{9,11},{10,... | collective-permute-start | bytes 239624 | tf_op jit(solution)/shard_map/ppermute | solution.py:945
  277.9 12.5 %collective-permute-start.42 = (f32[192,384]{1,0:T(8,128)S(1)}, f32[192,384]{1,0:T(8,128)S(1)}, u32[]{:S(2)}, u32[]{:S(2)}) collective-permute-start(f32[192,384]{1,0:T(8,128)S(1)} %get-tuple-element.264), channel_id=1, source_target_pairs={{0,16},{16,0},{1,17},{17,1},{2,18},{18,2},{3,19},{19,3},{4,20},{20... | collective-permute-start | bytes 884744 | tf_op jit(solution)/shard_map/ppermute | solution.py:941
  287.5 16.3 %collective-permute-start.34 = (bf16[400,384]{1,0:T(8,128)(2,1)S(1)}, bf16[400,384]{1,0:T(8,128)(2,1)S(1)}, u32[]{:S(2)}, u32[]{:S(2)}) collective-permute-start(bf16[400,384]{1,0:T(8,128)(2,1)S(1)} %pad_maximum_fusion.3), channel_id=1, source_target_pairs={{0,8},{1,9},{2,10},{3,11},{4,12},{5,13},{6,14},{7,15},{8,0},{9,1},... | collective-permute-start | bytes 921608 | tf_op jit(solution)/shard_map/ppermute | solution.py:945
  (34 other events, 188.5 us)

commit v5 on v4

--- a/solution.py
+++ b/solution.py
@@ -859,12 +859,22 @@
                 else:
                     x, o, dp, db = buffers
                     terms = [(x, dp, 0), (x, dp, 1), (x, dp, 2), (o, db, 0)]
-                for part, (left, right, block) in enumerate(terms):
+                part = 0
+                while part < 4:
+                    left, right, block = terms[part]
+                    follows = part < 3 and terms[part + 1][1] is right and terms[part + 1][2] == block + 1
+                    span = 2 if follows else 1
                     for half in range(2):
                         value = dot(
-                            left[:, half * HALF : (half + 1) * HALF], right[:, block * HALF : (block + 1) * HALF], 0, 0
+                            left[:, half * HALF : (half + 1) * HALF],
+                            right[:, block * HALF : (block + span) * HALF], 0, 0,
                         )
-                        pieces.put(value, plan[part], half * (n // 2), n // 2, slots[part])
+                        for more in range(span):
+                            pieces.put(
+                                value[:, more * HALF : (more + 1) * HALF], plan[part + more], half * (n // 2), n // 2,
+                                slots[part + more],
+                            )
+                    part += span
             if with_bias and unit[0] == "attn":
                 sums = [col_sum(dp[:, col * HALF : (col + 1) * HALF].astype(F32)) for col in range(3)]
                 tile = jnp.concatenate(sums + [jnp.zeros((TILE - 3, HALF), F32)], axis=0).astype(BF)
@@ -1022,13 +1032,13 @@
 
     wq, wo, wu, wd = qkv_weight[0], out_weight[0], up_weight[0], down_weight[0]
     wq_r = swap(wq)
-    vec = pack_vectors((qv_bias, out_bias, gain_one, shift_one, down_bias, gain_two, shift_two, up_bias))
+    ends = seq_ends.reshape(1, 2 * T)
+    termc = term_cotangent.reshape(1, 2 * T)
+    vec = pack_vectors((after(qv_bias, scal, ends, termc), out_bias, gain_one, shift_one, down_bias, gain_two, shift_two, up_bias))
     vec_r = swap(vec)
     wo_r = swap(after(wo, vec))
     wu_r = swap(after(wu, wq_r, vec_r, wo_r))
     wd_r = swap(after(wd, wq_r, vec_r, wo_r))
-    ends = seq_ends.reshape(1, 2 * T)
-    termc = term_cotangent.reshape(1, 2 * T)
     head = head_weight.reshape(1, D)
 
     qkv1, a1, xh1_low, pack1, rstd1_low = first_attention(scal, tokens, ends, vec, vec_r, wq, wq_r, wo, wo_r)

time: 320 us -> 319 us (level)
  transfers between devices with their start and end apart: 43 -> 43, of which waited for: 10 -> 11; matrix products, arithmetic and copies ran while one was open for 13% -> 13% of each run, Pallas kernels for 41% -> 41%
where the time goes in v5:
time: 319 us; the launch traced here: 314 us
  Pallas kernels  163 us (51%)
  waiting for transfers between devices  58.2 us (18%)
  starting transfers between devices  39.6 us (12%)
  other arithmetic  34.5 us (11%)
  local copies, waits for them, and re-layouts  17.7 us (6%)
    pallas_call x11, Pallas kernels, kernel_call(): pl.pallas_call(wrapped, in_specs=specs, out_specs=[spec for _, _, spec in...  163 us
    ppermute x20, waiting for transfers between devices, across(): return lax.ppermute(array, 'dp', [(i, i ^ bit) for i in range(n)])  49.1 us
    ppermute x20, starting transfers between devices, across(): return lax.ppermute(array, 'dp', [(i, i ^ bit) for i in range(n)])  33.9 us
    convert_element_type x14, other arithmetic, outgoing(): send = sum((lax.dynamic_index_in_dim(part, 1 - mine, place, keepdims=Fals...  19.1 us
    unnamed x49, local copies, waits for them, and re-layouts  9.44 us
    ppermute x23, waiting for transfers between devices, swap(): return lax.ppermute(array, 'section', SWAP)  9.1 us
  transfers between devices with their start and end apart: 43, of which 11 were waited for; matrix products, arithmetic and copies ran while one was open for 13% of the time, Pallas kernels for 41%

profile of v5, /device:TPU:0, one launch (start us, length us, event | category | flops | bytes accessed | tf_op | source)
XLA Modules:
  0.0 314.4 jit_solution(13660074845881592987)
XLA Ops:
  3.8 5.2 %collective-permute-done.refs_4_.refs_5_.refs_8_ = f32[1,9216]{1,0:T(1,128)S(1)} collective-permute-done((f32[1,9216]{1,0:T(1,128)}, f32[1,9216]{1,0:T(1,128)S(1)}, u32[]{:S(2)}, u32[]{:S(2)}) %collective-permute-start) | collective-permute-done | bytes 36896 | tf_op jit(solution)/shard_map/ppermute | solution.py:951
  11.8 17.3 %first_attention.1 = (bf16[512,2304]{1,0:T(8,128)(2,1)}, bf16[12,512,512]{2,1,0:T(8,128)(2,1)}, f32[512,768]{1,0:T(8,128)}, bf16[512,1536]{1,0:T(8,128)(2,1)}, f32[1,512]{1,0:T(1,128)}) custom-call(s32[3]{0:T(128)} %pad_add_fusion.refs_0_, bf16[1024,768]{1,0:T(8,128)(2,1)} %refs_6_.3, s32[1,1024]{1,0:T(1,128)} %bitcast.208, ...), custom_call_target="tpu_custom_call" | custom-call | flops 15000000512 | bytes 30001000 | tf_op jit(solution)/shard_map/first_attention/pallas_call | solution.py:118
  29.2 30.0 %middle.1 = (bf16[512,5376]{1,0:T(8,128)(2,1)}, bf16[512,3072]{1,0:T(8,128)(2,1)}, f32[512,768]{1,0:T(8,128)}, bf16[512,2304]{1,0:T(8,128)(2,1)}, bf16[12,512,51...) custom-call(s32[3]{0:T(128)} %pad_add_fusion.refs_0_, ...), custom_call_target="tpu_custom_call" | custom-call | flops 30000001024 | bytes 60001000 | tf_op jit(solution)/shard_map/middle/pallas_call | solution.py:118
  60.4 10.7 %top.1 = (bf16[512,768]{1,0:T(8,128)(2,1)}, f32[512,768]{1,0:T(8,128)}, bf16[512,384]{1,0:T(8,128)(2,1)}, bf16[512,384]{1,0:T(8,128)(2,1)}, bf16[512,768]{1,0:T(...) custom-call(s32[3]{0:T(128)} %pad_add_fusion.refs_0_, bf16[512,3072]{1,0:T(8,128)(2,1)} %get-tuple-element.115.refs_1_, ...), custom_call_target="tpu_custom_call" | custom-call | flops 10000001024 | bytes 20001000 | tf_op jit(solution)/shard_map/top/pallas_call | solution.py:118
  71.6 2.0 collective-permute-done.8.refs_4_
  75.9 8.5 %high_down_grads.1 = (bf16[8,192,384]{2,1,0:T(8,128)(2,1)}, bf16[8,192,384]{2,1,0:T(8,128)(2,1)}) custom-call(s32[3]{0:T(128)} %pad_add_fusion.refs_0_, bf16[512,3072]{1,0:T(8,128)(2,1)} %get-tuple-element.115.refs_1_, bf16[512,3072]{1,0:T(8,128)(2,1)} %copy-done.20, bf16[512,384]{1,0:T(8,128)(2,1)} %get-tuple-element.119.refs_3_, bf16[512,384]{1,0:T(8,128)(2,1)} %copy-done.22), custom_call_target="tpu_custom_call" | custom-call | flops 7000001024 | bytes 14001000 | tf_op jit(solution)/shard_map/high_down_grads/pallas_call | solution.py:118
  84.5 2.9 collective-permute-start.9
  87.4 29.6 %layer_backward.2 = (bf16[512,1536]{1,0:T(8,128)(2,1)}, bf16[512,768]{1,0:T(8,128)(2,1)}, bf16[512,1152]{1,0:T(8,128)(2,1)}, bf16[512,1024]{1,0:T(8,128)(2,1)}, ...) custom-call(s32[3]{0:T(128)} %pad_add_fusion.refs_0_, ...), custom_call_target="tpu_custom_call" | custom-call | flops 25000001536 | bytes 50001000 | tf_op jit(solution)/shard_map/layer_backward/pallas_call | solution.py:118
  118.1 2.2 add_convert_fusion.4
  121.8 1.8 collective-permute-done.15.refs_18_
  124.8 18.4 %high_grads.1 = (bf16[8,288,384]{2,1,0:T(8,128)(2,1)}, bf16[8,288,384]{2,1,0:T(8,128)(2,1)}, bf16[8,288,384]{2,1,0:T(8,128)(2,1)}, bf16[8,288,384]{2,1,0:T(8,128)(2,1)}) custom-call(s32[3]{0:T(128)} %pad_add_fusion.refs_0_, bf16[512,5376]{1,0:T(8,128)(2,1)} %get-tuple-element.114.refs_13_.refs_1_.refs_6_.refs_8_.refs_15_, ...), custom_call_target="tpu_custom_call" | custom-call | flops 1000 | bytes 1000 | tf_op jit(solution)/shard_map/high_grads/pallas_call | solution.py:118
  154.6 27.9 %layer_backward.3 = (bf16[512,1536]{1,0:T(8,128)(2,1)}, bf16[512,768]{1,0:T(8,128)(2,1)}, bf16[512,1152]{1,0:T(8,128)(2,1)}, bf16[512,1024]{1,0:T(8,128)(2,1)}, ...) custom-call(s32[3]{0:T(128)} %pad_add_fusion.refs_0_, ...), custom_call_target="tpu_custom_call" | custom-call | flops 1000 | bytes 1000 | tf_op jit(solution)/shard_map/layer_backward/pallas_call | solution.py:118
  183.0 2.7 collective-permute-done.18
  185.7 2.6 add_convert_fusion.1
  188.8 2.3 add_convert_fusion
  194.4 14.4 %low_grads.1 = (bf16[8,208,384]{2,1,0:T(8,128)(2,1)}, bf16[8,208,384]{2,1,0:T(8,128)(2,1)}, bf16[8,192,384]{2,1,0:T(8,128)(2,1)}, bf16[8,192,384]{2,1,0:T(8,128)(2,1)}) custom-call(s32[3]{0:T(128)} %pad_add_fusion.refs_0_, bf16[512,1536]{1,0:T(8,128)(2,1)} %get-tuple-element.148.refs_1_.refs_13_.refs_7_, ...), custom_call_target="tpu_custom_call" | custom-call | flops 1000 | bytes 1000 | tf_op jit(solution)/shard_map/low_grads/pallas_call | solution.py:118
  208.9 1.8 collective-permute-start.28
  213.2 2.0 fusion
  221.5 18.9 %collective-permute-done.37 = f32[1,19968]{1,0:T(1,128)S(1)} collective-permute-done((f32[1,19968]{1,0:T(1,128)S(1)}, f32[1,19968]{1,0:T(1,128)S(1)}, u32[]{:S(2)}, u32[]{:S(2)}) %collective-permute-start.37) | collective-permute-done | bytes 79904 | tf_op jit(solution)/shard_map/ppermute | solution.py:955
  240.4 2.6 collective-permute-start.41
  243.7 2.3 collective-permute-start.31
  252.4 2.7 collective-permute-start.30
  255.2 2.0 collective-permute-start.39
  257.3 4.6 %collective-permute-done.32 = bf16[768,384]{1,0:T(8,128)(2,1)S(1)} collective-permute-done((bf16[768,384]{1,0:T(8,128)(2,1)S(1)}, bf16[768,384]{1,0:T(8,128)(2,1)S(1)}, u32[]{:S(2)}, u32[]{:S(2)}) %collective-permute-start.32) | collective-permute-done | bytes 589856 | tf_op jit(solution)/shard_map/ppermute | solution.py:955
  266.2 4.5 %collective-permute-start.40 = (f32[1,19968]{1,0:T(1,128)S(1)}, f32[1,19968]{1,0:T(1,128)S(1)}, u32[]{:S(2)}, u32[]{:S(2)}) collective-permute-start(f32[1,19968]{1,0:T(1,128)S(1)} %add.733), channel_id=1, source_target_pairs={{0,2},{1,3},{2,0},{3,1},{4,6},{5,7},{6,4},{7,5},{8,10},{9,11},{10,... | collective-permute-start | bytes 239624 | tf_op jit(solution)/shard_map/ppermute | solution.py:955
  270.6 1.8 collective-permute-done.30
  276.9 7.2 %collective-permute-done.33 = bf16[800,384]{1,0:T(8,128)(2,1)S(1)} collective-permute-done((bf16[800,384]{1,0:T(8,128)(2,1)S(1)}, bf16[800,384]{1,0:T(8,128)(2,1)S(1)}, u32[]{:S(2)}, u32[]{:S(2)}) %collective-permute-start.33) | collective-permute-done | bytes 614432 | tf_op jit(solution)/shard_map/ppermute | solution.py:955
  284.1 1.9 fusion.11
  287.0 2.7 collective-permute-start.34
  290.7 12.7 %collective-permute-done.34 = bf16[400,384]{1,0:T(8,128)(2,1)S(1)} collective-permute-done((bf16[400,384]{1,0:T(8,128)(2,1)S(1)}, bf16[400,384]{1,0:T(8,128)(2,1)S(1)}, u32[]{:S(2)}, u32[]{:S(2)}) %collective-permute-start.34) | collective-permute-done | bytes 307232 | tf_op jit(solution)/shard_map/ppermute | solution.py:955
  304.8 2.5 finish_pieces.1
  310.4 2.3 place_pieces.1
  (174 shorter events, 62.0 us)
Async XLA Ops:
  0.6 8.3 %collective-permute-start.1 = (bf16[768,2304]{1,0:T(8,128)(2,1)}, bf16[768,2304]{1,0:T(8,128)(2,1)S(1)}, u32[]{:S(2)}, u32[]{:S(2)}) collective-permute-start(bf16[768,2304]{1,0:T(8,128)(2,1)} %bitcast.167), channel_id=1, source_target_pairs={{0,16},{16,0},{1,17},{17,1},{2,18},{18,2},{3,19},{19,3},{4,20},{20... | collective-permute-start | bytes 10616840 | tf_op jit(solution)/shard_map/ppermute | solution.py:951
  10.0 19.2 %collective-permute-start.3 = (bf16[768,3072]{1,0:T(8,128)(2,1)}, bf16[768,3072]{1,0:T(8,128)(2,1)}, u32[]{:S(2)}, u32[]{:S(2)}) collective-permute-start(bf16[768,3072]{1,0:T(8,128)(2,1)} %bitcast.158), channel_id=1, source_target_pairs={{0,16},{16,0},{1,17},{17,1},{2,18},{18,2},{3,19},{19,3},{4,20},{20... | collective-permute-start | bytes 14155784 | tf_op jit(solution)/shard_map/ppermute | solution.py:951
  10.4 18.8 %collective-permute-start.4 = (bf16[3072,768]{1,0:T(8,128)(2,1)}, bf16[3072,768]{1,0:T(8,128)(2,1)}, u32[]{:S(2)}, u32[]{:S(2)}) collective-permute-start(bf16[3072,768]{1,0:T(8,128)(2,1)} %bitcast.162), channel_id=1, source_target_pairs={{0,16},{16,0},{1,17},{17,1},{2,18},{18,2},{3,19},{19,3},{4,20},{20... | collective-permute-start | bytes 14155784 | tf_op jit(solution)/shard_map/ppermute | solution.py:951
  59.2 28.2 %collective-permute-start.6 = (bf16[512,5376]{1,0:T(8,128)(2,1)}, bf16[512,5376]{1,0:T(8,128)(2,1)}, u32[]{:S(2)}, u32[]{:S(2)}) collective-permute-start(bf16[512,5376]{1,0:T(8,128)(2,1)} %get-tuple-element.114.refs_13_.refs_1_.refs_6_.refs_8_.refs_15_), channel_id=1, source_target_pairs={{0,16},{16,0},{1,17},{17,1},{2,18},{18,2},{3,19},{19,3},{4,20},{20... | collective-permute-start | bytes 16515080 | tf_op jit(solution)/shard_map/ppermute | solution.py:951
  59.6 13.9 %collective-permute-start.7 = (bf16[512,3072]{1,0:T(8,128)(2,1)}, bf16[512,3072]{1,0:T(8,128)(2,1)S(1)}, u32[]{:S(2)}, u32[]{:S(2)}) collective-permute-start(bf16[512,3072]{1,0:T(8,128)(2,1)} %get-tuple-element.115.refs_1_), channel_id=1, source_target_pairs={{0,16},{16,0},{1,17},{17,1},{2,18},{18,2},{3,19},{19,3},{4,20},{20... | collective-permute-start | bytes 9437192 | tf_op jit(solution)/shard_map/ppermute | solution.py:951
  71.5 16.0 %collective-permute-start.5 = (bf16[512,768]{1,0:T(8,128)(2,1)}, bf16[512,768]{1,0:T(8,128)(2,1)S(1)}, u32[]{:S(2)}, u32[]{:S(2)}) collective-permute-start(bf16[512,768]{1,0:T(8,128)(2,1)} %get-tuple-element.117), channel_id=1, source_target_pairs={{0,16},{16,0},{1,17},{17,1},{2,18},{18,2},{3,19},{19,3},{4,20},{20... | collective-permute-start | bytes 2359304 | tf_op jit(solution)/shard_map/ppermute | solution.py:951
  84.5 33.6 %collective-permute-start.9 = (bf16[8,192,384]{2,1,0:T(8,128)(2,1)}, bf16[8,192,384]{2,1,0:T(8,128)(2,1)}, u32[]{:S(2)}, u32[]{:S(2)}) collective-permute-start(bf16[8,192,384]{2,1,0:T(8,128)(2,1)} %get-tuple-element.122), channel_id=1, source_target_pairs={{0,1},{1,0},{2,3},{3,2},{4,5},{5,4},{6,7},{7,6},{8,9},{9,8},{10,11... | collective-permute-start | bytes 3538952 | tf_op jit(solution)/shard_map/ppermute | solution.py:955
  120.3 27.7 %collective-permute-start.11 = (bf16[768,384]{1,0:T(8,128)(2,1)}, bf16[768,384]{1,0:T(8,128)(2,1)}, u32[]{:S(2)}, u32[]{:S(2)}) collective-permute-start(bf16[768,384]{1,0:T(8,128)(2,1)} %bitcast.12), channel_id=1, source_target_pairs={{0,2},{1,3},{2,0},{3,1},{4,6},{5,7},{6,4},{7,5},{8,10},{9,11},{10,... | collective-permute-start | bytes 1769480 | tf_op jit(solution)/shard_map/ppermute | solution.py:955
  123.6 30.9 %collective-permute-start.16 = (bf16[512,1536]{1,0:T(8,128)(2,1)S(1)}, bf16[512,1536]{1,0:T(8,128)(2,1)}, u32[]{:S(2)}, u32[]{:S(2)}) collective-permute-start(bf16[512,1536]{1,0:T(8,128)(2,1)S(1)} %copy-done), channel_id=1, source_target_pairs={{0,16},{16,0},{1,17},{17,1},{2,18},{18,2},{3,19},{19,3},{4,20},{20... | collective-permute-start | bytes 4718600 | tf_op jit(solution)/shard_map/ppermute | solution.py:951
  143.2 45.1 %collective-permute-start.21 = (bf16[8,288,384]{2,1,0:T(8,128)(2,1)}, bf16[8,288,384]{2,1,0:T(8,128)(2,1)}, u32[]{:S(2)}, u32[]{:S(2)}) collective-permute-start(bf16[8,288,384]{2,1,0:T(8,128)(2,1)} %get-tuple-element.147), channel_id=1, source_target_pairs={{0,2},{1,3},{2,0},{3,1},{4,6},{5,7},{6,4},{7,5},{8,10},{9,11},{10,... | collective-permute-start | bytes 5308424 | tf_op jit(solution)/shard_map/ppermute | solution.py:955
  144.8 40.9 %collective-permute-start.18 = (bf16[8,288,384]{2,1,0:T(8,128)(2,1)}, bf16[8,288,384]{2,1,0:T(8,128)(2,1)}, u32[]{:S(2)}, u32[]{:S(2)}) collective-permute-start(bf16[8,288,384]{2,1,0:T(8,128)(2,1)} %get-tuple-element.145), channel_id=1, source_target_pairs={{0,1},{1,0},{2,3},{3,2},{4,5},{5,4},{6,7},{7,6},{8,9},{9,8},{10,11... | collective-permute-start | bytes 5308424 | tf_op jit(solution)/shard_map/ppermute | solution.py:955
  149.8 32.7 %collective-permute-start.17 = (bf16[512,768]{1,0:T(8,128)(2,1)S(1)}, bf16[512,768]{1,0:T(8,128)(2,1)S(1)}, u32[]{:S(2)}, u32[]{:S(2)}) collective-permute-start(bf16[512,768]{1,0:T(8,128)(2,1)S(1)} %copy-done.10), channel_id=1, source_target_pairs={{0,16},{16,0},{1,17},{17,1},{2,18},{18,2},{3,19},{19,3},{4,20},{20... | collective-permute-start | bytes 2359304 | tf_op jit(solution)/shard_map/ppermute | solution.py:951
  152.7 38.5 %collective-permute-start.20 = (bf16[384,384]{1,0:T(8,128)(2,1)}, bf16[384,384]{1,0:T(8,128)(2,1)}, u32[]{:S(2)}, u32[]{:S(2)}) collective-permute-start(bf16[384,384]{1,0:T(8,128)(2,1)} %fusion.4), channel_id=1, source_target_pairs={{0,4},{1,5},{2,6},{3,7},{4,0},{5,1},{6,2},{7,3},{8,12},{9,13},{10,... | collective-permute-start | bytes 884744 | tf_op jit(solution)/shard_map/ppermute | solution.py:955
  182.5 10.3 %collective-permute-start.22 = (bf16[512,1024]{1,0:T(8,128)(2,1)}, bf16[512,1024]{1,0:T(8,128)(2,1)S(1)}, u32[]{:S(2)}, u32[]{:S(2)}) collective-permute-start(bf16[512,1024]{1,0:T(8,128)(2,1)} %get-tuple-element.167), channel_id=1, source_target_pairs={{0,16},{16,0},{1,17},{17,1},{2,18},{18,2},{3,19},{19,3},{4,20},{20... | collective-permute-start | bytes 3145736 | tf_op jit(solution)/shard_map/ppermute | solution.py:951
  182.6 10.3 %collective-permute-start.23 = (bf16[512,1024]{1,0:T(8,128)(2,1)}, bf16[512,1024]{1,0:T(8,128)(2,1)S(1)}, u32[]{:S(2)}, u32[]{:S(2)}) collective-permute-start(bf16[512,1024]{1,0:T(8,128)(2,1)} %get-tuple-element.168), channel_id=1, source_target_pairs={{0,16},{16,0},{1,17},{17,1},{2,18},{18,2},{3,19},{19,3},{4,20},{20... | collective-permute-start | bytes 3145736 | tf_op jit(solution)/shard_map/ppermute | solution.py:951
  188.3 23.7 %collective-permute-start.19 = (bf16[1152,384]{1,0:T(8,128)(2,1)}, bf16[1152,384]{1,0:T(8,128)(2,1)}, u32[]{:S(2)}, u32[]{:S(2)}) collective-permute-start(bf16[1152,384]{1,0:T(8,128)(2,1)} %bitcast.20), channel_id=1, source_target_pairs={{0,2},{1,3},{2,0},{3,1},{4,6},{5,7},{6,4},{7,5},{8,10},{9,11},{10,... | collective-permute-start | bytes 2654216 | tf_op jit(solution)/shard_map/ppermute | solution.py:955
  191.1 22.1 %collective-permute-start.25 = (bf16[1152,384]{1,0:T(8,128)(2,1)}, bf16[1152,384]{1,0:T(8,128)(2,1)}, u32[]{:S(2)}, u32[]{:S(2)}) collective-permute-start(bf16[1152,384]{1,0:T(8,128)(2,1)} %bitcast.27), channel_id=1, source_target_pairs={{0,1},{1,0},{2,3},{3,2},{4,5},{5,4},{6,7},{7,6},{8,9},{9,8},{10,11... | collective-permute-start | bytes 2654216 | tf_op jit(solution)/shard_map/ppermute | solution.py:955
  208.9 34.9 %collective-permute-start.28 = (bf16[8,192,384]{2,1,0:T(8,128)(2,1)}, bf16[8,192,384]{2,1,0:T(8,128)(2,1)}, u32[]{:S(2)}, u32[]{:S(2)}) collective-permute-start(bf16[8,192,384]{2,1,0:T(8,128)(2,1)} %get-tuple-element.172), channel_id=1, source_target_pairs={{0,2},{1,3},{2,0},{3,1},{4,6},{5,7},{6,4},{7,5},{8,10},{9,11},{10,... | collective-permute-start | bytes 3538952 | tf_op jit(solution)/shard_map/ppermute | solution.py:955
  210.6 32.5 %collective-permute-start.29 = (bf16[8,208,384]{2,1,0:T(8,128)(2,1)}, bf16[8,208,384]{2,1,0:T(8,128)(2,1)S(1)}, u32[]{:S(2)}, u32[]{:S(2)}) collective-permute-start(bf16[8,208,384]{2,1,0:T(8,128)(2,1)} %get-tuple-element.171), channel_id=1, source_target_pairs={{0,1},{1,0},{2,3},{3,2},{4,5},{5,4},{6,7},{7,6},{8,9},{9,8},{10,11... | collective-permute-start | bytes 3833864 | tf_op jit(solution)/shard_map/ppermute | solution.py:955
  216.3 30.9 %collective-permute-start.26 = (bf16[512,768]{1,0:T(8,128)(2,1)}, bf16[512,768]{1,0:T(8,128)(2,1)}, u32[]{:S(2)}, u32[]{:S(2)}) collective-permute-start(bf16[512,768]{1,0:T(8,128)(2,1)} %get-tuple-element.175), channel_id=1, source_target_pairs={{0,16},{16,0},{1,17},{17,1},{2,18},{18,2},{3,19},{19,3},{4,20},{20... | collective-permute-start | bytes 2359304 | tf_op jit(solution)/shard_map/ppermute | solution.py:951
  216.9 31.7 %collective-permute-start.27 = (bf16[1152,384]{1,0:T(8,128)(2,1)}, bf16[1152,384]{1,0:T(8,128)(2,1)}, u32[]{:S(2)}, u32[]{:S(2)}) collective-permute-start(bf16[1152,384]{1,0:T(8,128)(2,1)} %bitcast.33), channel_id=1, source_target_pairs={{0,4},{1,5},{2,6},{3,7},{4,0},{5,1},{6,2},{7,3},{8,12},{9,13},{10,... | collective-permute-start | bytes 2654216 | tf_op jit(solution)/shard_map/ppermute | solution.py:955
  219.4 21.1 %collective-permute-start.37 = (f32[1,19968]{1,0:T(1,128)S(1)}, f32[1,19968]{1,0:T(1,128)S(1)}, u32[]{:S(2)}, u32[]{:S(2)}) collective-permute-start(f32[1,19968]{1,0:T(1,128)S(1)} %add.730), channel_id=1, source_target_pairs={{0,4},{1,5},{2,6},{3,7},{4,0},{5,1},{6,2},{7,3},{8,12},{9,13},{10,... | collective-permute-start | bytes 239624 | tf_op jit(solution)/shard_map/ppermute | solution.py:955
  240.4 35.2 %collective-permute-start.41 = (bf16[192,384]{1,0:T(8,128)(2,1)S(1)}, bf16[192,384]{1,0:T(8,128)(2,1)S(1)}, u32[]{:S(2)}, u32[]{:S(2)}) collective-permute-start(bf16[192,384]{1,0:T(8,128)(2,1)S(1)} %fusion.12), channel_id=1, source_target_pairs={{0,8},{1,9},{2,10},{3,11},{4,12},{5,13},{6,14},{7,15},{8,0},{9,1},... | collective-permute-start | bytes 442376 | tf_op jit(solution)/shard_map/ppermute | solution.py:955
  243.1 12.0 %collective-permute-start.38 = (f32[1,19968]{1,0:T(1,128)S(1)}, f32[1,19968]{1,0:T(1,128)S(1)}, u32[]{:S(2)}, u32[]{:S(2)}) collective-permute-start(f32[1,19968]{1,0:T(1,128)S(1)} %add.731), channel_id=1, source_target_pairs={{0,8},{1,9},{2,10},{3,11},{4,12},{5,13},{6,14},{7,15},{8,0},{9,1},... | collective-permute-start | bytes 239624 | tf_op jit(solution)/shard_map/ppermute | solution.py:955
  243.7 19.3 %collective-permute-start.31 = (bf16[832,384]{1,0:T(8,128)(2,1)S(1)}, bf16[832,384]{1,0:T(8,128)(2,1)S(1)}, u32[]{:S(2)}, u32[]{:S(2)}) collective-permute-start(bf16[832,384]{1,0:T(8,128)(2,1)S(1)} %bitcast.198), channel_id=1, source_target_pairs={{0,2},{1,3},{2,0},{3,1},{4,6},{5,7},{6,4},{7,5},{8,10},{9,11},{10,... | collective-permute-start | bytes 1916936 | tf_op jit(solution)/shard_map/ppermute | solution.py:955
  247.2 14.7 %collective-permute-start.32 = (bf16[768,384]{1,0:T(8,128)(2,1)S(1)}, bf16[768,384]{1,0:T(8,128)(2,1)S(1)}, u32[]{:S(2)}, u32[]{:S(2)}) collective-permute-start(bf16[768,384]{1,0:T(8,128)(2,1)S(1)} %bitcast.206), channel_id=1, source_target_pairs={{0,1},{1,0},{2,3},{3,2},{4,5},{5,4},{6,7},{7,6},{8,9},{9,8},{10,11... | collective-permute-start | bytes 1769480 | tf_op jit(solution)/shard_map/ppermute | solution.py:955
  252.4 20.0 %collective-permute-start.30 = (bf16[576,384]{1,0:T(8,128)(2,1)S(1)}, bf16[576,384]{1,0:T(8,128)(2,1)S(1)}, u32[]{:S(2)}, u32[]{:S(2)}) collective-permute-start(bf16[576,384]{1,0:T(8,128)(2,1)S(1)} %pad_maximum_fusion.2), channel_id=1, source_target_pairs={{0,8},{1,9},{2,10},{3,11},{4,12},{5,13},{6,14},{7,15},{8,0},{9,1},... | collective-permute-start | bytes 1327112 | tf_op jit(solution)/shard_map/ppermute | solution.py:955
  255.2 10.8 %collective-permute-start.39 = (f32[1,19968]{1,0:T(1,128)S(1)}, f32[1,19968]{1,0:T(1,128)S(1)}, u32[]{:S(2)}, u32[]{:S(2)}) collective-permute-start(f32[1,19968]{1,0:T(1,128)S(1)} %add.732), channel_id=1, source_target_pairs={{0,1},{1,0},{2,3},{3,2},{4,5},{5,4},{6,7},{7,6},{8,9},{9,8},{10,11... | collective-permute-start | bytes 239624 | tf_op jit(solution)/shard_map/ppermute | solution.py:955
  263.2 20.9 %collective-permute-start.33 = (bf16[800,384]{1,0:T(8,128)(2,1)S(1)}, bf16[800,384]{1,0:T(8,128)(2,1)S(1)}, u32[]{:S(2)}, u32[]{:S(2)}) collective-permute-start(bf16[800,384]{1,0:T(8,128)(2,1)S(1)} %bitcast.203), channel_id=1, source_target_pairs={{0,4},{1,5},{2,6},{3,7},{4,0},{5,1},{6,2},{7,3},{8,12},{9,13},{10,... | collective-permute-start | bytes 1843208 | tf_op jit(solution)/shard_map/ppermute | solution.py:955
  266.2 24.5 %collective-permute-start.40 = (f32[1,19968]{1,0:T(1,128)S(1)}, f32[1,19968]{1,0:T(1,128)S(1)}, u32[]{:S(2)}, u32[]{:S(2)}) collective-permute-start(f32[1,19968]{1,0:T(1,128)S(1)} %add.733), channel_id=1, source_target_pairs={{0,2},{1,3},{2,0},{3,1},{4,6},{5,7},{6,4},{7,5},{8,10},{9,11},{10,... | collective-permute-start | bytes 239624 | tf_op jit(solution)/shard_map/ppermute | solution.py:955
  276.9 12.9 %collective-permute-start.42 = (f32[192,384]{1,0:T(8,128)S(1)}, f32[192,384]{1,0:T(8,128)S(1)}, u32[]{:S(2)}, u32[]{:S(2)}) collective-permute-start(f32[192,384]{1,0:T(8,128)S(1)} %get-tuple-element.266), channel_id=1, source_target_pairs={{0,16},{16,0},{1,17},{17,1},{2,18},{18,2},{3,19},{19,3},{4,20},{20... | collective-permute-start | bytes 884744 | tf_op jit(solution)/shard_map/ppermute | solution.py:951
  287.0 16.4 %collective-permute-start.34 = (bf16[400,384]{1,0:T(8,128)(2,1)S(1)}, bf16[400,384]{1,0:T(8,128)(2,1)S(1)}, u32[]{:S(2)}, u32[]{:S(2)}) collective-permute-start(bf16[400,384]{1,0:T(8,128)(2,1)S(1)} %pad_maximum_fusion.3), channel_id=1, source_target_pairs={{0,8},{1,9},{2,10},{3,11},{4,12},{5,13},{6,14},{7,15},{8,0},{9,1},... | collective-permute-start | bytes 921608 | tf_op jit(solution)/shard_map/ppermute | solution.py:955
  (34 other events, 188.0 us)
